TPU v7x, 128 devices: a whole 4x4x4 slice. The times are simulated.
128 devices in a mesh: row: 32 (over z, y, core), col: 4 (over x).
Axes of the slice: x: 4, y: 4, z: 4, core: 2. Of those that a mesh axis runs over, the one named last changes fastest.
Arguments:
- design: float32 [32768, 4096], P('row', 'col')
- signs: int32 [32768], P('row'), may hold values from -1 to 1, as said below
- sample_rows: int32 [8192], P('row'), may hold values from 0 to 32767
Outputs:
- sketch: float32 [8192, 4096], P('row', 'col')
- gram: float32 [4096, 4096], P('row', 'col')
Inputs may be any that keep to these rules, and one draw needn't show every extreme that they name: `signs`: every entry is -1 or 1.
All inputs are finite; a program needn't handle non-finite values.
Results may differ from a plain program's by a relative error of at most 0.0003.
Values sent between devices are 32-bit elements; how exact they have to be, the bound alone decides.
No kernel may reach another device: no remote copies, remote signals or barrier semaphores. Data moves between devices by JAX's collectives and lax.ppermute only.
A program may use at most 320 MiB of HBM per device.

v0:
```python
import jax
import jax.numpy as jnp
from jax import lax
from jax.sharding import PartitionSpec as P


def hadamard(order):
    index = jnp.arange(order, dtype=jnp.int32)
    both = index[:, None] & index[None, :]
    count = jnp.zeros((order, order), jnp.int32)
    for bit in range(max(order.bit_length() - 1, 0)):
        count = count + (both >> bit & 1)
    return (1 - 2 * (count % 2)).astype(jnp.float32)


def local_transform(signed):
    rows_here, width = signed.shape
    bits = rows_here.bit_length() - 1
    first = 2 ** (bits // 2)
    second = rows_here // first
    shaped = signed.reshape(first, second, width)
    shaped = jnp.einsum("ij,jbc->ibc", hadamard(first), shaped, precision=lax.Precision.HIGHEST)
    shaped = jnp.einsum("kb,ibc->ikc", hadamard(second), shaped, precision=lax.Precision.HIGHEST)
    return shaped.reshape(rows_here, width)


def shards(design, signs, sample_rows):
    rows_here, width = design.shape
    groups = lax.axis_size("row")
    myself = lax.axis_index("row")
    owned = sample_rows.shape[0]
    total_samples = owned * groups
    blocked = local_transform(design * signs[:, None].astype(jnp.float32))
    wanted = lax.all_gather(sample_rows, "row", axis=0, tiled=True)
    outer_index = wanted // rows_here
    inner_index = wanted % rows_here
    share = rows_here // groups
    received = lax.all_to_all(
        blocked.reshape(groups, share, width), "row", split_axis=0, concat_axis=0, tiled=True
    )
    combined = jnp.einsum(
        "qp,pic->qic", hadamard(groups), received, precision=lax.Precision.HIGHEST
    )
    combined = combined.reshape(rows_here, width)
    holder_match = (inner_index // share == myself).astype(jnp.float32)
    position = outer_index * share + inner_index % share
    gathered = lax.psum_scatter(
        combined[position] * holder_match[:, None], "row", scatter_dimension=0, tiled=True
    )
    sketch = gathered * (1.0 / jnp.sqrt(jnp.float32(total_samples)))
    sketch_wide = lax.all_gather(sketch, "col", axis=1, tiled=True)
    gram = lax.psum_scatter(
        jnp.dot(
            sketch_wide.T,
            sketch,
            precision=lax.Precision.HIGHEST,
            preferred_element_type=jnp.float32,
        ),
        "row",
        scatter_dimension=0,
        tiled=True,
    )
    return (sketch, gram)


def solution(mesh):
    in_specs = (P("row", "col"), P("row"), P("row"))
    out_specs = (P("row", "col"), P("row", "col"))
    return jax.shard_map(shards, mesh=mesh, in_specs=in_specs, out_specs=out_specs, check_vma=False)
```

profile of v0, /device:TPU:14, one launch (start us, length us, event | category | flops | bytes accessed | tf_op | source)
XLA Modules:
  0.0 535.4 jit_solution(16343070949700418858)
XLA Ops:
  7.2 0.7 convert_element_type.17
  7.9 2.5 broadcast_multiply_fusion.1
  10.4 6.3 %fusion.4 = f32[32,32,1024]{2,0,1:T(8,128)S(1)} fusion(f32[32,32,1024]{2,1,0:T(8,128)S(1)} %bitcast.14), kind=kOutput, calls=%fused_computation.6 | convolution fusion | flops 402682880 | bytes 8388608 | tf_op jit(solution)/shard_map/ij,jbc->ibc/dot_general | solution.py:22
  16.7 7.3 %fusion.6 = f32[32,32,1024]{2,1,0:T(8,128)} fusion(f32[32,32,1024]{2,0,1:T(8,128)S(1)} %fusion.4), kind=kOutput, calls=%fused_computation.8 | convolution fusion | flops 402682880 | bytes 8388608 | tf_op jit(solution)/shard_map/kb,ibc->ikc/dot_general | solution.py:23
  24.0 0.0 copy-start
  24.0 8.7 %all-to-all-start = ((f32[32,32,1024]{2,1,0:T(8,128)}), f32[32,32,1024]{2,1,0:T(8,128)}, u32[]{:S(2)}, u32[]{:S(2)}) async-start(f32[32,32,1024]{2,1,0:T(8,128)} %fusion.6), calls=%async_computation | async-start | bytes 8388608 | tf_op jit(solution)/shard_map/all_to_all | solution.py:38
  32.7 0.0 reduce-scatter.3.cloned.1.call-start
  32.8 0.0 copy-done
  32.8 67.0 %all-gather = s32[32,1,256]{2,1,0:T(1,128)S(1)} all-gather(s32[1,1,256]{2,1,0:T(1,128)S(1)} %bitcast.17), channel_id=1, replica_groups=mesh['row'=32,'col'=4] {'row'}, dimensions={0}, use_global_device_ids=true | all-gather | bytes 33792 | tf_op jit(solution)/shard_map/all_gather | solution.py:34
  99.8 0.1 fusion.12
  99.9 0.0 all-to-all-done
  99.9 8.1 %fusion = f32[32,32,1024]{2,0,1:T(8,128)S(1)} fusion(f32[32,32,1024]{2,1,0:T(8,128)} %all-to-all-done), kind=kOutput, calls=%fused_computation.2 | convolution fusion | flops 402682880 | bytes 8388608 | tf_op jit(solution)/shard_map/qp,pic->qic/dot_general | solution.py:41
  108.0 4.5 copy.9
  112.5 45.8 %gather_fusion = f32[8192,1024]{1,0:T(8,128)} fusion(f32[1024,1024]{1,0:T(8,128)} %bitcast.13, s32[8192]{0:T(1024)S(1)} %fusion.12), kind=kCustom, calls=%fused_computation | custom fusion | bytes 67141632 | tf_op jit(solution)/shard_map/gather | solution.py:48
  158.3 22.5 %broadcast_multiply_fusion = f32[8192,1024]{1,0:T(8,128)} fusion(f32[8192,1024]{1,0:T(8,128)} %gather_fusion, f32[8192]{0:T(1024)S(1)} %fusion.15), kind=kLoop, calls=%fused_computation.1 | loop fusion | flops 8388608 | bytes 67141632 | tf_op jit(solution)/shard_map/mul | solution.py:48
  180.8 0.0 reduce-scatter.3.cloned.1.call-update
  180.8 0.0 all-gather.3.cloned.1.call-start
  180.9 164.2 %reduce-scatter.3.cloned.1.call-done = f32[256,1024]{1,0:T(8,128)} async-done(((f32[8192,1024]{1,0:T(8,128)}), f32[256,1024]{1,0:T(8,128)}) %reduce-scatter.3.cloned.1.call-update) | async-done | bytes 1048592 | tf_op jit(solution)/shard_map/reduce_scatter | solution.py:47
  345.0 2.3 broadcast_multiply_fusion.2
  347.4 0.0 all-gather.3.cloned.1.call-update
  347.4 0.0 reduce-scatter.5.cloned.1.call-start
  347.5 46.4 %all-gather.3.cloned.1.call-done = f32[256,4096]{1,0:T(8,128)} async-done(((f32[256,1024]{1,0:T(8,128)}), f32[256,4096]{1,0:T(8,128)}) %all-gather.3.cloned.1.call-update) | async-done | bytes 4194320 | tf_op jit(solution)/shard_map/all_gather | solution.py:51
  393.9 17.5 %fusion.56 = f32[4096,1024]{1,0:T(8,128)} fusion(f32[256,4096]{1,0:T(8,128)} %all-gather.3.cloned.1.call-done, f32[256,1024]{1,0:T(8,128)} %broadcast_multiply_fusion.2), kind=kOutput, calls=%fused_computation.71 | convolution fusion | flops 12884901888 | bytes 22020096 | tf_op jit(solution)/shard_map/dot_general | solution.py:53
  411.4 0.0 reduce-scatter.5.cloned.1.call-update
  411.4 117.4 %reduce-scatter.5.cloned.1.call-done = f32[128,1024]{1,0:T(8,128)} async-done(((f32[4096,1024]{1,0:T(8,128)}), f32[128,1024]{1,0:T(8,128)}) %reduce-scatter.5.cloned.1.call-update) | async-done | bytes 524304 | tf_op jit(solution)/shard_map/reduce_scatter | solution.py:52
  (1 shorter events, 0.0 us)
Async XLA Ops:
  24.0 8.8 %copy-start = (s32[256]{0:T(256)S(1)}, s32[256]{0:T(256)}, u32[]{:S(2)}) copy-start(s32[256]{0:T(256)} %param.5) | copy-start | bytes 3076
  24.0 75.9 %all-to-all-start = ((f32[32,32,1024]{2,1,0:T(8,128)}), f32[32,32,1024]{2,1,0:T(8,128)}, u32[]{:S(2)}, u32[]{:S(2)}) async-start(f32[32,32,1024]{2,1,0:T(8,128)} %fusion.6), calls=%async_computation | async-start | bytes 8388608 | tf_op jit(solution)/shard_map/all_to_all | solution.py:38
  32.7 312.3 %reduce-scatter.3.cloned.1.call-start = ((), (), s32[]{:S(2)}) async-start(), calls=%async_computation.3 | async-start | bytes 34603008 | tf_op jit(solution)/shard_map/reduce_scatter | solution.py:47
  180.8 213.1 %all-gather.3.cloned.1.call-start = ((), (), s32[]{:S(2)}) async-start(), calls=%async_computation.4 | async-start | bytes 5242880 | tf_op jit(solution)/shard_map/all_gather | solution.py:51
  347.4 181.4 %reduce-scatter.5.cloned.1.call-start = ((), (), s32[]{:S(2)}) async-start(), calls=%async_computation.5 | async-start | bytes 17301504 | tf_op jit(solution)/shard_map/reduce_scatter | solution.py:52
Sparse Core Ops, SparseCore 0:
  181.0 164.0 reduce-scatter.2
  347.5 46.3 all-gather.2
  411.6 117.2 reduce-scatter.4
where the time goes:
time: 536 us; the launch traced here: 535 us
  waiting for transfers between devices  328 us (61%)
  blocking collectives  67 us (12%)
  local copies, waits for them, and re-layouts  50.2 us (9%)
  matrix products  39.2 us (7%)
  other arithmetic  28.2 us (5%)
  between operations  13.8 us (3%)
  starting transfers between devices  8.86 us (2%)
    reduce_scatter x1, waiting for transfers between devices, shards(): lax.psum_scatter(combined[position] * holder_match[:, None], 'row', scatt...  164 us
    reduce_scatter x1, waiting for transfers between devices, shards(): lax.psum_scatter(jnp.dot(sketch_wide.T, sketch, precision=lax.Precision.H...  117 us
    all_gather x1, blocking collectives, shards(): wanted = lax.all_gather(sample_rows, 'row', axis=0, tiled=True)  67 us
    all_gather x1, waiting for transfers between devices, shards(): sketch_wide = lax.all_gather(sketch, 'col', axis=1, tiled=True)  46.4 us
    gather x1, local copies, waits for them, and re-layouts, shards(): combined[position] * holder_match[:, None]  45.8 us
    mul x1, other arithmetic, shards(): combined[position] * holder_match[:, None]  22.5 us
    dot_general x1, matrix products, shards(): jnp.dot(sketch_wide.T, sketch, precision=lax.Precision.HIGHEST, preferred...  17.5 us
  transfers between devices with their start and end apart: 4, of which 3 were waited for; matrix products, arithmetic and copies ran while one was open for 0% of the time, Pallas kernels for 0%

commit v1 on v0

v1 whole, which is shorter than its diff:
```python
import functools

import jax
import jax.numpy as jnp
import numpy as np
from jax import lax
from jax.experimental import pallas as pl
from jax.experimental.pallas import tpu as pltpu
from jax.sharding import PartitionSpec as P

NZ = NY = 4
SIDE = 4
LANE = 128
VMEM = 56 * 2**20


def place(z, y, c):
    return (z % NZ) * 2 * NY + (y % NY) * 2 + c


FIRST = [[place(z, y, 0) for y in range(4)] for z in range(4)]
FIRST += [[place(z, y, 1) for z in range(4)] for y in range(4)]
SECOND = [[place(z, y, 0) for z in range(4)] for y in range(4)]
SECOND += [[place(z, y, 1) for y in range(4)] for z in range(4)]
SIBLING = [(i, i ^ 1) for i in range(32)]


def around(step):
    return [(i, (i + step) % SIDE) for i in range(SIDE)]


def hadamard(order):
    index = np.arange(order)
    both = index[:, None] & index[None, :]
    count = np.zeros((order, order), np.int64)
    for bit in range(order.bit_length() - 1):
        count += both >> bit & 1
    return 1 - 2 * (count % 2)


def split(value):
    high = value.astype(jnp.bfloat16)
    low = (value - high.astype(jnp.float32)).astype(jnp.bfloat16)
    return high, low


def butterfly(parts):
    half = len(parts) // 2
    if half == 0:
        return parts
    low, high = butterfly(parts[:half]), butterfly(parts[half:])
    return [a + b for a, b in zip(low, high)] + [a - b for a, b in zip(low, high)]


def local_kernel(which_ref, table_ref, signs_ref, design_ref, out_ref):
    parts = []
    size = table_ref.shape[0]
    for number in range(design_ref.shape[0] // size):
        rows = pl.ds(number * size, size)
        signed = design_ref[rows, :] * signs_ref[rows, :]
        high, low = split(signed)
        part = jnp.dot(table_ref[...], high, preferred_element_type=jnp.float32)
        part += jnp.dot(table_ref[...], low, preferred_element_type=jnp.float32)
        parts.append(part)
    for number, part in enumerate(butterfly(parts)):
        out_ref[0, pl.ds(number * size, size), :] = part


def local_transform(design, signs, table, which):
    rows, width = design.shape
    blocks = width // (2 * LANE)
    size = table.shape[0]
    return pl.pallas_call(
        local_kernel,
        grid_spec=pltpu.PrefetchScalarGridSpec(
            num_scalar_prefetch=1,
            grid=(blocks,),
            in_specs=[
                pl.BlockSpec((size, size), lambda j, w: (0, 0)),
                pl.BlockSpec((rows, 1), lambda j, w: (0, 0)),
                pl.BlockSpec((rows, LANE), lambda j, w: (0, 2 * j + w[0])),
            ],
            out_specs=pl.BlockSpec((1, rows, LANE), lambda j, w: (j, 0, 0)),
        ),
        out_shape=jax.ShapeDtypeStruct((blocks, rows, LANE), jnp.float32),
        compiler_params=pltpu.CompilerParams(vmem_limit_bytes=VMEM),
        cost_estimate=pl.CostEstimate(flops=2**30, bytes_accessed=2**22, transcendentals=0),
    )(which, table, signs, design)


def sample_kernel(scale, index_ref, own_ref, other_ref, out_ref, mixed_ref):
    rows = own_ref.shape[1]
    step = pl.program_id(0)

    @pl.when(step == 0)
    def _():
        chunk = 64

        @pl.loop(0, rows // chunk)
        def _(number):
            here = pl.ds(number * chunk, chunk)
            sums, differences = [], []
            for src in range(SIDE):
                own, other = own_ref[src, here, :] * scale, other_ref[src, here, :] * scale
                sums.append(own + other)
                differences.append(own - other)
            for core, parts in enumerate((sums, differences)):
                for outer, part in enumerate(butterfly(parts)):
                    at = (outer * 2 + core) * rows + number * chunk
                    mixed_ref[pl.ds(at, chunk), :] = part
                    mixed_ref[pl.ds(2 * SIDE * rows + at, chunk), :] = -part

    count = out_ref.shape[1]
    group = 16

    @pl.loop(0, count // group)
    def _(number):
        for lane in range(group):
            at = number * group + lane
            source = index_ref[step * count + at]
            out_ref[0, pl.ds(at, 1), :] = mixed_ref[pl.ds(source, 1), :]


def sampled_rows(index, own, other, scale):
    total = index.shape[0]
    count = total // SIDE
    rows = own.shape[1]
    return pl.pallas_call(
        functools.partial(sample_kernel, scale),
        grid_spec=pltpu.PrefetchScalarGridSpec(
            num_scalar_prefetch=1,
            grid=(SIDE,),
            in_specs=[
                pl.BlockSpec((SIDE, rows, LANE), lambda s, i: (0, 0, 0)),
                pl.BlockSpec((SIDE, rows, LANE), lambda s, i: (0, 0, 0)),
            ],
            out_specs=pl.BlockSpec((1, count, LANE), lambda s, i: (s, 0, 0)),
            scratch_shapes=[pltpu.VMEM((4 * SIDE * rows, LANE), jnp.float32)],
        ),
        out_shape=jax.ShapeDtypeStruct((SIDE, count, LANE), jnp.float32),
        compiler_params=pltpu.CompilerParams(vmem_limit_bytes=VMEM),
        cost_estimate=pl.CostEstimate(flops=2**24, bytes_accessed=2**24, transcendentals=0),
    )(index, own, other)


def gram_kernel(
    place_ref, mine_ref, sibling_ref, right_ref, left_ref, far_a_ref, far_b_ref, out_ref,
    left_high, left_low, right_high, right_low,
):
    me, core = place_ref[0], place_ref[1]
    step = pl.program_id(0)
    depth = mine_ref.shape[1]

    @pl.when(step == 0)
    def _():
        for distance, refs in enumerate(((mine_ref,), (right_ref,), (far_a_ref, far_b_ref), (left_ref,))):
            column = lax.rem(me + SIDE - distance, SIDE)
            at = 0
            for ref in refs:
                for number in range(ref.shape[0]):
                    high, low = split(ref[number])
                    left_high[column, at] = high
                    left_low[column, at] = low
                    at += 1
        for number in range(SIDE):
            mine, theirs = mine_ref[number], sibling_ref[number]
            zero = jnp.where(core == 0, mine, theirs)
            one = jnp.where(core == 0, theirs, mine)
            for part, value in enumerate((zero, one)):
                high, low = split(value)
                here = pl.ds((2 * number + part) * LANE, LANE)
                right_high[:, here] = high
                right_low[:, here] = low

    def block(ref, second):
        column = jnp.where(core == 0, second, step)
        number = jnp.where(core == 0, step, second)
        return ref[column, number]

    high = jnp.concatenate([block(left_high, second) for second in range(SIDE)], axis=1)
    low = jnp.concatenate([block(left_low, second) for second in range(SIDE)], axis=1)

    def product(a, b):
        return lax.dot_general(a, b, (((0,), (0,)), ((), ())), preferred_element_type=jnp.float32)

    wide = 256
    for number in range(right_high.shape[1] // wide):
        here = pl.ds(number * wide, wide)
        value = product(high, right_high[:, here])
        value += product(low, right_high[:, here])
        value += product(high, right_low[:, here])
        for second in range(SIDE):
            out_ref[0, second, :, here] = value[second * LANE : (second + 1) * LANE]


def gram_shares(where, mine, sibling, right, left, far_a, far_b):
    depth = mine.shape[1]
    width = 2 * SIDE * LANE

    def whole(array):
        return pl.BlockSpec(array.shape, lambda s, w: (0, 0, 0))

    operands = (mine, sibling, right, left, far_a, far_b)
    return pl.pallas_call(
        gram_kernel,
        grid_spec=pltpu.PrefetchScalarGridSpec(
            num_scalar_prefetch=1,
            grid=(SIDE,),
            in_specs=[whole(array) for array in operands],
            out_specs=pl.BlockSpec((1, SIDE, LANE, width), lambda s, w: (s, 0, 0, 0)),
            scratch_shapes=[
                pltpu.VMEM((SIDE, SIDE, depth, LANE), jnp.bfloat16),
                pltpu.VMEM((SIDE, SIDE, depth, LANE), jnp.bfloat16),
                pltpu.VMEM((depth, width), jnp.bfloat16),
                pltpu.VMEM((depth, width), jnp.bfloat16),
            ],
        ),
        out_shape=jax.ShapeDtypeStruct((SIDE, SIDE, LANE, width), jnp.float32),
        compiler_params=pltpu.CompilerParams(vmem_limit_bytes=VMEM),
        cost_estimate=pl.CostEstimate(flops=6 * 2**30, bytes_accessed=2**24, transcendentals=0),
    )(where, *operands)


def exchange(value, groups):
    return lax.all_to_all(value, "row", 0, 0, tiled=True, axis_index_groups=groups)


def row_index(wanted, z, y, core):
    rest = wanted.shape[0] // 16
    grid = wanted.reshape(NZ, NY, rest)
    grid = jnp.where(core == 0, grid, jnp.swapaxes(grid, 0, 1))
    inner = grid % 1024
    outer = grid // 1024
    outer_z, outer_y, outer_core = outer // 8, outer // 2 % 4, outer % 2
    first = jnp.where(core == 0, outer_y, outer_z)
    second = jnp.where(core == 0, outer_z, outer_y)
    both = second & jnp.where(core == 0, z, y)
    negative = (both ^ (both >> 1) ^ (outer_core & core)) & 1
    return (inner + 1024 * (first * 2 + outer_core) + 8192 * negative).reshape(-1).astype(jnp.int32)


def shards(design, signs, sample_rows):
    owned = sample_rows.shape[0]
    myself = lax.axis_index("row")
    column = lax.axis_index("col")
    z, y, core = myself // 8, myself // 2 % 4, myself % 2
    total = owned * lax.axis_size("row")
    scale = float(np.float32(1.0) / np.sqrt(np.float32(total)))

    table = jnp.asarray(hadamard(256), jnp.bfloat16)
    sign_column = signs.astype(jnp.float32)[:, None]
    sent = local_transform(design, sign_column, table, (1 - core).astype(jnp.int32)[None])
    kept = local_transform(design, sign_column, table, core.astype(jnp.int32)[None])
    swapped = lax.ppermute(sent, "row", SIBLING)
    wanted = lax.all_gather(sample_rows, "row", axis=0, tiled=True)
    index = row_index(wanted, z, y, core)

    own = exchange(kept, FIRST)
    other = exchange(swapped, FIRST)
    picked = sampled_rows(index, own, other, scale)
    arrived = exchange(picked, SECOND)
    summed = jnp.sum(arrived, axis=0).reshape(SIDE, 2 * owned, LANE)
    mine = exchange(summed, FIRST)

    right = lax.ppermute(mine, "col", around(1))
    left = lax.ppermute(mine, "col", around(3))
    far_a = lax.ppermute(right[: SIDE // 2], "col", around(1))
    far_b = lax.ppermute(left[SIDE // 2 :], "col", around(3))
    sibling = lax.ppermute(mine, "row", SIBLING)

    def rows_of(array):
        return lax.dynamic_slice_in_dim(array, core * owned, owned, 1)

    pair = jnp.stack([rows_of(mine), rows_of(sibling)])
    pair = jnp.where(core == 0, pair, pair[::-1])
    sketch = pair.transpose(2, 1, 0, 3).reshape(owned, 2 * SIDE * LANE)

    where = jnp.stack([column, core]).astype(jnp.int32)
    shares = gram_shares(where, mine, sibling, right, left, far_a, far_b)
    part = jnp.sum(exchange(shares, FIRST), axis=0)
    gram = jnp.sum(exchange(part, SECOND), axis=0)
    return (sketch, gram)


def solution(mesh):
    in_specs = (P("row", "col"), P("row"), P("row"))
    out_specs = (P("row", "col"), P("row", "col"))
    return jax.shard_map(shards, mesh=mesh, in_specs=in_specs, out_specs=out_specs, check_vma=False)
```

time: 536 us -> 280 us (0.52)
  waiting for transfers between devices: 328 us -> 39.2 us
  blocking collectives: 67 us -> 158 us
  local copies, waits for them, and re-layouts: 50.2 us -> 9.22 us
  Pallas kernels: 0 us -> 40.2 us
  matrix products: 39.2 us -> 0 us
  other arithmetic: 28.2 us -> 11.1 us
  between operations: 13.8 us -> 0.78 us
  starting transfers between devices: 8.86 us -> 15.4 us
    reduce_scatter x2 -> x0, waiting for transfers between devices: 282 us -> none  [the longest x1 164 us: shards(): lax.psum_scatter(combined[position] * holder_match[:, None], 'row', scatt...]
    all_to_all x0 -> x4, blocking collectives: none -> 125 us  [exchange(): lax.all_to_all(value, 'row', 0, 0, tiled=True, axis_index_groups=groups)]
    all_gather x1 -> x0, waiting for transfers between devices: 46.4 us -> none  [shards(): sketch_wide = lax.all_gather(sketch, 'col', axis=1, tiled=True)]
    gather x1 -> x0, local copies, waits for them, and re-layouts: 45.8 us -> none  [shards(): combined[position] * holder_match[:, None]]
    pallas_call x0 -> x4, Pallas kernels: none -> 40.2 us  [the longest x1 17.1 us: sampled_rows(): pl.pallas_call(functools.partial(sample_kernel, scale), grid_spec=pltpu.P...]
    dot_general x4 -> x0, matrix products: 39.2 us -> none  [the longest x1 17.5 us: shards(): jnp.dot(sketch_wide.T, sketch, precision=lax.Precision.HIGHEST, preferred...]
    all_gather x1, blocking collectives: 67 us -> 32.9 us  [shards(): wanted = lax.all_gather(sample_rows, 'row', axis=0, tiled=True)]
    ppermute x0 -> x6, waiting for transfers between devices: none -> 27.9 us  [the longest x1 20.7 us: shards(): left = lax.ppermute(mine, 'col', around(3))]
  transfers between devices with their start and end apart: 4 -> 8, of which waited for: 3 -> 4; matrix products, arithmetic and copies ran while one was open for 0% -> 2% of each run, Pallas kernels for 0% -> 2%
where the time goes in v1:
time: 280 us; the launch traced here: 274 us
  blocking collectives  158 us (56%)
  Pallas kernels  40.2 us (14%)
  waiting for transfers between devices  39.2 us (14%)
  starting transfers between devices  15.4 us (6%)
  other arithmetic  11.1 us (4%)
  local copies, waits for them, and re-layouts  9.22 us (3%)
    all_to_all x4, blocking collectives, exchange(): lax.all_to_all(value, 'row', 0, 0, tiled=True, axis_index_groups=groups)  125 us
    all_gather x1, blocking collectives, shards(): wanted = lax.all_gather(sample_rows, 'row', axis=0, tiled=True)  32.9 us
    ppermute x1, waiting for transfers between devices, shards(): left = lax.ppermute(mine, 'col', around(3))  20.7 us
    pallas_call x1, Pallas kernels, sampled_rows(): pl.pallas_call(functools.partial(sample_kernel, scale), grid_spec=pltpu.P...  17.1 us
    pallas_call x1, Pallas kernels, gram_shares(): pl.pallas_call(gram_kernel, grid_spec=pltpu.PrefetchScalarGridSpec(num_sc...  13.1 us
    all_to_all x2, waiting for transfers between devices, exchange(): lax.all_to_all(value, 'row', 0, 0, tiled=True, axis_index_groups=groups)  11.3 us
    pallas_call x2, Pallas kernels, local_transform(): pl.pallas_call(local_kernel, grid_spec=pltpu.PrefetchScalarGridSpec(num_s...  9.98 us
    all_to_all x2, starting transfers between devices, exchange(): lax.all_to_all(value, 'row', 0, 0, tiled=True, axis_index_groups=groups)  8.91 us
  transfers between devices with their start and end apart: 8, of which 4 were waited for; matrix products, arithmetic and copies ran while one was open for 2% of the time, Pallas kernels for 2%

profile of v1, /device:TPU:14, one launch (start us, length us, event | category | flops | bytes accessed | tf_op | source)
XLA Modules:
  0.0 274.2 jit_solution(877605614642834726)
XLA Ops:
  0.6 0.7 convert_element_type.3
  1.3 1.0 copy.21.signs_ref
  2.4 5.0 %shard_map.60 = f32[4,1024,128]{2,1,0:T(8,128)} custom-call(s32[1]{0:T(128)} %bitcast.4.which_ref, bf16[256,256]{1,0:T(8,128)(2,1)} %constant.117.clone.table_ref, f32[1024,1]{1,0:T(8,128)} %copy.21.signs_ref, f32[1024,1024]{1,0:T(8,128)} %design_ref.3), custom_call_target="tpu_custom_call" | custom-call | flops 1073741824 | bytes 4194304 | tf_op jit(solution)/shard_map/pallas_call | solution.py:73
  7.3 0.0 collective-permute-start
  7.3 5.0 %shard_map.59 = f32[4,1024,128]{2,1,0:T(8,128)} custom-call(s32[1]{0:T(128)} %bitcast.2.which_ref, bf16[256,256]{1,0:T(8,128)(2,1)} %constant.117.clone.table_ref, f32[1024,1]{1,0:T(8,128)} %copy.21.signs_ref, f32[1024,1024]{1,0:T(8,128)} %design_ref.3), custom_call_target="tpu_custom_call" | custom-call | flops 1073741824 | bytes 4194304 | tf_op jit(solution)/shard_map/pallas_call | solution.py:73
  12.3 20.1 %all_to_all.30.own_ref = f32[4,1024,128]{2,1,0:T(8,128)} all-to-all(f32[4,1024,128]{2,1,0:T(8,128)} %shard_map.59), channel_id=1, replica_groups={{0,8,16,24},{32,40,48,56},{64,72,80,88},{96,104,112,120},{4,36,68,100},..., dimensions={0} | all-to-all | bytes 4194304 | tf_op jit(solution)/shard_map/all_to_all | solution.py:225
  32.4 0.0 copy-start.5
  32.4 0.0 collective-permute-done
  32.4 5.2 %all-to-all-start.1 = ((f32[4,1024,128]{2,1,0:T(8,128)}), f32[4,1024,128]{2,1,0:T(8,128)S(1)}, u32[]{:S(2)}, u32[]{:S(2)}) async-start(f32[4,1024,128]{2,1,0:T(8,128)} %collective-permute-done), calls=%async_computation.1 | async-start | bytes 4194304 | tf_op jit(solution)/shard_map/all_to_all | solution.py:225
  37.6 0.0 copy-done.5
  37.6 32.9 %all-gather = s32[32,1,256]{2,1,0:T(1,128)S(1)} all-gather(s32[1,1,256]{2,1,0:T(1,128)S(1)} %bitcast.24), channel_id=1, replica_groups=mesh['row'=32,'col'=4] {'row'}, dimensions={0}, use_global_device_ids=true | all-gather | bytes 33792 | tf_op jit(solution)/shard_map/all_gather | solution.py:255
  70.5 0.1 reduce
  70.6 0.2 fusion.3
  70.8 0.6 copy.25
  71.5 0.0 all-to-all-done.1.other_ref
  71.5 0.0 copy-start
  71.5 1.3 copy-done
  72.8 17.1 %shard_map.61 = f32[4,2048,128]{2,1,0:T(8,128)} custom-call(s32[8192]{0:T(1024)} %bitcast.22, f32[4,1024,128]{2,1,0:T(8,128)} %all_to_all.30.own_ref, f32[4,1024,128]{2,1,0:T(8,128)} %copy-done), custom_call_target="tpu_custom_call" | custom-call | flops 16777216 | bytes 16777216 | tf_op jit(solution)/shard_map/pallas_call | solution.py:128
  89.9 33.4 %all_to_all.31 = f32[4,2048,128]{2,1,0:T(8,128)} all-to-all(f32[4,2048,128]{2,1,0:T(8,128)} %shard_map.61), channel_id=1, replica_groups={{0,32,64,96},{8,40,72,104},{16,48,80,112},{24,56,88,120},{4,12,20,28},{..., dimensions={0} | all-to-all | bytes 8388608 | tf_op jit(solution)/shard_map/all_to_all | solution.py:225
  123.3 2.5 reduce_sum.27
  125.9 13.7 %all_to_all.32.mine_ref = f32[4,512,128]{2,1,0:T(8,128)S(1)} all-to-all(f32[4,512,128]{2,1,0:T(8,128)S(1)} %bitcast.21), channel_id=1, replica_groups={{0,8,16,24},{32,40,48,56},{64,72,80,88},{96,104,112,120},{4,36,68,100},..., dimensions={0} | all-to-all | bytes 2097152 | tf_op jit(solution)/shard_map/all_to_all | solution.py:225
  139.6 0.0 copy-start.1
  139.6 0.8 collective-permute-start.3
  140.4 2.4 collective-permute-start.2
  142.8 0.0 collective-permute-start.1
  142.8 20.7 %collective-permute-done.3.left_ref = f32[4,512,128]{2,1,0:T(8,128)S(1)} collective-permute-done((f32[4,512,128]{2,1,0:T(8,128)S(1)}, f32[4,512,128]{2,1,0:T(8,128)S(1)}, u32[]{:S(2)}, u32[]{:S(2)}) %collective-permute-start.3) | collective-permute-done | bytes 1048608 | tf_op jit(solution)/shard_map/ppermute | solution.py:266
  163.5 0.0 copy-start.3
  163.5 0.1 collective-permute-start.5
  163.6 0.0 collective-permute-done.2.right_ref
  163.6 0.0 copy-start.4
  163.6 1.1 copy-done.4
  164.8 3.2 %collective-permute-start.4 = (f32[2,512,128]{2,1,0:T(8,128)S(1)}, f32[2,512,128]{2,1,0:T(8,128)}, u32[]{:S(2)}, u32[]{:S(2)}) collective-permute-start(f32[2,512,128]{2,1,0:T(8,128)S(1)} %slice.8), channel_id=1, source_target_pairs={{0,1},{1,2},{2,3},{3,0},{4,5},{5,6},{6,7},{7,4},{8,9},{9,10},{10,1... | collective-permute-start | bytes 1572872 | tf_op jit(solution)/shard_map/ppermute | solution.py:267
  168.0 0.6 pad_add_fusion.place_ref
  168.6 0.0 collective-permute-done.1.sibling_ref
  168.6 6.9 %collective-permute-done.5.far_b_ref = f32[2,512,128]{2,1,0:T(8,128)} collective-permute-done((f32[2,512,128]{2,1,0:T(8,128)S(1)}, f32[2,512,128]{2,1,0:T(8,128)}, u32[]{:S(2)}, u32[]{:S(2)}) %collective-permute-start.5) | collective-permute-done | bytes 524320 | tf_op jit(solution)/shard_map/ppermute | solution.py:268
  175.5 0.3 collective-permute-done.4.far_a_ref
  175.8 0.0 copy-done.1
  175.8 0.0 copy-done.3
  175.8 13.1 %shard_map.62 = f32[4,4,128,1024]{3,2,1,0:T(8,128)} custom-call(s32[2]{0:T(128)} %pad_add_fusion.place_ref, f32[4,512,128]{2,1,0:T(8,128)} %copy-done.1, f32[4,512,128]{2,1,0:T(8,128)} %collective-permute-done.1.sibling_ref, f32[4,512,128]{2,1,0:T(8,128)} %copy-done.4, f32[4,512,128]{2,1,0:T(8,128)} %copy-done.3, ...), custom_call_target="tpu_custom_call" | custom-call | flops 6442450944 | bytes 16777216 | tf_op jit(solution)/shard_map/pallas_call | solution.py:204
  188.9 58.2 %all_to_all.33 = f32[4,4,128,1024]{3,2,1,0:T(8,128)} all-to-all(f32[4,4,128,1024]{3,2,1,0:T(8,128)} %shard_map.62), channel_id=1, replica_groups={{0,8,16,24},{32,40,48,56},{64,72,80,88},{96,104,112,120},{4,36,68,100},..., dimensions={0} | all-to-all | bytes 16777216 | tf_op jit(solution)/shard_map/all_to_all | solution.py:225
  247.1 5.9 %reduce_sum.28 = f32[4,128,1024]{2,1,0:T(8,128)} reduce(f32[4,4,128,1024]{3,2,1,0:T(8,128)} %all_to_all.33, f32[]{:T(128)} %constant.113.clone.1), dimensions={0}, to_apply=%region_1.2 | reduce | flops 1572864 | bytes 10485764 | tf_op jit(solution)/shard_map/reduce_sum | solution.py:280
  253.0 0.0 copy-start.2
  253.0 3.7 %all-to-all-start.5 = ((f32[4,128,1024]{2,1,0:T(8,128)}), f32[4,128,1024]{2,1,0:T(8,128)S(1)}, u32[]{:S(2)}, u32[]{:S(2)}) async-start(f32[4,128,1024]{2,1,0:T(8,128)} %reduce_sum.28), calls=%async_computation.5 | async-start | bytes 4194304 | tf_op jit(solution)/shard_map/all_to_all | solution.py:225
  256.7 0.0 copy-done.2
  256.8 1.1 dynamic-slice_bitcast_fusion
  257.9 0.1 pad_maximum_fusion
  257.9 0.1 fusion
  258.0 1.3 copy.23
  259.4 2.5 copy.24
  261.9 11.3 %all-to-all-done.5 = f32[4,128,1024]{2,1,0:T(8,128)S(1)} async-done(((f32[4,128,1024]{2,1,0:T(8,128)}), f32[4,128,1024]{2,1,0:T(8,128)S(1)}, u32[]{:S(2)}, u32[]{:S(2)}) %all-to-all-start.5) | async-done | bytes 2097184 | tf_op jit(solution)/shard_map/all_to_all | solution.py:225
  273.2 1.0 reduce_sum.29
  (4 shorter events, 0.1 us)
Async XLA Ops:
  7.3 25.1 %collective-permute-start = (f32[4,1024,128]{2,1,0:T(8,128)}, f32[4,1024,128]{2,1,0:T(8,128)}, u32[]{:S(2)}, u32[]{:S(2)}) collective-permute-start(f32[4,1024,128]{2,1,0:T(8,128)} %shard_map.60), channel_id=1, source_target_pairs={{0,4},{4,0},{8,12},{12,8},{16,20},{20,16},{24,28},{28,24},{32,36},... | collective-permute-start | bytes 6291464 | tf_op jit(solution)/shard_map/ppermute | solution.py:254
  32.4 5.2 %copy-start.5 = (s32[256]{0:T(256)S(1)}, s32[256]{0:T(256)}, u32[]{:S(2)}) copy-start(s32[256]{0:T(256)} %param.6) | copy-start | bytes 3076
  32.4 39.0 %all-to-all-start.1 = ((f32[4,1024,128]{2,1,0:T(8,128)}), f32[4,1024,128]{2,1,0:T(8,128)S(1)}, u32[]{:S(2)}, u32[]{:S(2)}) async-start(f32[4,1024,128]{2,1,0:T(8,128)} %collective-permute-done), calls=%async_computation.1 | async-start | bytes 4194304 | tf_op jit(solution)/shard_map/all_to_all | solution.py:225
  71.5 1.3 copy-start
  139.6 36.2 %copy-start.1 = (f32[4,512,128]{2,1,0:T(8,128)}, f32[4,512,128]{2,1,0:T(8,128)S(1)}, u32[]{:S(2)}) copy-start(f32[4,512,128]{2,1,0:T(8,128)S(1)} %all_to_all.32.mine_ref) | copy-start | bytes 3145732
  139.6 23.9 %collective-permute-start.3 = (f32[4,512,128]{2,1,0:T(8,128)S(1)}, f32[4,512,128]{2,1,0:T(8,128)S(1)}, u32[]{:S(2)}, u32[]{:S(2)}) collective-permute-start(f32[4,512,128]{2,1,0:T(8,128)S(1)} %all_to_all.32.mine_ref), channel_id=1, source_target_pairs={{0,3},{1,0},{2,1},{3,2},{4,7},{5,4},{6,5},{7,6},{8,11},{9,8},{10,9... | collective-permute-start | bytes 3145736 | tf_op jit(solution)/shard_map/ppermute | solution.py:266
  140.4 23.2 %collective-permute-start.2 = (f32[4,512,128]{2,1,0:T(8,128)S(1)}, f32[4,512,128]{2,1,0:T(8,128)S(1)}, u32[]{:S(2)}, u32[]{:S(2)}) collective-permute-start(f32[4,512,128]{2,1,0:T(8,128)S(1)} %all_to_all.32.mine_ref), channel_id=1, source_target_pairs={{0,1},{1,2},{2,3},{3,0},{4,5},{5,6},{6,7},{7,4},{8,9},{9,10},{10,1... | collective-permute-start | bytes 3145736 | tf_op jit(solution)/shard_map/ppermute | solution.py:265
  142.8 25.7 %collective-permute-start.1 = (f32[4,512,128]{2,1,0:T(8,128)S(1)}, f32[4,512,128]{2,1,0:T(8,128)}, u32[]{:S(2)}, u32[]{:S(2)}) collective-permute-start(f32[4,512,128]{2,1,0:T(8,128)S(1)} %all_to_all.32.mine_ref), channel_id=1, source_target_pairs={{0,4},{4,0},{8,12},{12,8},{16,20},{20,16},{24,28},{28,24},{32,36},... | collective-permute-start | bytes 3145736 | tf_op jit(solution)/shard_map/ppermute | solution.py:269
  163.5 12.3 %copy-start.3 = (f32[4,512,128]{2,1,0:T(8,128)}, f32[4,512,128]{2,1,0:T(8,128)S(1)}, u32[]{:S(2)}) copy-start(f32[4,512,128]{2,1,0:T(8,128)S(1)} %collective-permute-done.3.left_ref) | copy-start | bytes 3145732
  163.5 11.9 %collective-permute-start.5 = (f32[2,512,128]{2,1,0:T(8,128)S(1)}, f32[2,512,128]{2,1,0:T(8,128)}, u32[]{:S(2)}, u32[]{:S(2)}) collective-permute-start(f32[2,512,128]{2,1,0:T(8,128)S(1)} %slice.9), channel_id=1, source_target_pairs={{0,3},{1,0},{2,1},{3,2},{4,7},{5,4},{6,5},{7,6},{8,11},{9,8},{10,9... | collective-permute-start | bytes 1572872 | tf_op jit(solution)/shard_map/ppermute | solution.py:268
  163.6 1.1 copy-start.4
  164.8 10.9 %collective-permute-start.4 = (f32[2,512,128]{2,1,0:T(8,128)S(1)}, f32[2,512,128]{2,1,0:T(8,128)}, u32[]{:S(2)}, u32[]{:S(2)}) collective-permute-start(f32[2,512,128]{2,1,0:T(8,128)S(1)} %slice.8), channel_id=1, source_target_pairs={{0,1},{1,2},{2,3},{3,0},{4,5},{5,6},{6,7},{7,4},{8,9},{9,10},{10,1... | collective-permute-start | bytes 1572872 | tf_op jit(solution)/shard_map/ppermute | solution.py:267
  253.0 3.8 %copy-start.2 = (f32[4,512,128]{2,1,0:T(8,128)S(1)}, f32[4,512,128]{2,1,0:T(8,128)}, u32[]{:S(2)}) copy-start(f32[4,512,128]{2,1,0:T(8,128)} %copy-done.1) | copy-start | bytes 3145732
  253.0 20.2 %all-to-all-start.5 = ((f32[4,128,1024]{2,1,0:T(8,128)}), f32[4,128,1024]{2,1,0:T(8,128)S(1)}, u32[]{:S(2)}, u32[]{:S(2)}) async-start(f32[4,128,1024]{2,1,0:T(8,128)} %reduce_sum.28), calls=%async_computation.5 | async-start | bytes 4194304 | tf_op jit(solution)/shard_map/all_to_all | solution.py:225

commit v2 on v0

v2 whole, which is shorter than its diff:
```python
import functools

import jax
import jax.numpy as jnp
import numpy as np
from jax import lax
from jax.experimental import pallas as pl
from jax.experimental.pallas import tpu as pltpu
from jax.sharding import PartitionSpec as P

SIDE = 4
LANE = 128
VMEM = 56 * 2**20


def place(z, y, c):
    return z * 8 + y * 2 + c


def partners(ring, step):
    pairs = []
    for z in range(SIDE):
        for y in range(SIDE):
            for c in range(2):
                along_y = c == ring
                other = (z, y ^ step) if along_y else (z ^ step, y)
                pairs.append((place(z, y, c), place(*other, c)))
    return pairs


FIRST, SECOND = 0, 1


def hop(value, ring, step):
    return lax.ppermute(value, "row", partners(ring, step))


def to_sibling(value):
    return lax.ppermute(value, "row", [(i, i ^ 1) for i in range(32)])


def across(value, step):
    return lax.ppermute(value, "row", [(i ^ 1, j) for i, j in partners(FIRST, step)])


def around(value, step):
    return lax.ppermute(value, "col", [(i, (i + step) % SIDE) for i in range(SIDE)])


def hadamard(order):
    index = np.arange(order)
    both = index[:, None] & index[None, :]
    count = np.zeros((order, order), np.int64)
    for bit in range(order.bit_length() - 1):
        count += both >> bit & 1
    return 1 - 2 * (count % 2)


def split(value):
    high = value.astype(jnp.bfloat16)
    low = (value - high.astype(jnp.float32)).astype(jnp.bfloat16)
    return high, low


def butterfly(parts):
    half = len(parts) // 2
    if half == 0:
        return parts
    low, high = butterfly(parts[:half]), butterfly(parts[half:])
    return [a + b for a, b in zip(low, high)] + [a - b for a, b in zip(low, high)]


def fixed(shape):
    return pl.BlockSpec(shape, lambda *_: (0,) * len(shape))


def f32(*shape):
    return jax.ShapeDtypeStruct(shape, jnp.float32)


def call(kernel, grid, in_specs, out_specs, out_shape, scalars=0, scratch=(), flops=2**24, moved=2**23):
    return pl.pallas_call(
        kernel,
        grid_spec=pltpu.PrefetchScalarGridSpec(
            num_scalar_prefetch=scalars,
            grid=grid,
            in_specs=in_specs,
            out_specs=out_specs,
            scratch_shapes=scratch,
        ),
        out_shape=out_shape,
        compiler_params=pltpu.CompilerParams(vmem_limit_bytes=VMEM),
        cost_estimate=pl.CostEstimate(flops=flops, bytes_accessed=moved, transcendentals=0),
    )


def local_kernel(_, table_ref, signs_ref, own_ref, other_ref, *refs):
    outs, held_ref, sems = refs[:-2], refs[-2], refs[-1]
    step = pl.program_id(0)
    size = table_ref.shape[0]
    parts = []
    for number in range(own_ref.shape[0] // size):
        rows = pl.ds(number * size, size)
        signed_table = table_ref[...] * signs_ref[:, rows].astype(jnp.bfloat16)
        high, low = split(jnp.concatenate([own_ref[rows, :], other_ref[rows, :]], axis=1))
        part = jnp.dot(signed_table, high, preferred_element_type=jnp.float32)
        parts.append(part + jnp.dot(signed_table, low, preferred_element_type=jnp.float32))
    for number, part in enumerate(butterfly(parts)):
        rows = pl.ds(number * size, size)
        held_ref[step, 0, rows, :] = part[:, :LANE]
        held_ref[step, 1, rows, :] = part[:, LANE:]

    def copy(k, side):
        return pltpu.make_async_copy(held_ref.at[k, side], outs[SIDE * side + k], sems.at[k, side])

    for k in range(SIDE):

        @pl.when(step == k)
        def _():
            copy(k, 0).start()
            copy(k, 1).start()

    @pl.when(step == SIDE - 1)
    def _():
        for k in range(SIDE):
            copy(k, 0).wait()
            copy(k, 1).wait()


def local_transform(where, design, signs, table):
    rows = design.shape[0]
    size = table.shape[0]
    return call(
        local_kernel,
        (SIDE,),
        [
            fixed((size, size)),
            fixed((1, rows)),
            pl.BlockSpec((rows, LANE), lambda k, w: (0, 2 * (w[1] ^ k) + w[0])),
            pl.BlockSpec((rows, LANE), lambda k, w: (0, 2 * (w[2] ^ k) + 1 - w[0])),
        ],
        [pl.BlockSpec(memory_space=pl.ANY)] * (2 * SIDE),
        [f32(rows, LANE)] * (2 * SIDE),
        scalars=1,
        scratch=[pltpu.VMEM((SIDE, 2, rows, LANE), jnp.float32), pltpu.SemaphoreType.DMA((SIDE, 2))],
        flops=2**30,
        moved=2**23,
    )(where, table, signs, design, design)


def sample_kernel(scale, chunk, owned, where_ref, index_ref, *refs):
    sources, outs = refs[: 2 * SIDE], refs[2 * SIDE : 3 * SIDE]
    mixed_ref, picked_ref, sems = refs[3 * SIDE :]
    step = pl.program_id(0)
    block = sources[0].shape[0]
    rows = block * pl.num_programs(0)
    size = 32

    @pl.loop(0, block // size)
    def _(number):
        here = pl.ds(pl.multiple_of(number * size, size), size)
        sums, differences = [], []
        for k in range(SIDE):
            own, other = sources[k][here, :] * scale, sources[SIDE + k][here, :] * scale
            sums.append(own + other)
            differences.append(own - other)
        for core, parts in enumerate((sums, differences)):
            for outer, part in enumerate(butterfly(parts)):
                at = (outer * 2 + core) * rows + step * block + number * size
                mixed_ref[pl.ds(pl.multiple_of(at, size), size), :] = part
                mixed_ref[pl.ds(pl.multiple_of(2 * SIDE * rows + at, size), size), :] = -part

    @pl.when(step == pl.num_programs(0) - 1)
    def _():
        core, first, second = where_ref[0], where_ref[1], where_ref[2]
        group = 64
        copies = []
        for m in (2, 1, 3, 0):
            for k in range(SIDE):
                outer, inner = jnp.where(core == 0, second ^ m, first ^ k), jnp.where(core == 0, first ^ k, second ^ m)
                start = (outer * 8 + inner * 2 + chunk) * owned

                @pl.loop(0, owned // group)
                def _(number):
                    for lane in range(group):
                        at = number * group + lane
                        picked_ref[m, pl.ds(k * owned + at, 1), :] = mixed_ref[pl.ds(index_ref[start + at], 1), :]

            copies.append(pltpu.make_async_copy(picked_ref.at[m], outs[m], sems.at[m]))
            copies[-1].start()
        for copy in copies:
            copy.wait()


def sampled_rows(where, index, sources, scale, chunk, owned):
    rows = sources[0].shape[0]
    steps = 2
    return call(
        functools.partial(sample_kernel, scale, chunk, owned),
        (steps,),
        [pl.BlockSpec((rows // steps, LANE), lambda s, w, i: (s, 0))] * (2 * SIDE),
        [pl.BlockSpec(memory_space=pl.ANY)] * SIDE,
        [f32(SIDE * owned, LANE)] * SIDE,
        scalars=2,
        scratch=[
            pltpu.VMEM((4 * SIDE * rows, LANE), jnp.float32),
            pltpu.VMEM((SIDE, SIDE * owned, LANE), jnp.float32),
            pltpu.SemaphoreType.DMA((SIDE,)),
        ],
    )(where, index, *sources)


def rows_sum_kernel(*refs):
    sources, outs = refs[:SIDE], refs[SIDE:]
    owned = outs[0].shape[0]
    for k, out_ref in enumerate(outs):
        here = pl.ds(k * owned, owned)
        out_ref[...] = (sources[0][here, :] + sources[1][here, :]) + (sources[2][here, :] + sources[3][here, :])


def rows_sum(*operands):
    owned = operands[0].shape[0] // SIDE
    return call(
        rows_sum_kernel,
        (),
        [fixed(operand.shape) for operand in operands],
        [fixed((owned, LANE))] * SIDE,
        [f32(owned, LANE)] * SIDE,
    )(*operands)


def sketch_kernel(where_ref, mine_zero, mine_one, sibling_zero, sibling_one, out_ref):
    core, first, second = where_ref[0], where_ref[1], where_ref[2]
    for step in range(SIDE):
        mine = jnp.where(core == 0, mine_zero[step], mine_one[step])
        theirs = jnp.where(core == 0, sibling_zero[step], sibling_one[step])
        for block, value in ((2 * (first ^ step) + core, mine), (2 * (second ^ step) + 1 - core, theirs)):
            out_ref[:, pl.ds(pl.multiple_of(block * LANE, LANE), LANE)] = value


def sketch_rows(where, *operands):
    owned = operands[0].shape[1]
    width = 2 * SIDE * LANE
    return call(
        sketch_kernel,
        (1,),
        [fixed(operand.shape) for operand in operands],
        fixed((owned, width)),
        f32(owned, width),
        scalars=1,
    )(where, *operands)


def gram_kernel(half, plan, where_ref, *refs):
    inputs, outs = refs[:12], refs[12 : 12 + len(plan)]
    right_in, left_in, *held, right_sems, left_sems, out_sems = refs[12 + len(plan) :]
    core, first, second, me = (where_ref[i] for i in range(4))
    owned = right_in.shape[0] // 2
    blocks = [(number, block) for number, entries in enumerate(plan) for block in entries]

    def right_copy(chunk, number, side):
        mine, sibling = inputs[6 * chunk], inputs[6 * chunk + 1]
        j = 2 * half + number
        source = (mine.at[first ^ j], sibling.at[second ^ j])[side]
        block = 2 * number + jnp.where(side == 0, core, 1 - core)
        rows, lanes = pl.ds(chunk * owned, owned), pl.ds(pl.multiple_of(block * LANE, LANE), LANE)
        return pltpu.make_async_copy(source, right_in.at[rows, lanes], right_sems.at[chunk, number, side])

    rights = [right_copy(chunk, number, side) for chunk in range(2) for number in range(2) for side in range(2)]
    for copy in rights:
        copy.start()
    lefts = []
    for slot, (_, (k, m)) in enumerate(blocks):
        column = jnp.where(core == 0, second ^ m, first ^ k)
        step = jnp.where(core == 0, k, first ^ second ^ m)
        distance = lax.rem(me + SIDE - column, SIDE)
        for chunk in range(2):
            mine, _, right, left, far_a, far_b = inputs[6 * chunk : 6 * chunk + 6]
            target = left_in.at[slot, pl.ds(chunk * owned, owned), :]
            sem = left_sems.at[slot, chunk]
            cases = [(distance == 0, mine, step), (distance == 1, right, step), (distance == 3, left, step)]
            cases.append(((distance == 2) & (step < 2), far_a, jnp.minimum(step, 1)))
            cases.append(((distance == 2) & (step >= 2), far_b, jnp.maximum(step, 2) - 2))
            for chosen, ref, at in cases:

                @pl.when(chosen)
                def _():
                    pltpu.make_async_copy(ref.at[at], target, sem).start()

            lefts.append(pltpu.make_async_copy(mine.at[0], target, sem))

    def product(a, b):
        return lax.dot_general(a, b, (((0,), (0,)), ((), ())), preferred_element_type=jnp.float32)

    for copy in rights:
        copy.wait()
    right_high, right_low = split(right_in[...])
    group = 4
    copies = []
    done = [0] * len(plan)
    for base in range(0, len(blocks), group):
        for copy in lefts[2 * base : 2 * (base + group)]:
            copy.wait()
        high, low = split(jnp.concatenate([left_in[base + i] for i in range(group)], axis=1))
        value = product(high, right_high) + product(low, right_high) + product(high, right_low)
        for i in range(group):
            number = blocks[base + i][0]
            held[number][done[number]] = value[i * LANE : (i + 1) * LANE]
            done[number] += 1
            if done[number] == len(plan[number]):
                copies.append(pltpu.make_async_copy(held[number], outs[number], out_sems.at[number]))
                copies[-1].start()
    for copy in copies:
        copy.wait()


def gram_shares(where, operands, half, plan):
    owned = operands[0].shape[1]
    wide = SIDE * LANE
    shapes = [(len(entries), LANE, wide) for entries in plan]
    slots = sum(len(entries) for entries in plan)
    return call(
        functools.partial(gram_kernel, half, plan),
        (),
        [pl.BlockSpec(memory_space=pltpu.SMEM)] + [pl.BlockSpec(memory_space=pl.ANY)] * len(operands),
        [pl.BlockSpec(memory_space=pl.ANY)] * len(plan),
        [f32(*shape) for shape in shapes],
        scratch=[
            pltpu.VMEM((2 * owned, wide), jnp.float32),
            pltpu.VMEM((slots, 2 * owned, LANE), jnp.float32),
            *[pltpu.VMEM(shape, jnp.float32) for shape in shapes],
            pltpu.SemaphoreType.DMA((2, 2, 2)),
            pltpu.SemaphoreType.DMA((slots, 2)),
            pltpu.SemaphoreType.DMA((len(plan),)),
        ],
        flops=3 * 2**29,
        moved=5 * 2**20,
    )(where, *operands)


def ring_sum_kernel(kept_ref, from_one, from_three, last_one, last_three, *outs):
    for side, (early, late) in enumerate(((from_one, last_three), (from_three, last_one))):
        for part in range(2):
            outs[2 * side + part][...] = kept_ref[2 * side + part] + early[2 + part] + late[part]


def ring_sum(*operands):
    wide = operands[0].shape[-1]
    return call(
        ring_sum_kernel,
        (),
        [fixed(operand.shape) for operand in operands],
        [fixed((LANE, wide))] * SIDE,
        [f32(LANE, wide)] * SIDE,
    )(*operands)


def combine_kernel(*refs):
    out_ref = refs[-1]
    wide = refs[0].shape[1]
    for half in range(2):
        a, b, c, d = refs[SIDE * half : SIDE * half + SIDE]
        out_ref[:, pl.ds(half * wide, wide)] = (a[...] + b[...]) + (c[...] + d[...])


def combine(*operands):
    rows, wide = operands[0].shape
    return call(
        combine_kernel,
        (),
        [fixed(operand.shape) for operand in operands],
        fixed((rows, 2 * wide)),
        f32(rows, 2 * wide),
    )(*operands)


def sample_index(sample_rows, z, y, core):
    groups = lax.axis_size("row")
    spread = jnp.broadcast_to(sample_rows, (groups, sample_rows.shape[0]))
    wanted = lax.all_to_all(spread, "row", 0, 0, tiled=True).reshape(-1)
    first_here, second_here = jnp.where(core == 0, y, z), jnp.where(core == 0, z, y)
    inner, outer = wanted % 1024, wanted // 1024
    outer_z, outer_y, outer_core = outer // 8, outer // 2 % 4, outer % 2
    first = jnp.where(core == 0, outer_y, outer_z)
    second = jnp.where(core == 0, outer_z, outer_y)
    both = (first & first_here) ^ (second & second_here)
    negative = (both ^ (both >> 1) ^ (outer_core & core)) & 1
    return (inner + 1024 * (first * 2 + outer_core) + 8192 * negative).astype(jnp.int32)


def shards(design, signs, sample_rows):
    owned = sample_rows.shape[0]
    myself = lax.axis_index("row")
    column = lax.axis_index("col")
    z, y, core = myself // 8, myself // 2 % 4, myself % 2
    first, second = jnp.where(core == 0, y, z), jnp.where(core == 0, z, y)
    where = jnp.stack([core, first, second, column]).astype(jnp.int32)
    total = owned * lax.axis_size("row")
    scale = float(np.float32(1.0) / np.sqrt(np.float32(total)))

    table = jnp.asarray(hadamard(256), jnp.bfloat16)
    index = sample_index(sample_rows, z, y, core)
    pieces = local_transform(where, design, signs[None, :], table)
    sources = [pieces[0]] + [hop(pieces[step], FIRST, step) for step in (1, 2, 3)]
    sources += [across(pieces[SIDE + step], step) for step in range(SIDE)]

    gathered = []
    for chunk in range(2):
        picked = sampled_rows(where, index, sources, scale, chunk, owned)
        sums = rows_sum(picked[0], *[hop(picked[step], SECOND, step) for step in (1, 2, 3)])
        mine = jnp.stack([sums[0]] + [hop(sums[step], FIRST, step) for step in (1, 2, 3)])
        right, left = around(mine, 1), around(mine, 3)
        far_a, far_b = around(right[: SIDE // 2], 1), around(left[SIDE // 2 :], 3)
        gathered.append((mine, to_sibling(mine), right, left, far_a, far_b))

    sketch = sketch_rows(where, gathered[0][0], gathered[1][0], gathered[0][1], gathered[1][1])

    operands = gathered[0] + gathered[1]
    low, high = (0, 1), (2, 3)

    def blocks(*entries):
        return [(first, second) for first, seconds in entries for second in seconds]

    early = [gram_shares(where, operands, half, [blocks((2, low), (1, low)), blocks((2, high), (3, high))]) for half in range(2)]
    late_plan = [blocks((1, high)), blocks((3, low)), blocks((0, low), (0, high))]
    late = [gram_shares(where, operands, half, late_plan) for half in range(2)]
    parts = []
    for (to_one, to_three), (rest_one, rest_three, here) in zip(early, late):
        from_one, from_three = hop(to_one, FIRST, 1), hop(to_three, FIRST, 3)
        last_one = hop(rest_one + from_three[:2], FIRST, 1)
        last_three = hop(rest_three + from_one[:2], FIRST, 3)
        sums = ring_sum(here, from_one, from_three, last_one, last_three)
        parts += [sums[0]] + [hop(sums[step], SECOND, step) for step in (1, 2, 3)]
    return (sketch, combine(*parts))


def solution(mesh):
    in_specs = (P("row", "col"), P("row"), P("row"))
    out_specs = (P("row", "col"), P("row", "col"))
    return jax.shard_map(shards, mesh=mesh, in_specs=in_specs, out_specs=out_specs, check_vma=False)
```

time: 536 us -> 213 us (0.40)
  waiting for transfers between devices: 328 us -> 62.8 us
  Pallas kernels: 0 us -> 66.6 us
  blocking collectives: 67 us -> 15.8 us
  starting transfers between devices: 8.86 us -> 52.4 us
  local copies, waits for them, and re-layouts: 50.2 us -> 6.73 us
  matrix products: 39.2 us -> 0 us
  other arithmetic: 28.2 us -> 4.88 us
  between operations: 13.8 us -> 1.2 us
    reduce_scatter x2 -> x0, waiting for transfers between devices: 282 us -> none  [the longest x1 164 us: shards(): lax.psum_scatter(combined[position] * holder_match[:, None], 'row', scatt...]
    all_gather x1 -> x0, blocking collectives: 67 us -> none  [shards(): wanted = lax.all_gather(sample_rows, 'row', axis=0, tiled=True)]
    pallas_call x0 -> x13, Pallas kernels: none -> 66.6 us  [the longest x4 24.5 us: gram_shares(): call(functools.partial(gram_kernel, half, plan), (), [pl.BlockSpec(memory...]
    ppermute x0 -> x43, waiting for transfers between devices: none -> 62.8 us  [the longest x29 37.2 us: hop(): return lax.ppermute(value, 'row', partners(ring, step))]
    ppermute x0 -> x43, starting transfers between devices: none -> 52.4 us  [the longest x29 39.9 us: hop(): return lax.ppermute(value, 'row', partners(ring, step))]
    all_gather x1 -> x0, waiting for transfers between devices: 46.4 us -> none  [shards(): sketch_wide = lax.all_gather(sketch, 'col', axis=1, tiled=True)]
    gather x1 -> x0, local copies, waits for them, and re-layouts: 45.8 us -> none  [shards(): combined[position] * holder_match[:, None]]
    dot_general x4 -> x0, matrix products: 39.2 us -> none  [the longest x1 17.5 us: shards(): jnp.dot(sketch_wide.T, sketch, precision=lax.Precision.HIGHEST, preferred...]
  transfers between devices with their start and end apart: 4 -> 43, of which waited for: 3 -> 18; matrix products, arithmetic and copies ran while one was open for 0% -> 2% of each run, Pallas kernels for 0% -> 20%
where the time goes in v2:
time: 213 us; the launch traced here: 210 us
  Pallas kernels  66.6 us (31%)
  waiting for transfers between devices  62.8 us (29%)
  starting transfers between devices  52.4 us (25%)
  blocking collectives  15.8 us (7%)
  local copies, waits for them, and re-layouts  6.73 us (3%)
  other arithmetic  4.88 us (2%)
    ppermute x29, starting transfers between devices, hop(): return lax.ppermute(value, 'row', partners(ring, step))  39.9 us
    ppermute x29, waiting for transfers between devices, hop(): return lax.ppermute(value, 'row', partners(ring, step))  37.2 us
    ppermute x8, waiting for transfers between devices, around(): lax.ppermute(value, 'col', [(i, (i + step) % SIDE) for i in range(SIDE)])  25.6 us
    pallas_call x4, Pallas kernels, gram_shares(): call(functools.partial(gram_kernel, half, plan), (), [pl.BlockSpec(memory...  24.5 us
    pallas_call x2, Pallas kernels, sampled_rows(): call(functools.partial(sample_kernel, scale, chunk, owned), (steps,), [pl...  18.7 us
    all_to_all x1, blocking collectives, sample_index(): wanted = lax.all_to_all(spread, 'row', 0, 0, tiled=True).reshape(-1)  15.8 us
    ppermute x8, starting transfers between devices, around(): lax.ppermute(value, 'col', [(i, (i + step) % SIDE) for i in range(SIDE)])  8.08 us
    unnamed x86, local copies, waits for them, and re-layouts  6.64 us
  transfers between devices with their start and end apart: 43, of which 18 were waited for; matrix products, arithmetic and copies ran while one was open for 2% of the time, Pallas kernels for 20%

profile of v2, /device:TPU:14, one launch (start us, length us, event | category | flops | bytes accessed | tf_op | source)
XLA Modules:
  0.0 210.4 jit_solution(4563493828778853255)
XLA Ops:
  1.2 6.6 %shard_map.59 = (f32[1024,128]{1,0:T(8,128)}, f32[1024,128]{1,0:T(8,128)}, f32[1024,128]{1,0:T(8,128)}, f32[1024,128]{1,0:T(8,128)}, f32[1024,128]{1,0:T(8,128)}...) custom-call(s32[4]{0:T(128)} %pad_add_fusion._.where_ref, ...), custom_call_target="tpu_custom_call" | custom-call | flops 1073741824 | bytes 8388608 | tf_op jit(solution)/shard_map/pallas_call | solution.py:133
  8.4 2.6 %collective-permute-start.1 = (f32[1024,128]{1,0:T(8,128)}, f32[1024,128]{1,0:T(8,128)S(1)}, u32[]{:S(2)}, u32[]{:S(2)}) collective-permute-start(f32[1024,128]{1,0:T(8,128)} %get-tuple-element.46), channel_id=1, source_target_pairs={{0,16},{4,68},{8,24},{12,76},{16,0},{20,84},{24,8},{28,92},{32,48}... | collective-permute-start | bytes 1572872 | tf_op jit(solution)/shard_map/ppermute | solution.py:35
  11.4 1.3 collective-permute-start.3
  12.7 0.7 collective-permute-start.4
  13.4 5.2 %collective-permute-done.refs_1_ = f32[1024,128]{1,0:T(8,128)S(1)} collective-permute-done((f32[1024,128]{1,0:T(8,128)}, f32[1024,128]{1,0:T(8,128)S(1)}, u32[]{:S(2)}, u32[]{:S(2)}) %collective-permute-start) | collective-permute-done | bytes 524320 | tf_op jit(solution)/shard_map/ppermute | solution.py:35
  18.6 1.9 collective-permute-start.5
  20.6 10.3 %collective-permute-done.1.refs_2_ = f32[1024,128]{1,0:T(8,128)S(1)} collective-permute-done((f32[1024,128]{1,0:T(8,128)}, f32[1024,128]{1,0:T(8,128)S(1)}, u32[]{:S(2)}, u32[]{:S(2)}) %collective-permute-start.1) | collective-permute-done | bytes 524320 | tf_op jit(solution)/shard_map/ppermute | solution.py:35
  30.9 15.8 %all_to_all.6 = s32[32,1,256]{2,1,0:T(1,128)S(1)} all-to-all(s32[32,1,256]{2,1,0:T(1,128)S(1)} %broadcast_in_dim.6), channel_id=1, replica_groups=mesh['row'=32,'col'=4] {'row'}, dimensions={0} | all-to-all | bytes 65536 | tf_op jit(solution)/shard_map/all_to_all | solution.py:380
  46.8 0.7 fusion.1.index_ref
  47.6 0.7 copy-done.6
  49.0 9.3 %shard_map.62 = (f32[1024,128]{1,0:T(8,128)}, f32[1024,128]{1,0:T(8,128)}, f32[1024,128]{1,0:T(8,128)}, f32[1024,128]{1,0:T(8,128)}) custom-call(s32[4]{0:T(128)} %pad_add_fusion._.where_ref, s32[8192]{0:T(1024)} %fusion.1.index_ref, f32[1024,128]{1,0:T(8,128)} %get-tuple-element.44.refs_0_, f32[1024,128]{1,0:T(8,128)} %copy-done.4, f32[1024,128]{1,0:T(8,128)} %copy-done.5, ...), custom_call_target="tpu_custom_call" | custom-call | flops 16777216 | bytes 8388608 | tf_op jit(solution)/shard_map/pallas_call | solution.py:198
  59.0 2.0 collective-permute-start.14
  61.0 2.1 collective-permute-start.15
  63.1 9.3 %shard_map.60 = (f32[1024,128]{1,0:T(8,128)}, f32[1024,128]{1,0:T(8,128)}, f32[1024,128]{1,0:T(8,128)}, f32[1024,128]{1,0:T(8,128)}) custom-call(s32[4]{0:T(128)} %pad_add_fusion._.where_ref, s32[8192]{0:T(1024)} %fusion.1.index_ref, f32[1024,128]{1,0:T(8,128)} %get-tuple-element.44.refs_0_, f32[1024,128]{1,0:T(8,128)} %copy-done.4, f32[1024,128]{1,0:T(8,128)} %copy-done.5, ...), custom_call_target="tpu_custom_call" | custom-call | flops 16777216 | bytes 8388608 | tf_op jit(solution)/shard_map/pallas_call | solution.py:198
  72.5 2.6 %collective-permute-start.8 = (f32[1024,128]{1,0:T(8,128)}, f32[1024,128]{1,0:T(8,128)S(1)}, u32[]{:S(2)}, u32[]{:S(2)}) collective-permute-start(f32[1024,128]{1,0:T(8,128)} %get-tuple-element.54), channel_id=1, source_target_pairs={{0,64},{4,20},{8,72},{12,28},{16,80},{20,4},{24,88},{28,12},{32,96... | collective-permute-start | bytes 1572872 | tf_op jit(solution)/shard_map/ppermute | solution.py:35
  75.1 2.1 collective-permute-start.9
  77.3 0.8 copy-done.22
  78.2 2.4 %shard_map.63 = (f32[256,128]{1,0:T(8,128)}, f32[256,128]{1,0:T(8,128)}, f32[256,128]{1,0:T(8,128)}, f32[256,128]{1,0:T(8,128)}) custom-call(f32[1024,128]{1,0:T(8,128)} %get-tuple-element.60.refs_0_, f32[1024,128]{1,0:T(8,128)} %copy-done.21, f32[1024,128]{1,0:T(8,128)} %copy-done.22, f32[1024,128]{1,0:T(8,128)} %copy-done.23), custom_call_target="tpu_custom_call" | custom-call | flops 16777216 | bytes 8388608 | tf_op jit(solution)/shard_map/pallas_call | solution.py:223
  80.6 1.4 collective-permute-start.16
  82.6 4.4 %collective-permute-done.16 = f32[256,128]{1,0:T(8,128)S(1)} collective-permute-done((f32[256,128]{1,0:T(8,128)}, f32[256,128]{1,0:T(8,128)S(1)}, u32[]{:S(2)}, u32[]{:S(2)}) %collective-permute-start.16) | collective-permute-done | bytes 131104 | tf_op jit(solution)/shard_map/ppermute | solution.py:35
  87.6 1.1 collective-permute-done.17
  88.7 3.5 %collective-permute-done.18 = f32[256,128]{1,0:T(8,128)S(1)} collective-permute-done((f32[256,128]{1,0:T(8,128)}, f32[256,128]{1,0:T(8,128)S(1)}, u32[]{:S(2)}, u32[]{:S(2)}) %collective-permute-start.18) | collective-permute-done | bytes 131104 | tf_op jit(solution)/shard_map/ppermute | solution.py:35
  92.2 0.9 pad_maximum_fusion.1.mine_one.refs_6_
  95.0 2.4 %shard_map.61 = (f32[256,128]{1,0:T(8,128)}, f32[256,128]{1,0:T(8,128)}, f32[256,128]{1,0:T(8,128)}, f32[256,128]{1,0:T(8,128)}) custom-call(f32[1024,128]{1,0:T(8,128)} %get-tuple-element.52.refs_0_, f32[1024,128]{1,0:T(8,128)} %copy-done.18, f32[1024,128]{1,0:T(8,128)} %copy-done.19, f32[1024,128]{1,0:T(8,128)} %copy-done.20), custom_call_target="tpu_custom_call" | custom-call | flops 16777216 | bytes 8388608 | tf_op jit(solution)/shard_map/pallas_call | solution.py:223
  97.3 2.7 %collective-permute-start.10 = (f32[256,128]{1,0:T(8,128)}, f32[256,128]{1,0:T(8,128)S(1)}, u32[]{:S(2)}, u32[]{:S(2)}) collective-permute-start(f32[256,128]{1,0:T(8,128)} %get-tuple-element.57), channel_id=1, source_target_pairs={{0,8},{4,36},{8,0},{12,44},{16,24},{20,52},{24,16},{28,60},{32,40}... | collective-permute-start | bytes 393224 | tf_op jit(solution)/shard_map/ppermute | solution.py:35
  100.1 1.4 collective-permute-start.12
  101.5 1.6 collective-permute-start.26
  103.2 3.5 %collective-permute-done.11 = f32[256,128]{1,0:T(8,128)S(1)} collective-permute-done((f32[256,128]{1,0:T(8,128)}, f32[256,128]{1,0:T(8,128)S(1)}, u32[]{:S(2)}, u32[]{:S(2)}) %collective-permute-start.11) | collective-permute-done | bytes 131104 | tf_op jit(solution)/shard_map/ppermute | solution.py:35
  106.7 0.9 pad_maximum_fusion.mine_zero.refs_0_
  107.7 1.6 collective-permute-start.21
  110.3 7.1 %collective-permute-done.26.refs_9_ = f32[4,256,128]{2,1,0:T(8,128)S(1)} collective-permute-done((f32[4,256,128]{2,1,0:T(8,128)S(1)}, f32[4,256,128]{2,1,0:T(8,128)S(1)}, u32[]{:S(2)}, u32[]{:S(2)}) %collective-permute-start.26) | collective-permute-done | bytes 524320 | tf_op jit(solution)/shard_map/ppermute | solution.py:47
  117.8 4.8 %collective-permute-done.21.refs_2_ = f32[4,256,128]{2,1,0:T(8,128)S(1)} collective-permute-done((f32[4,256,128]{2,1,0:T(8,128)S(1)}, f32[4,256,128]{2,1,0:T(8,128)S(1)}, u32[]{:S(2)}, u32[]{:S(2)}) %collective-permute-start.21) | collective-permute-done | bytes 524320 | tf_op jit(solution)/shard_map/ppermute | solution.py:47
  122.6 1.5 collective-permute-start.28
  124.1 4.6 %collective-permute-done.22.refs_3_ = f32[4,256,128]{2,1,0:T(8,128)S(1)} collective-permute-done((f32[4,256,128]{2,1,0:T(8,128)S(1)}, f32[4,256,128]{2,1,0:T(8,128)S(1)}, u32[]{:S(2)}, u32[]{:S(2)}) %collective-permute-start.22) | collective-permute-done | bytes 524320 | tf_op jit(solution)/shard_map/ppermute | solution.py:47
  129.0 1.8 collective-permute-start.24
  130.8 3.5 %collective-permute-done.28.refs_11_ = f32[2,256,128]{2,1,0:T(8,128)S(1)} collective-permute-done((f32[2,256,128]{2,1,0:T(8,128)S(1)}, f32[2,256,128]{2,1,0:T(8,128)S(1)}, u32[]{:S(2)}, u32[]{:S(2)}) %collective-permute-start.28) | collective-permute-done | bytes 262176 | tf_op jit(solution)/shard_map/ppermute | solution.py:47
  134.3 2.9 %collective-permute-done.23.refs_4_ = f32[2,256,128]{2,1,0:T(8,128)S(1)} collective-permute-done((f32[2,256,128]{2,1,0:T(8,128)S(1)}, f32[2,256,128]{2,1,0:T(8,128)S(1)}, u32[]{:S(2)}, u32[]{:S(2)}) %collective-permute-start.23) | collective-permute-done | bytes 262176 | tf_op jit(solution)/shard_map/ppermute | solution.py:47
  137.2 2.7 %collective-permute-done.24.refs_5_ = f32[2,256,128]{2,1,0:T(8,128)S(1)} collective-permute-done((f32[2,256,128]{2,1,0:T(8,128)S(1)}, f32[2,256,128]{2,1,0:T(8,128)S(1)}, u32[]{:S(2)}, u32[]{:S(2)}) %collective-permute-start.24) | collective-permute-done | bytes 262176 | tf_op jit(solution)/shard_map/ppermute | solution.py:47
  140.0 0.7 copy-done.42
  140.7 6.1 %shard_map.69 = (f32[4,128,512]{2,1,0:T(8,128)}, f32[4,128,512]{2,1,0:T(8,128)}) custom-call(s32[4]{0:T(128)} %pad_add_fusion._.where_ref, f32[4,256,128]{2,1,0:T(8,128)} %copy-done.12, f32[4,256,128]{2,1,0:T(8,128)} %copy-done.17, f32[4,256,128]{2,1,0:T(8,128)} %copy-done.36, f32[4,256,128]{2,1,0:T(8,128)} %copy-done.37, f32[2,256,128]{2,1,0:T(8,128)} %copy-done.41, ...), custom_call_target="tpu_custom_call" | custom-call | flops 1610612736 | bytes 5242880 | tf_op jit(solution)/shard_map/pallas_call | solution.py:322
  146.9 1.7 collective-permute-start.36
  149.1 6.1 %shard_map.66 = (f32[4,128,512]{2,1,0:T(8,128)}, f32[4,128,512]{2,1,0:T(8,128)}) custom-call(s32[4]{0:T(128)} %pad_add_fusion._.where_ref, f32[4,256,128]{2,1,0:T(8,128)} %copy-done.12, f32[4,256,128]{2,1,0:T(8,128)} %copy-done.17, f32[4,256,128]{2,1,0:T(8,128)} %copy-done.36, f32[4,256,128]{2,1,0:T(8,128)} %copy-done.37, f32[2,256,128]{2,1,0:T(8,128)} %copy-done.41, ...), custom_call_target="tpu_custom_call" | custom-call | flops 1610612736 | bytes 5242880 | tf_op jit(solution)/shard_map/pallas_call | solution.py:322
  155.2 1.2 collective-permute-start.29
  156.4 1.3 collective-permute-start.30
  157.8 6.1 %shard_map.68 = (f32[2,128,512]{2,1,0:T(8,128)}, f32[2,128,512]{2,1,0:T(8,128)}, f32[4,128,512]{2,1,0:T(8,128)}) custom-call(s32[4]{0:T(128)} %pad_add_fusion._.where_ref, f32[4,256,128]{2,1,0:T(8,128)} %copy-done.12, f32[4,256,128]{2,1,0:T(8,128)} %copy-done.17, f32[4,256,128]{2,1,0:T(8,128)} %copy-done.36, f32[4,256,128]{2,1,0:T(8,128)} %copy-done.37, ...), custom_call_target="tpu_custom_call" | custom-call | flops 1610612736 | bytes 5242880 | tf_op jit(solution)/shard_map/pallas_call | solution.py:322
  163.9 6.2 %shard_map.65 = (f32[2,128,512]{2,1,0:T(8,128)}, f32[2,128,512]{2,1,0:T(8,128)}, f32[4,128,512]{2,1,0:T(8,128)}) custom-call(s32[4]{0:T(128)} %pad_add_fusion._.where_ref, f32[4,256,128]{2,1,0:T(8,128)} %copy-done.12, f32[4,256,128]{2,1,0:T(8,128)} %copy-done.17, f32[4,256,128]{2,1,0:T(8,128)} %copy-done.36, f32[4,256,128]{2,1,0:T(8,128)} %copy-done.37, ...), custom_call_target="tpu_custom_call" | custom-call | flops 1610612736 | bytes 5242880 | tf_op jit(solution)/shard_map/pallas_call | solution.py:322
  170.2 0.8 collective-permute-start.39
  171.1 2.2 %collective-permute-start.38 = (f32[2,128,512]{2,1,0:T(8,128)S(1)}, f32[2,128,512]{2,1,0:T(8,128)S(1)}, u32[]{:S(2)}, u32[]{:S(2)}) collective-permute-start(f32[2,128,512]{2,1,0:T(8,128)S(1)} %slice_add_fusion.1), channel_id=1, source_target_pairs={{0,8},{4,36},{8,0},{12,44},{16,24},{20,52},{24,16},{28,60},{32,40}... | collective-permute-start | bytes 1572872 | tf_op jit(solution)/shard_map/ppermute | solution.py:35
  173.3 1.5 slice_add_fusion.2
  174.8 1.5 collective-permute-start.32
  176.3 1.4 collective-permute-start.31
  177.7 2.7 %collective-permute-done.39.last_three = f32[2,128,512]{2,1,0:T(8,128)S(1)} collective-permute-done((f32[2,128,512]{2,1,0:T(8,128)S(1)}, f32[2,128,512]{2,1,0:T(8,128)S(1)}, u32[]{:S(2)}, u32[]{:S(2)}) %collective-permute-start.39) | collective-permute-done | bytes 524320 | tf_op jit(solution)/shard_map/ppermute | solution.py:35
  180.5 0.8 copy-done.26
  181.4 3.2 %shard_map.70 = (f32[128,512]{1,0:T(8,128)}, f32[128,512]{1,0:T(8,128)}, f32[128,512]{1,0:T(8,128)}, f32[128,512]{1,0:T(8,128)}) custom-call(f32[4,128,512]{2,1,0:T(8,128)} %get-tuple-element.77.kept_ref, f32[4,128,512]{2,1,0:T(8,128)} %copy-done.2, f32[4,128,512]{2,1,0:T(8,128)} %copy-done.3, f32[2,128,512]{2,1,0:T(8,128)} %copy-done.27, ...), custom_call_target="tpu_custom_call" | custom-call | flops 16777216 | bytes 8388608 | tf_op jit(solution)/shard_map/pallas_call | solution.py:349
  184.6 3.5 %collective-permute-start.41 = (f32[128,512]{1,0:T(8,128)}, f32[128,512]{1,0:T(8,128)S(1)}, u32[]{:S(2)}, u32[]{:S(2)}) collective-permute-start(f32[128,512]{1,0:T(8,128)} %get-tuple-element.84), channel_id=1, source_target_pairs={{0,64},{4,20},{8,72},{12,28},{16,80},{20,4},{24,88},{28,12},{32,96... | collective-permute-start | bytes 786440 | tf_op jit(solution)/shard_map/ppermute | solution.py:35
  188.2 1.2 collective-permute-start.42
  189.4 0.8 copy-done.24
  190.3 3.3 %shard_map.67 = (f32[128,512]{1,0:T(8,128)}, f32[128,512]{1,0:T(8,128)}, f32[128,512]{1,0:T(8,128)}, f32[128,512]{1,0:T(8,128)}) custom-call(f32[4,128,512]{2,1,0:T(8,128)} %get-tuple-element.68.kept_ref, f32[4,128,512]{2,1,0:T(8,128)} %copy-done, f32[4,128,512]{2,1,0:T(8,128)} %copy-done.1, f32[2,128,512]{2,1,0:T(8,128)} %copy-done.25, ...), custom_call_target="tpu_custom_call" | custom-call | flops 16777216 | bytes 8388608 | tf_op jit(solution)/shard_map/pallas_call | solution.py:349
  193.6 3.5 %collective-permute-start.34 = (f32[128,512]{1,0:T(8,128)}, f32[128,512]{1,0:T(8,128)S(1)}, u32[]{:S(2)}, u32[]{:S(2)}) collective-permute-start(f32[128,512]{1,0:T(8,128)} %get-tuple-element.75), channel_id=1, source_target_pairs={{0,64},{4,20},{8,72},{12,28},{16,80},{20,4},{24,88},{28,12},{32,96... | collective-permute-start | bytes 786440 | tf_op jit(solution)/shard_map/ppermute | solution.py:35
  197.1 1.2 collective-permute-start.35
  198.3 3.3 %shard_map.64 = f32[256,1024]{1,0:T(8,128)} custom-call(s32[4]{0:T(128)} %pad_add_fusion._.where_ref, f32[4,256,128]{2,1,0:T(8,128)} %copy-done.12, f32[4,256,128]{2,1,0:T(8,128)} %copy-done.11, f32[4,256,128]{2,1,0:T(8,128)} %copy-done.17, f32[4,256,128]{2,1,0:T(8,128)} %copy-done.16), custom_call_target="tpu_custom_call" | custom-call | flops 16777216 | bytes 8388608 | tf_op jit(solution)/shard_map/pallas_call | solution.py:244
  201.6 3.0 %collective-permute-done.34.refs_2_ = f32[128,512]{1,0:T(8,128)S(1)} collective-permute-done((f32[128,512]{1,0:T(8,128)}, f32[128,512]{1,0:T(8,128)S(1)}, u32[]{:S(2)}, u32[]{:S(2)}) %collective-permute-start.34) | collective-permute-done | bytes 262176 | tf_op jit(solution)/shard_map/ppermute | solution.py:35
  204.6 2.7 %collective-permute-done.35.refs_3_ = f32[128,512]{1,0:T(8,128)S(1)} collective-permute-done((f32[128,512]{1,0:T(8,128)}, f32[128,512]{1,0:T(8,128)S(1)}, u32[]{:S(2)}, u32[]{:S(2)}) %collective-permute-start.35) | collective-permute-done | bytes 262176 | tf_op jit(solution)/shard_map/ppermute | solution.py:35
  208.0 2.4 %shard_map.71 = f32[128,1024]{1,0:T(8,128)} custom-call(f32[128,512]{1,0:T(8,128)} %get-tuple-element.73.refs_0_, f32[128,512]{1,0:T(8,128)} %copy-done.31, f32[128,512]{1,0:T(8,128)} %copy-done.32, f32[128,512]{1,0:T(8,128)} %copy-done.33, f32[128,512]{1,0:T(8,128)} %get-tuple-element.82.refs_4_, f32[128,512]{1,0:T(8,128)} %copy-done.28, ...), custom_call_target="tpu_custom_call" | custom-call | flops 16777216 | bytes 8388608 | tf_op jit(solution)/shard_map/pallas_call | solution.py:368
  (135 shorter events, 10.3 us)
Async XLA Ops:
  1.2 29.7 %copy-start.38 = (s32[256]{0:T(256)S(1)}, s32[256]{0:T(256)}, u32[]{:S(2)}) copy-start(s32[256]{0:T(256)} %param.6) | copy-start | bytes 3076
  7.8 10.8 %collective-permute-start = (f32[1024,128]{1,0:T(8,128)}, f32[1024,128]{1,0:T(8,128)S(1)}, u32[]{:S(2)}, u32[]{:S(2)}) collective-permute-start(f32[1024,128]{1,0:T(8,128)} %get-tuple-element.45), channel_id=1, source_target_pairs={{0,8},{4,36},{8,0},{12,44},{16,24},{20,52},{24,16},{28,60},{32,40}... | collective-permute-start | bytes 1572872 | tf_op jit(solution)/shard_map/ppermute | solution.py:35
  8.4 22.5 %collective-permute-start.1 = (f32[1024,128]{1,0:T(8,128)}, f32[1024,128]{1,0:T(8,128)S(1)}, u32[]{:S(2)}, u32[]{:S(2)}) collective-permute-start(f32[1024,128]{1,0:T(8,128)} %get-tuple-element.46), channel_id=1, source_target_pairs={{0,16},{4,68},{8,24},{12,76},{16,0},{20,84},{24,8},{28,92},{32,48}... | collective-permute-start | bytes 1572872 | tf_op jit(solution)/shard_map/ppermute | solution.py:35
  11.0 36.5 %collective-permute-start.2 = (f32[1024,128]{1,0:T(8,128)}, f32[1024,128]{1,0:T(8,128)S(1)}, u32[]{:S(2)}, u32[]{:S(2)}) collective-permute-start(f32[1024,128]{1,0:T(8,128)} %get-tuple-element.47), channel_id=1, source_target_pairs={{0,24},{4,100},{8,16},{12,108},{16,8},{20,116},{24,0},{28,124},{32... | collective-permute-start | bytes 1572872 | tf_op jit(solution)/shard_map/ppermute | solution.py:35
  11.4 36.1 %collective-permute-start.3 = (f32[1024,128]{1,0:T(8,128)}, f32[1024,128]{1,0:T(8,128)S(1)}, u32[]{:S(2)}, u32[]{:S(2)}) collective-permute-start(f32[1024,128]{1,0:T(8,128)} %get-tuple-element.48), channel_id=1, source_target_pairs={{4,0},{0,4},{12,8},{8,12},{20,16},{16,20},{28,24},{24,28},{36,32},... | collective-permute-start | bytes 1572872 | tf_op jit(solution)/shard_map/ppermute | solution.py:43
  12.7 34.8 %collective-permute-start.4 = (f32[1024,128]{1,0:T(8,128)}, f32[1024,128]{1,0:T(8,128)S(1)}, u32[]{:S(2)}, u32[]{:S(2)}) collective-permute-start(f32[1024,128]{1,0:T(8,128)} %get-tuple-element.49), channel_id=1, source_target_pairs={{4,8},{0,36},{12,0},{8,44},{20,24},{16,52},{28,16},{24,60},{36,40}... | collective-permute-start | bytes 1572872 | tf_op jit(solution)/shard_map/ppermute | solution.py:43
  18.6 28.9 %copy-start.4 = (f32[1024,128]{1,0:T(8,128)}, f32[1024,128]{1,0:T(8,128)S(1)}, u32[]{:S(2)}) copy-start(f32[1024,128]{1,0:T(8,128)S(1)} %collective-permute-done.refs_1_) | copy-start | bytes 1572868
  18.6 28.9 %collective-permute-start.5 = (f32[1024,128]{1,0:T(8,128)}, f32[1024,128]{1,0:T(8,128)S(1)}, u32[]{:S(2)}, u32[]{:S(2)}) collective-permute-start(f32[1024,128]{1,0:T(8,128)} %get-tuple-element.50), channel_id=1, source_target_pairs={{4,16},{0,68},{12,24},{8,76},{20,0},{16,84},{28,8},{24,92},{36,48}... | collective-permute-start | bytes 1572872 | tf_op jit(solution)/shard_map/ppermute | solution.py:43
  30.9 16.7 %copy-start.5 = (f32[1024,128]{1,0:T(8,128)}, f32[1024,128]{1,0:T(8,128)S(1)}, u32[]{:S(2)}) copy-start(f32[1024,128]{1,0:T(8,128)S(1)} %collective-permute-done.1.refs_2_) | copy-start | bytes 1572868
  30.9 16.6 %collective-permute-start.6 = (f32[1024,128]{1,0:T(8,128)}, f32[1024,128]{1,0:T(8,128)S(1)}, u32[]{:S(2)}, u32[]{:S(2)}) collective-permute-start(f32[1024,128]{1,0:T(8,128)} %get-tuple-element.51), channel_id=1, source_target_pairs={{4,24},{0,100},{12,16},{8,108},{20,8},{16,116},{28,0},{24,124},{36... | collective-permute-start | bytes 1572872 | tf_op jit(solution)/shard_map/ppermute | solution.py:43
  58.3 16.8 %collective-permute-start.13 = (f32[1024,128]{1,0:T(8,128)}, f32[1024,128]{1,0:T(8,128)S(1)}, u32[]{:S(2)}, u32[]{:S(2)}) collective-permute-start(f32[1024,128]{1,0:T(8,128)} %get-tuple-element.61), channel_id=1, source_target_pairs={{0,32},{4,12},{8,40},{12,4},{16,48},{20,28},{24,56},{28,20},{32,0}... | collective-permute-start | bytes 1572872 | tf_op jit(solution)/shard_map/ppermute | solution.py:35
  59.0 18.2 %collective-permute-start.14 = (f32[1024,128]{1,0:T(8,128)}, f32[1024,128]{1,0:T(8,128)S(1)}, u32[]{:S(2)}, u32[]{:S(2)}) collective-permute-start(f32[1024,128]{1,0:T(8,128)} %get-tuple-element.62), channel_id=1, source_target_pairs={{0,64},{4,20},{8,72},{12,28},{16,80},{20,4},{24,88},{28,12},{32,96... | collective-permute-start | bytes 1572872 | tf_op jit(solution)/shard_map/ppermute | solution.py:35
  61.0 16.2 %collective-permute-start.15 = (f32[1024,128]{1,0:T(8,128)}, f32[1024,128]{1,0:T(8,128)S(1)}, u32[]{:S(2)}, u32[]{:S(2)}) collective-permute-start(f32[1024,128]{1,0:T(8,128)} %get-tuple-element.63), channel_id=1, source_target_pairs={{0,96},{4,28},{8,104},{12,20},{16,112},{20,12},{24,120},{28,4},{32... | collective-permute-start | bytes 1572872 | tf_op jit(solution)/shard_map/ppermute | solution.py:35
  72.4 21.2 %collective-permute-start.7 = (f32[1024,128]{1,0:T(8,128)}, f32[1024,128]{1,0:T(8,128)S(1)}, u32[]{:S(2)}, u32[]{:S(2)}) collective-permute-start(f32[1024,128]{1,0:T(8,128)} %get-tuple-element.53), channel_id=1, source_target_pairs={{0,32},{4,12},{8,40},{12,4},{16,48},{20,28},{24,56},{28,20},{32,0}... | collective-permute-start | bytes 1572872 | tf_op jit(solution)/shard_map/ppermute | solution.py:35
  72.5 21.1 %collective-permute-start.8 = (f32[1024,128]{1,0:T(8,128)}, f32[1024,128]{1,0:T(8,128)S(1)}, u32[]{:S(2)}, u32[]{:S(2)}) collective-permute-start(f32[1024,128]{1,0:T(8,128)} %get-tuple-element.54), channel_id=1, source_target_pairs={{0,64},{4,20},{8,72},{12,28},{16,80},{20,4},{24,88},{28,12},{32,96... | collective-permute-start | bytes 1572872 | tf_op jit(solution)/shard_map/ppermute | solution.py:35
  75.1 19.0 %collective-permute-start.9 = (f32[1024,128]{1,0:T(8,128)}, f32[1024,128]{1,0:T(8,128)S(1)}, u32[]{:S(2)}, u32[]{:S(2)}) collective-permute-start(f32[1024,128]{1,0:T(8,128)} %get-tuple-element.55), channel_id=1, source_target_pairs={{0,96},{4,28},{8,104},{12,20},{16,112},{20,12},{24,120},{28,4},{32... | collective-permute-start | bytes 1572872 | tf_op jit(solution)/shard_map/ppermute | solution.py:35
  80.6 6.4 %collective-permute-start.16 = (f32[256,128]{1,0:T(8,128)}, f32[256,128]{1,0:T(8,128)S(1)}, u32[]{:S(2)}, u32[]{:S(2)}) collective-permute-start(f32[256,128]{1,0:T(8,128)} %get-tuple-element.65), channel_id=1, source_target_pairs={{0,8},{4,36},{8,0},{12,44},{16,24},{20,52},{24,16},{28,60},{32,40}... | collective-permute-start | bytes 393224 | tf_op jit(solution)/shard_map/ppermute | solution.py:35
  82.0 6.7 %collective-permute-start.17 = (f32[256,128]{1,0:T(8,128)}, f32[256,128]{1,0:T(8,128)S(1)}, u32[]{:S(2)}, u32[]{:S(2)}) collective-permute-start(f32[256,128]{1,0:T(8,128)} %get-tuple-element.66), channel_id=1, source_target_pairs={{0,16},{4,68},{8,24},{12,76},{16,0},{20,84},{24,8},{28,92},{32,48}... | collective-permute-start | bytes 393224 | tf_op jit(solution)/shard_map/ppermute | solution.py:35
  87.0 5.2 %collective-permute-start.18 = (f32[256,128]{1,0:T(8,128)}, f32[256,128]{1,0:T(8,128)S(1)}, u32[]{:S(2)}, u32[]{:S(2)}) collective-permute-start(f32[256,128]{1,0:T(8,128)} %get-tuple-element.67), channel_id=1, source_target_pairs={{0,24},{4,100},{8,16},{12,108},{16,8},{20,116},{24,0},{28,124},{32... | collective-permute-start | bytes 393224 | tf_op jit(solution)/shard_map/ppermute | solution.py:35
  93.1 46.8 %copy-start.11 = (f32[4,256,128]{2,1,0:T(8,128)}, f32[4,256,128]{2,1,0:T(8,128)S(1)}, u32[]{:S(2)}) copy-start(f32[4,256,128]{2,1,0:T(8,128)S(1)} %pad_maximum_fusion.1.mine_one.refs_6_) | copy-start | bytes 1572868
  93.1 16.8 %collective-permute-start.25 = (f32[4,256,128]{2,1,0:T(8,128)S(1)}, f32[4,256,128]{2,1,0:T(8,128)S(1)}, u32[]{:S(2)}, u32[]{:S(2)}) collective-permute-start(f32[4,256,128]{2,1,0:T(8,128)S(1)} %pad_maximum_fusion.1.mine_one.refs_6_), channel_id=1, source_target_pairs={{0,1},{1,2},{2,3},{3,0},{4,5},{5,6},{6,7},{7,4},{8,9},{9,10},{10,1... | collective-permute-start | bytes 1572872 | tf_op jit(solution)/shard_map/ppermute | solution.py:47
  97.3 5.9 %collective-permute-start.10 = (f32[256,128]{1,0:T(8,128)}, f32[256,128]{1,0:T(8,128)S(1)}, u32[]{:S(2)}, u32[]{:S(2)}) collective-permute-start(f32[256,128]{1,0:T(8,128)} %get-tuple-element.57), channel_id=1, source_target_pairs={{0,8},{4,36},{8,0},{12,44},{16,24},{20,52},{24,16},{28,60},{32,40}... | collective-permute-start | bytes 393224 | tf_op jit(solution)/shard_map/ppermute | solution.py:35
  100.1 6.7 %collective-permute-start.11 = (f32[256,128]{1,0:T(8,128)}, f32[256,128]{1,0:T(8,128)S(1)}, u32[]{:S(2)}, u32[]{:S(2)}) collective-permute-start(f32[256,128]{1,0:T(8,128)} %get-tuple-element.58), channel_id=1, source_target_pairs={{0,16},{4,68},{8,24},{12,76},{16,0},{20,84},{24,8},{28,92},{32,48}... | collective-permute-start | bytes 393224 | tf_op jit(solution)/shard_map/ppermute | solution.py:35
  100.1 6.6 %collective-permute-start.12 = (f32[256,128]{1,0:T(8,128)}, f32[256,128]{1,0:T(8,128)S(1)}, u32[]{:S(2)}, u32[]{:S(2)}) collective-permute-start(f32[256,128]{1,0:T(8,128)} %get-tuple-element.59), channel_id=1, source_target_pairs={{0,24},{4,100},{8,16},{12,108},{16,8},{20,116},{24,0},{28,124},{32... | collective-permute-start | bytes 393224 | tf_op jit(solution)/shard_map/ppermute | solution.py:35
  101.5 15.9 %collective-permute-start.26 = (f32[4,256,128]{2,1,0:T(8,128)S(1)}, f32[4,256,128]{2,1,0:T(8,128)S(1)}, u32[]{:S(2)}, u32[]{:S(2)}) collective-permute-start(f32[4,256,128]{2,1,0:T(8,128)S(1)} %pad_maximum_fusion.1.mine_one.refs_6_), channel_id=1, source_target_pairs={{0,3},{1,0},{2,1},{3,2},{4,7},{5,4},{6,5},{7,6},{8,11},{9,8},{10,9... | collective-permute-start | bytes 1572872 | tf_op jit(solution)/shard_map/ppermute | solution.py:47
  107.7 32.2 %copy-start.12 = (f32[4,256,128]{2,1,0:T(8,128)}, f32[4,256,128]{2,1,0:T(8,128)S(1)}, u32[]{:S(2)}) copy-start(f32[4,256,128]{2,1,0:T(8,128)S(1)} %pad_maximum_fusion.mine_zero.refs_0_) | copy-start | bytes 1572868
  107.7 14.9 %collective-permute-start.21 = (f32[4,256,128]{2,1,0:T(8,128)S(1)}, f32[4,256,128]{2,1,0:T(8,128)S(1)}, u32[]{:S(2)}, u32[]{:S(2)}) collective-permute-start(f32[4,256,128]{2,1,0:T(8,128)S(1)} %pad_maximum_fusion.mine_zero.refs_0_), channel_id=1, source_target_pairs={{0,1},{1,2},{2,3},{3,0},{4,5},{5,6},{6,7},{7,4},{8,9},{9,10},{10,1... | collective-permute-start | bytes 1572872 | tf_op jit(solution)/shard_map/ppermute | solution.py:47
  109.3 19.4 %collective-permute-start.22 = (f32[4,256,128]{2,1,0:T(8,128)S(1)}, f32[4,256,128]{2,1,0:T(8,128)S(1)}, u32[]{:S(2)}, u32[]{:S(2)}) collective-permute-start(f32[4,256,128]{2,1,0:T(8,128)S(1)} %pad_maximum_fusion.mine_zero.refs_0_), channel_id=1, source_target_pairs={{0,3},{1,0},{2,1},{3,2},{4,7},{5,4},{6,5},{7,6},{8,11},{9,8},{10,9... | collective-permute-start | bytes 1572872 | tf_op jit(solution)/shard_map/ppermute | solution.py:47
  109.8 19.2 %collective-permute-start.20 = (f32[4,256,128]{2,1,0:T(8,128)S(1)}, f32[4,256,128]{2,1,0:T(8,128)S(1)}, u32[]{:S(2)}, u32[]{:S(2)}) collective-permute-start(f32[4,256,128]{2,1,0:T(8,128)S(1)} %pad_maximum_fusion.1.mine_one.refs_6_), channel_id=1, source_target_pairs={{0,4},{4,0},{8,12},{12,8},{16,20},{20,16},{24,28},{28,24},{32,36},... | collective-permute-start | bytes 1572872 | tf_op jit(solution)/shard_map/ppermute | solution.py:39
  109.9 30.0 %copy-start.34 = (f32[4,256,128]{2,1,0:T(8,128)}, f32[4,256,128]{2,1,0:T(8,128)S(1)}, u32[]{:S(2)}) copy-start(f32[4,256,128]{2,1,0:T(8,128)S(1)} %collective-permute-done.25.refs_8_) | copy-start | bytes 1572868
  109.9 20.9 %collective-permute-start.19 = (f32[4,256,128]{2,1,0:T(8,128)S(1)}, f32[4,256,128]{2,1,0:T(8,128)S(1)}, u32[]{:S(2)}, u32[]{:S(2)}) collective-permute-start(f32[4,256,128]{2,1,0:T(8,128)S(1)} %pad_maximum_fusion.mine_zero.refs_0_), channel_id=1, source_target_pairs={{0,4},{4,0},{8,12},{12,8},{16,20},{20,16},{24,28},{28,24},{32,36},... | collective-permute-start | bytes 1572872 | tf_op jit(solution)/shard_map/ppermute | solution.py:39
  117.4 22.5 %copy-start.35 = (f32[4,256,128]{2,1,0:T(8,128)}, f32[4,256,128]{2,1,0:T(8,128)S(1)}, u32[]{:S(2)}) copy-start(f32[4,256,128]{2,1,0:T(8,128)S(1)} %collective-permute-done.26.refs_9_) | copy-start | bytes 1572868
  117.4 13.4 %collective-permute-start.27 = (f32[2,256,128]{2,1,0:T(8,128)S(1)}, f32[2,256,128]{2,1,0:T(8,128)S(1)}, u32[]{:S(2)}, u32[]{:S(2)}) collective-permute-start(f32[2,256,128]{2,1,0:T(8,128)S(1)} %slice.34), channel_id=1, source_target_pairs={{0,1},{1,2},{2,3},{3,0},{4,5},{5,6},{6,7},{7,4},{8,9},{9,10},{10,1... | collective-permute-start | bytes 786440 | tf_op jit(solution)/shard_map/ppermute | solution.py:47
  122.6 17.4 %copy-start.36 = (f32[4,256,128]{2,1,0:T(8,128)}, f32[4,256,128]{2,1,0:T(8,128)S(1)}, u32[]{:S(2)}) copy-start(f32[4,256,128]{2,1,0:T(8,128)S(1)} %collective-permute-done.21.refs_2_) | copy-start | bytes 1572868
  122.6 11.7 %collective-permute-start.28 = (f32[2,256,128]{2,1,0:T(8,128)S(1)}, f32[2,256,128]{2,1,0:T(8,128)S(1)}, u32[]{:S(2)}, u32[]{:S(2)}) collective-permute-start(f32[2,256,128]{2,1,0:T(8,128)S(1)} %slice.35), channel_id=1, source_target_pairs={{0,3},{1,0},{2,1},{3,2},{4,7},{5,4},{6,5},{7,6},{8,11},{9,8},{10,9... | collective-permute-start | bytes 786440 | tf_op jit(solution)/shard_map/ppermute | solution.py:47
  128.7 11.3 %copy-start.37 = (f32[4,256,128]{2,1,0:T(8,128)}, f32[4,256,128]{2,1,0:T(8,128)S(1)}, u32[]{:S(2)}) copy-start(f32[4,256,128]{2,1,0:T(8,128)S(1)} %collective-permute-done.22.refs_3_) | copy-start | bytes 1572868
  128.7 8.5 %collective-permute-start.23 = (f32[2,256,128]{2,1,0:T(8,128)S(1)}, f32[2,256,128]{2,1,0:T(8,128)S(1)}, u32[]{:S(2)}, u32[]{:S(2)}) collective-permute-start(f32[2,256,128]{2,1,0:T(8,128)S(1)} %slice.32), channel_id=1, source_target_pairs={{0,1},{1,2},{2,3},{3,0},{4,5},{5,6},{6,7},{7,4},{8,9},{9,10},{10,1... | collective-permute-start | bytes 786440 | tf_op jit(solution)/shard_map/ppermute | solution.py:47
  129.0 11.0 %copy-start.16 = (f32[4,256,128]{2,1,0:T(8,128)}, f32[4,256,128]{2,1,0:T(8,128)S(1)}, u32[]{:S(2)}) copy-start(f32[4,256,128]{2,1,0:T(8,128)S(1)} %collective-permute-done.20.sibling_one.refs_7_) | copy-start | bytes 1572868
  129.0 10.9 %collective-permute-start.24 = (f32[2,256,128]{2,1,0:T(8,128)S(1)}, f32[2,256,128]{2,1,0:T(8,128)S(1)}, u32[]{:S(2)}, u32[]{:S(2)}) collective-permute-start(f32[2,256,128]{2,1,0:T(8,128)S(1)} %slice.33), channel_id=1, source_target_pairs={{0,3},{1,0},{2,1},{3,2},{4,7},{5,4},{6,5},{7,6},{8,11},{9,8},{10,9... | collective-permute-start | bytes 786440 | tf_op jit(solution)/shard_map/ppermute | solution.py:47
  130.8 9.1 %copy-start.17 = (f32[4,256,128]{2,1,0:T(8,128)}, f32[4,256,128]{2,1,0:T(8,128)S(1)}, u32[]{:S(2)}) copy-start(f32[4,256,128]{2,1,0:T(8,128)S(1)} %collective-permute-done.19.sibling_zero.refs_1_) | copy-start | bytes 1572868
  130.8 9.1 %copy-start.39 = (f32[2,256,128]{2,1,0:T(8,128)}, f32[2,256,128]{2,1,0:T(8,128)S(1)}, u32[]{:S(2)}) copy-start(f32[2,256,128]{2,1,0:T(8,128)S(1)} %collective-permute-done.27.refs_10_) | copy-start | bytes 786436
  146.9 23.3 %collective-permute-start.36 = (f32[4,128,512]{2,1,0:T(8,128)}, f32[4,128,512]{2,1,0:T(8,128)S(1)}, u32[]{:S(2)}, u32[]{:S(2)}) collective-permute-start(f32[4,128,512]{2,1,0:T(8,128)} %get-tuple-element.78), channel_id=1, source_target_pairs={{0,8},{4,36},{8,0},{12,44},{16,24},{20,52},{24,16},{28,60},{32,40}... | collective-permute-start | bytes 3145736 | tf_op jit(solution)/shard_map/ppermute | solution.py:35
  148.5 22.5 %collective-permute-start.37 = (f32[4,128,512]{2,1,0:T(8,128)}, f32[4,128,512]{2,1,0:T(8,128)S(1)}, u32[]{:S(2)}, u32[]{:S(2)}) collective-permute-start(f32[4,128,512]{2,1,0:T(8,128)} %get-tuple-element.79), channel_id=1, source_target_pairs={{0,24},{4,100},{8,16},{12,108},{16,8},{20,116},{24,0},{28,124},{32... | collective-permute-start | bytes 3145736 | tf_op jit(solution)/shard_map/ppermute | solution.py:35
  155.2 18.1 %collective-permute-start.29 = (f32[4,128,512]{2,1,0:T(8,128)}, f32[4,128,512]{2,1,0:T(8,128)S(1)}, u32[]{:S(2)}, u32[]{:S(2)}) collective-permute-start(f32[4,128,512]{2,1,0:T(8,128)} %get-tuple-element.69), channel_id=1, source_target_pairs={{0,8},{4,36},{8,0},{12,44},{16,24},{20,52},{24,16},{28,60},{32,40}... | collective-permute-start | bytes 3145736 | tf_op jit(solution)/shard_map/ppermute | solution.py:35
  156.4 19.8 %collective-permute-start.30 = (f32[4,128,512]{2,1,0:T(8,128)}, f32[4,128,512]{2,1,0:T(8,128)S(1)}, u32[]{:S(2)}, u32[]{:S(2)}) collective-permute-start(f32[4,128,512]{2,1,0:T(8,128)} %get-tuple-element.70), channel_id=1, source_target_pairs={{0,24},{4,100},{8,16},{12,108},{16,8},{20,116},{24,0},{28,124},{32... | collective-permute-start | bytes 3145736 | tf_op jit(solution)/shard_map/ppermute | solution.py:35
  163.8 6.3 %copy-start.15 = (f32[2,128,512]{2,1,0:T(8,128)S(1)}, f32[2,128,512]{2,1,0:T(8,128)}, u32[]{:S(2)}) copy-start(f32[2,128,512]{2,1,0:T(8,128)} %get-tuple-element.81) | copy-start | bytes 1572868
  163.9 7.1 %copy-start.14 = (f32[2,128,512]{2,1,0:T(8,128)S(1)}, f32[2,128,512]{2,1,0:T(8,128)}, u32[]{:S(2)}) copy-start(f32[2,128,512]{2,1,0:T(8,128)} %get-tuple-element.80) | copy-start | bytes 1572868
  170.1 6.2 %copy-start.13 = (f32[2,128,512]{2,1,0:T(8,128)S(1)}, f32[2,128,512]{2,1,0:T(8,128)}, u32[]{:S(2)}) copy-start(f32[2,128,512]{2,1,0:T(8,128)} %get-tuple-element.71) | copy-start | bytes 1572868
  170.1 10.3 %copy-start.2 = (f32[4,128,512]{2,1,0:T(8,128)}, f32[4,128,512]{2,1,0:T(8,128)S(1)}, u32[]{:S(2)}) copy-start(f32[4,128,512]{2,1,0:T(8,128)S(1)} %collective-permute-done.36.from_one) | copy-start | bytes 3145732
  170.2 10.1 %collective-permute-start.39 = (f32[2,128,512]{2,1,0:T(8,128)S(1)}, f32[2,128,512]{2,1,0:T(8,128)S(1)}, u32[]{:S(2)}, u32[]{:S(2)}) collective-permute-start(f32[2,128,512]{2,1,0:T(8,128)S(1)} %slice_add_fusion), channel_id=1, source_target_pairs={{0,24},{4,100},{8,16},{12,108},{16,8},{20,116},{24,0},{28,124},{32... | collective-permute-start | bytes 1572872 | tf_op jit(solution)/shard_map/ppermute | solution.py:35
  171.0 9.5 %copy-start.3 = (f32[4,128,512]{2,1,0:T(8,128)}, f32[4,128,512]{2,1,0:T(8,128)S(1)}, u32[]{:S(2)}) copy-start(f32[4,128,512]{2,1,0:T(8,128)S(1)} %collective-permute-done.37.from_three) | copy-start | bytes 3145732
  171.1 9.4 %collective-permute-start.38 = (f32[2,128,512]{2,1,0:T(8,128)S(1)}, f32[2,128,512]{2,1,0:T(8,128)S(1)}, u32[]{:S(2)}, u32[]{:S(2)}) collective-permute-start(f32[2,128,512]{2,1,0:T(8,128)S(1)} %slice_add_fusion.1), channel_id=1, source_target_pairs={{0,8},{4,36},{8,0},{12,44},{16,24},{20,52},{24,16},{28,60},{32,40}... | collective-permute-start | bytes 1572872 | tf_op jit(solution)/shard_map/ppermute | solution.py:35
  173.3 16.1 %copy-start = (f32[4,128,512]{2,1,0:T(8,128)}, f32[4,128,512]{2,1,0:T(8,128)S(1)}, u32[]{:S(2)}) copy-start(f32[4,128,512]{2,1,0:T(8,128)S(1)} %collective-permute-done.29.from_one) | copy-start | bytes 3145732
  174.8 14.6 %collective-permute-start.32 = (f32[2,128,512]{2,1,0:T(8,128)S(1)}, f32[2,128,512]{2,1,0:T(8,128)S(1)}, u32[]{:S(2)}, u32[]{:S(2)}) collective-permute-start(f32[2,128,512]{2,1,0:T(8,128)S(1)} %slice_add_fusion.2), channel_id=1, source_target_pairs={{0,24},{4,100},{8,16},{12,108},{16,8},{20,116},{24,0},{28,124},{32... | collective-permute-start | bytes 1572872 | tf_op jit(solution)/shard_map/ppermute | solution.py:35
  176.3 13.1 %copy-start.1 = (f32[4,128,512]{2,1,0:T(8,128)}, f32[4,128,512]{2,1,0:T(8,128)S(1)}, u32[]{:S(2)}) copy-start(f32[4,128,512]{2,1,0:T(8,128)S(1)} %collective-permute-done.30.from_three) | copy-start | bytes 3145732
  176.3 13.0 %collective-permute-start.31 = (f32[2,128,512]{2,1,0:T(8,128)S(1)}, f32[2,128,512]{2,1,0:T(8,128)S(1)}, u32[]{:S(2)}, u32[]{:S(2)}) collective-permute-start(f32[2,128,512]{2,1,0:T(8,128)S(1)} %slice_add_fusion.3), channel_id=1, source_target_pairs={{0,8},{4,36},{8,0},{12,44},{16,24},{20,52},{24,16},{28,60},{32,40}... | collective-permute-start | bytes 1572872 | tf_op jit(solution)/shard_map/ppermute | solution.py:35
  184.6 12.5 %collective-permute-start.40 = (f32[128,512]{1,0:T(8,128)}, f32[128,512]{1,0:T(8,128)S(1)}, u32[]{:S(2)}, u32[]{:S(2)}) collective-permute-start(f32[128,512]{1,0:T(8,128)} %get-tuple-element.83), channel_id=1, source_target_pairs={{0,32},{4,12},{8,40},{12,4},{16,48},{20,28},{24,56},{28,20},{32,0}... | collective-permute-start | bytes 786440 | tf_op jit(solution)/shard_map/ppermute | solution.py:35
  184.6 17.0 %collective-permute-start.41 = (f32[128,512]{1,0:T(8,128)}, f32[128,512]{1,0:T(8,128)S(1)}, u32[]{:S(2)}, u32[]{:S(2)}) collective-permute-start(f32[128,512]{1,0:T(8,128)} %get-tuple-element.84), channel_id=1, source_target_pairs={{0,64},{4,20},{8,72},{12,28},{16,80},{20,4},{24,88},{28,12},{32,96... | collective-permute-start | bytes 786440 | tf_op jit(solution)/shard_map/ppermute | solution.py:35
  188.2 13.4 %collective-permute-start.42 = (f32[128,512]{1,0:T(8,128)}, f32[128,512]{1,0:T(8,128)S(1)}, u32[]{:S(2)}, u32[]{:S(2)}) collective-permute-start(f32[128,512]{1,0:T(8,128)} %get-tuple-element.85), channel_id=1, source_target_pairs={{0,96},{4,28},{8,104},{12,20},{16,112},{20,12},{24,120},{28,4},{32... | collective-permute-start | bytes 786440 | tf_op jit(solution)/shard_map/ppermute | solution.py:35
  193.6 8.0 %collective-permute-start.33 = (f32[128,512]{1,0:T(8,128)}, f32[128,512]{1,0:T(8,128)S(1)}, u32[]{:S(2)}, u32[]{:S(2)}) collective-permute-start(f32[128,512]{1,0:T(8,128)} %get-tuple-element.74), channel_id=1, source_target_pairs={{0,32},{4,12},{8,40},{12,4},{16,48},{20,28},{24,56},{28,20},{32,0}... | collective-permute-start | bytes 786440 | tf_op jit(solution)/shard_map/ppermute | solution.py:35
  193.6 11.0 %collective-permute-start.34 = (f32[128,512]{1,0:T(8,128)}, f32[128,512]{1,0:T(8,128)S(1)}, u32[]{:S(2)}, u32[]{:S(2)}) collective-permute-start(f32[128,512]{1,0:T(8,128)} %get-tuple-element.75), channel_id=1, source_target_pairs={{0,64},{4,20},{8,72},{12,28},{16,80},{20,4},{24,88},{28,12},{32,96... | collective-permute-start | bytes 786440 | tf_op jit(solution)/shard_map/ppermute | solution.py:35
  197.1 10.2 %copy-start.28 = (f32[128,512]{1,0:T(8,128)}, f32[128,512]{1,0:T(8,128)S(1)}, u32[]{:S(2)}) copy-start(f32[128,512]{1,0:T(8,128)S(1)} %collective-permute-done.40.refs_5_) | copy-start | bytes 786436
  197.1 10.2 %collective-permute-start.35 = (f32[128,512]{1,0:T(8,128)}, f32[128,512]{1,0:T(8,128)S(1)}, u32[]{:S(2)}, u32[]{:S(2)}) collective-permute-start(f32[128,512]{1,0:T(8,128)} %get-tuple-element.76), channel_id=1, source_target_pairs={{0,96},{4,28},{8,104},{12,20},{16,112},{20,12},{24,120},{28,4},{32... | collective-permute-start | bytes 786440 | tf_op jit(solution)/shard_map/ppermute | solution.py:35
  201.6 5.7 %copy-start.29 = (f32[128,512]{1,0:T(8,128)}, f32[128,512]{1,0:T(8,128)S(1)}, u32[]{:S(2)}) copy-start(f32[128,512]{1,0:T(8,128)S(1)} %collective-permute-done.41.refs_6_) | copy-start | bytes 786436
  (22 other events, 39.9 us)

commit v3 on v2

--- a/solution.py
+++ b/solution.py
@@ -29,6 +29,20 @@
 
 
 FIRST, SECOND = 0, 1
+CUTS = (0, 512, 1024)
+
+
+def groups(ring):
+    lines = []
+    for fixed_at in range(SIDE):
+        for c in range(2):
+            along_y = c == ring
+            lines.append([place(fixed_at, i, c) if along_y else place(i, fixed_at, c) for i in range(SIDE)])
+    return lines
+
+
+def exchange(value, ring):
+    return lax.all_to_all(value, "row", 0, 0, tiled=True, axis_index_groups=groups(ring))
 
 
 def hop(value, ring, step):
@@ -172,19 +186,19 @@
 
     @pl.when(step == pl.num_programs(0) - 1)
     def _():
-        core, first, second = where_ref[0], where_ref[1], where_ref[2]
+        core, second = where_ref[0], where_ref[2]
         group = 64
         copies = []
         for m in (2, 1, 3, 0):
             for k in range(SIDE):
-                outer, inner = jnp.where(core == 0, second ^ m, first ^ k), jnp.where(core == 0, first ^ k, second ^ m)
+                outer, inner = jnp.where(core == 0, second ^ m, k), jnp.where(core == 0, k, second ^ m)
                 start = (outer * 8 + inner * 2 + chunk) * owned
 
                 @pl.loop(0, owned // group)
                 def _(number):
                     for lane in range(group):
                         at = number * group + lane
-                        picked_ref[m, pl.ds(k * owned + at, 1), :] = mixed_ref[pl.ds(index_ref[start + at], 1), :]
+                        picked_ref[m, k, pl.ds(at, 1), :] = mixed_ref[pl.ds(index_ref[start + at], 1), :]
 
             copies.append(pltpu.make_async_copy(picked_ref.at[m], outs[m], sems.at[m]))
             copies[-1].start()
@@ -200,42 +214,23 @@
         (steps,),
         [pl.BlockSpec((rows // steps, LANE), lambda s, w, i: (s, 0))] * (2 * SIDE),
         [pl.BlockSpec(memory_space=pl.ANY)] * SIDE,
-        [f32(SIDE * owned, LANE)] * SIDE,
+        [f32(SIDE, owned, LANE)] * SIDE,
         scalars=2,
         scratch=[
             pltpu.VMEM((4 * SIDE * rows, LANE), jnp.float32),
-            pltpu.VMEM((SIDE, SIDE * owned, LANE), jnp.float32),
+            pltpu.VMEM((SIDE, SIDE, owned, LANE), jnp.float32),
             pltpu.SemaphoreType.DMA((SIDE,)),
         ],
     )(where, index, *sources)
 
 
-def rows_sum_kernel(*refs):
-    sources, outs = refs[:SIDE], refs[SIDE:]
-    owned = outs[0].shape[0]
-    for k, out_ref in enumerate(outs):
-        here = pl.ds(k * owned, owned)
-        out_ref[...] = (sources[0][here, :] + sources[1][here, :]) + (sources[2][here, :] + sources[3][here, :])
-
-
-def rows_sum(*operands):
-    owned = operands[0].shape[0] // SIDE
-    return call(
-        rows_sum_kernel,
-        (),
-        [fixed(operand.shape) for operand in operands],
-        [fixed((owned, LANE))] * SIDE,
-        [f32(owned, LANE)] * SIDE,
-    )(*operands)
-
-
 def sketch_kernel(where_ref, mine_zero, mine_one, sibling_zero, sibling_one, out_ref):
-    core, first, second = where_ref[0], where_ref[1], where_ref[2]
-    for step in range(SIDE):
-        mine = jnp.where(core == 0, mine_zero[step], mine_one[step])
-        theirs = jnp.where(core == 0, sibling_zero[step], sibling_one[step])
-        for block, value in ((2 * (first ^ step) + core, mine), (2 * (second ^ step) + 1 - core, theirs)):
-            out_ref[:, pl.ds(pl.multiple_of(block * LANE, LANE), LANE)] = value
+    core = where_ref[0]
+    for j in range(SIDE):
+        mine = jnp.where(core == 0, mine_zero[j], mine_one[j])
+        theirs = jnp.where(core == 0, sibling_zero[j], sibling_one[j])
+        out_ref[:, pl.ds(2 * j * LANE, LANE)] = jnp.where(core == 0, mine, theirs)
+        out_ref[:, pl.ds((2 * j + 1) * LANE, LANE)] = jnp.where(core == 0, theirs, mine)
 
 
 def sketch_rows(where, *operands):
@@ -251,36 +246,34 @@
     )(where, *operands)
 
 
-def gram_kernel(half, plan, where_ref, *refs):
-    inputs, outs = refs[:12], refs[12 : 12 + len(plan)]
-    right_in, left_in, *held, right_sems, left_sems, out_sems = refs[12 + len(plan) :]
+def gram_kernel(plan, where_ref, *refs):
+    inputs, outs = refs[:12], refs[12 : 12 + 2 * len(plan)]
+    right_in, left_in, *held, right_sems, left_sems, out_sems = refs[12 + 2 * len(plan) :]
     core, first, second, me = (where_ref[i] for i in range(4))
     owned = right_in.shape[0] // 2
     blocks = [(number, block) for number, entries in enumerate(plan) for block in entries]
 
-    def right_copy(chunk, number, side):
-        mine, sibling = inputs[6 * chunk], inputs[6 * chunk + 1]
-        j = 2 * half + number
-        source = (mine.at[first ^ j], sibling.at[second ^ j])[side]
-        block = 2 * number + jnp.where(side == 0, core, 1 - core)
+    def right_copy(chunk, j, side):
+        source = inputs[6 * chunk + side].at[j]
+        block = 2 * j + jnp.where(side == 0, core, 1 - core)
         rows, lanes = pl.ds(chunk * owned, owned), pl.ds(pl.multiple_of(block * LANE, LANE), LANE)
-        return pltpu.make_async_copy(source, right_in.at[rows, lanes], right_sems.at[chunk, number, side])
-
-    rights = [right_copy(chunk, number, side) for chunk in range(2) for number in range(2) for side in range(2)]
+        return pltpu.make_async_copy(source, right_in.at[rows, lanes], right_sems.at[chunk, j, side])
+
+    rights = [right_copy(chunk, j, side) for chunk in range(2) for j in range(SIDE) for side in range(2)]
     for copy in rights:
         copy.start()
     lefts = []
     for slot, (_, (k, m)) in enumerate(blocks):
         column = jnp.where(core == 0, second ^ m, first ^ k)
-        step = jnp.where(core == 0, k, first ^ second ^ m)
+        j = jnp.where(core == 0, first ^ k, second ^ m)
         distance = lax.rem(me + SIDE - column, SIDE)
         for chunk in range(2):
             mine, _, right, left, far_a, far_b = inputs[6 * chunk : 6 * chunk + 6]
             target = left_in.at[slot, pl.ds(chunk * owned, owned), :]
             sem = left_sems.at[slot, chunk]
-            cases = [(distance == 0, mine, step), (distance == 1, right, step), (distance == 3, left, step)]
-            cases.append(((distance == 2) & (step < 2), far_a, jnp.minimum(step, 1)))
-            cases.append(((distance == 2) & (step >= 2), far_b, jnp.maximum(step, 2) - 2))
+            cases = [(distance == 0, mine, j), (distance == 1, right, j), (distance == 3, left, j)]
+            cases.append(((distance == 2) & (j < 2), far_a, jnp.minimum(j, 1)))
+            cases.append(((distance == 2) & (j >= 2), far_b, jnp.maximum(j, 2) - 2))
             for chosen, ref, at in cases:
 
                 @pl.when(chosen)
@@ -302,76 +295,45 @@
         for copy in lefts[2 * base : 2 * (base + group)]:
             copy.wait()
         high, low = split(jnp.concatenate([left_in[base + i] for i in range(group)], axis=1))
-        value = product(high, right_high) + product(low, right_high) + product(high, right_low)
-        for i in range(group):
-            number = blocks[base + i][0]
-            held[number][done[number]] = value[i * LANE : (i + 1) * LANE]
-            done[number] += 1
-            if done[number] == len(plan[number]):
-                copies.append(pltpu.make_async_copy(held[number], outs[number], out_sems.at[number]))
-                copies[-1].start()
+        for half in range(2):
+            here = slice(CUTS[half], CUTS[half + 1])
+            value = product(high, right_high[:, here]) + product(low, right_high[:, here])
+            value += product(high, right_low[:, here])
+            at = list(done)
+            for i in range(group):
+                number = blocks[base + i][0]
+                slot = 2 * number + half
+                held[slot][at[number]] = value[i * LANE : (i + 1) * LANE]
+                at[number] += 1
+                if at[number] == len(plan[number]):
+                    copies.append(pltpu.make_async_copy(held[slot], outs[slot], out_sems.at[slot]))
+                    copies[-1].start()
+        done = at
     for copy in copies:
         copy.wait()
 
 
-def gram_shares(where, operands, half, plan):
+def gram_shares(where, operands, plan):
     owned = operands[0].shape[1]
-    wide = SIDE * LANE
-    shapes = [(len(entries), LANE, wide) for entries in plan]
+    shapes = [(len(entries), LANE, CUTS[half + 1] - CUTS[half]) for entries in plan for half in range(2)]
     slots = sum(len(entries) for entries in plan)
     return call(
-        functools.partial(gram_kernel, half, plan),
+        functools.partial(gram_kernel, plan),
         (),
         [pl.BlockSpec(memory_space=pltpu.SMEM)] + [pl.BlockSpec(memory_space=pl.ANY)] * len(operands),
-        [pl.BlockSpec(memory_space=pl.ANY)] * len(plan),
+        [pl.BlockSpec(memory_space=pl.ANY)] * len(shapes),
         [f32(*shape) for shape in shapes],
         scratch=[
-            pltpu.VMEM((2 * owned, wide), jnp.float32),
+            pltpu.VMEM((2 * owned, CUTS[-1]), jnp.float32),
             pltpu.VMEM((slots, 2 * owned, LANE), jnp.float32),
             *[pltpu.VMEM(shape, jnp.float32) for shape in shapes],
-            pltpu.SemaphoreType.DMA((2, 2, 2)),
+            pltpu.SemaphoreType.DMA((2, SIDE, 2)),
             pltpu.SemaphoreType.DMA((slots, 2)),
-            pltpu.SemaphoreType.DMA((len(plan),)),
+            pltpu.SemaphoreType.DMA((len(shapes),)),
         ],
-        flops=3 * 2**29,
-        moved=5 * 2**20,
+        flops=3 * 2**30,
+        moved=2**23,
     )(where, *operands)
-
-
-def ring_sum_kernel(kept_ref, from_one, from_three, last_one, last_three, *outs):
-    for side, (early, late) in enumerate(((from_one, last_three), (from_three, last_one))):
-        for part in range(2):
-            outs[2 * side + part][...] = kept_ref[2 * side + part] + early[2 + part] + late[part]
-
-
-def ring_sum(*operands):
-    wide = operands[0].shape[-1]
-    return call(
-        ring_sum_kernel,
-        (),
-        [fixed(operand.shape) for operand in operands],
-        [fixed((LANE, wide))] * SIDE,
-        [f32(LANE, wide)] * SIDE,
-    )(*operands)
-
-
-def combine_kernel(*refs):
-    out_ref = refs[-1]
-    wide = refs[0].shape[1]
-    for half in range(2):
-        a, b, c, d = refs[SIDE * half : SIDE * half + SIDE]
-        out_ref[:, pl.ds(half * wide, wide)] = (a[...] + b[...]) + (c[...] + d[...])
-
-
-def combine(*operands):
-    rows, wide = operands[0].shape
-    return call(
-        combine_kernel,
-        (),
-        [fixed(operand.shape) for operand in operands],
-        fixed((rows, 2 * wide)),
-        f32(rows, 2 * wide),
-    )(*operands)
 
 
 def sample_index(sample_rows, z, y, core):
@@ -399,16 +361,22 @@
     scale = float(np.float32(1.0) / np.sqrt(np.float32(total)))
 
     table = jnp.asarray(hadamard(256), jnp.bfloat16)
+    pieces = local_transform(where, design, signs[None, :], table)
+    own, theirs = pieces[:SIDE], list(pieces[SIDE:])
+    sample_rows, _ = lax.optimization_barrier((sample_rows, own[0]))
     index = sample_index(sample_rows, z, y, core)
-    pieces = local_transform(where, design, signs[None, :], table)
-    sources = [pieces[0]] + [hop(pieces[step], FIRST, step) for step in (1, 2, 3)]
-    sources += [across(pieces[SIDE + step], step) for step in range(SIDE)]
+    index, theirs[0], theirs[3] = lax.optimization_barrier((index, theirs[0], theirs[3]))
+    sources = [own[0]] + [hop(own[step], FIRST, step) for step in (1, 2, 3)]
+    sources += [across(theirs[step], step) for step in range(SIDE)]
 
     gathered = []
     for chunk in range(2):
         picked = sampled_rows(where, index, sources, scale, chunk, owned)
-        sums = rows_sum(picked[0], *[hop(picked[step], SECOND, step) for step in (1, 2, 3)])
-        mine = jnp.stack([sums[0]] + [hop(sums[step], FIRST, step) for step in (1, 2, 3)])
+        arrived = [hop(picked[step], SECOND, step) for step in (1, 2, 3)]
+        sums = (picked[0] + arrived[0]) + (arrived[1] + arrived[2])
+        mine = exchange(sums, FIRST)
+        if gathered:
+            mine, *_ = lax.optimization_barrier((mine, gathered[0][2], gathered[0][3]))
         right, left = around(mine, 1), around(mine, 3)
         far_a, far_b = around(right[: SIDE // 2], 1), around(left[SIDE // 2 :], 3)
         gathered.append((mine, to_sibling(mine), right, left, far_a, far_b))
@@ -421,17 +389,20 @@
     def blocks(*entries):
         return [(first, second) for first, seconds in entries for second in seconds]
 
-    early = [gram_shares(where, operands, half, [blocks((2, low), (1, low)), blocks((2, high), (3, high))]) for half in range(2)]
-    late_plan = [blocks((1, high)), blocks((3, low)), blocks((0, low), (0, high))]
-    late = [gram_shares(where, operands, half, late_plan) for half in range(2)]
+    early = gram_shares(where, operands, [blocks((2, low), (1, low)), blocks((2, high), (3, high))])
+    late = gram_shares(where, operands, [blocks((1, high)), blocks((3, low)), blocks((0, low), (0, high))])
     parts = []
-    for (to_one, to_three), (rest_one, rest_three, here) in zip(early, late):
+    for half in range(2):
+        to_one, to_three = early[half::2]
+        rest_one, rest_three, here = late[half::2]
         from_one, from_three = hop(to_one, FIRST, 1), hop(to_three, FIRST, 3)
         last_one = hop(rest_one + from_three[:2], FIRST, 1)
         last_three = hop(rest_three + from_one[:2], FIRST, 3)
-        sums = ring_sum(here, from_one, from_three, last_one, last_three)
-        parts += [sums[0]] + [hop(sums[step], SECOND, step) for step in (1, 2, 3)]
-    return (sketch, combine(*parts))
+        sums = [here[0] + from_one[2] + last_three[0], here[1] + from_one[3] + last_three[1]]
+        sums += [here[2] + from_three[2] + last_one[0], here[3] + from_three[3] + last_one[1]]
+        arrived = [hop(sums[step], SECOND, step) for step in (1, 2, 3)]
+        parts.append((sums[0] + arrived[0]) + (arrived[1] + arrived[2]))
+    return (sketch, jnp.concatenate(parts, axis=1))
 
 
 def solution(mesh):

time: 213 us -> 199 us (0.934)
  Pallas kernels: 66.6 us -> 45.3 us
  waiting for transfers between devices: 62.8 us -> 52.3 us
  starting transfers between devices: 52.4 us -> 61.3 us
  other arithmetic: 4.88 us -> 12.2 us
  blocking collectives: 15.8 us -> 22.5 us
  local copies, waits for them, and re-layouts: 6.73 us -> 2.29 us
    pallas_call x9 -> x2, Pallas kernels: 38 us -> 16.8 us  [gram_shares(): call(functools.partial(gram_kernel, plan), (), [pl.BlockSpec(memory_space...]
    ppermute x29 -> x23, waiting for transfers between devices: 37.2 us -> 20.4 us  [hop(): return lax.ppermute(value, 'row', partners(ring, step))]
    ppermute x4, waiting for transfers between devices: 0.01 us -> 10.9 us  [across(): lax.ppermute(value, 'row', [(i ^ 1, j) for i, j in partners(FIRST, step)])]
    ppermute x8, waiting for transfers between devices: 25.6 us -> 16.8 us  [around(): lax.ppermute(value, 'col', [(i, (i + step) % SIDE) for i in range(SIDE)])]
    all_to_all x0 -> x1, starting transfers between devices: none -> 7.43 us  [sample_index(): wanted = lax.all_to_all(spread, 'row', 0, 0, tiled=True).reshape(-1)]
    all_to_all x1 -> x2, blocking collectives: 15.8 us -> 22.5 us  [exchange(): lax.all_to_all(value, 'row', 0, 0, tiled=True, axis_index_groups=groups(r...]
    unnamed x86 -> x48, local copies, waits for them, and re-layouts: 6.64 us -> 1.6 us
    all_to_all x0 -> x1, waiting for transfers between devices: none -> 4.24 us  [sample_index(): wanted = lax.all_to_all(spread, 'row', 0, 0, tiled=True).reshape(-1)]
  transfers between devices with their start and end apart: 43 -> 38, of which waited for: 18 -> 18; matrix products, arithmetic and copies ran while one was open for 2% -> 6% of each run, Pallas kernels for 20% -> 11%
where the time goes in v3:
time: 199 us; the launch traced here: 197 us
  starting transfers between devices  61.3 us (31%)
  waiting for transfers between devices  52.3 us (26%)
  Pallas kernels  45.3 us (23%)
  blocking collectives  22.5 us (11%)
  other arithmetic  12.2 us (6%)
  local copies, waits for them, and re-layouts  2.29 us (1%)
    ppermute x23, starting transfers between devices, hop(): return lax.ppermute(value, 'row', partners(ring, step))  39 us
    all_to_all x2, blocking collectives, exchange(): lax.all_to_all(value, 'row', 0, 0, tiled=True, axis_index_groups=groups(r...  22.5 us
    ppermute x23, waiting for transfers between devices, hop(): return lax.ppermute(value, 'row', partners(ring, step))  20.4 us
    pallas_call x2, Pallas kernels, sampled_rows(): call(functools.partial(sample_kernel, scale, chunk, owned), (steps,), [pl...  18.7 us
    pallas_call x2, Pallas kernels, gram_shares(): call(functools.partial(gram_kernel, plan), (), [pl.BlockSpec(memory_space...  16.8 us
    ppermute x8, waiting for transfers between devices, around(): lax.ppermute(value, 'col', [(i, (i + step) % SIDE) for i in range(SIDE)])  16.8 us
    ppermute x4, waiting for transfers between devices, across(): lax.ppermute(value, 'row', [(i ^ 1, j) for i, j in partners(FIRST, step)])  10.9 us
    ppermute x8, starting transfers between devices, around(): lax.ppermute(value, 'col', [(i, (i + step) % SIDE) for i in range(SIDE)])  8.99 us
  transfers between devices with their start and end apart: 38, of which 18 were waited for; matrix products, arithmetic and copies ran while one was open for 6% of the time, Pallas kernels for 11%

profile of v3, /device:TPU:14, one launch (start us, length us, event | category | flops | bytes accessed | tf_op | source)
XLA Modules:
  0.0 196.9 jit_solution(15504519608407486957)
XLA Ops:
  0.7 0.7 pad_add_fusion._.where_ref
  1.3 6.6 %shard_map.59 = (f32[1024,128]{1,0:T(8,128)}, f32[1024,128]{1,0:T(8,128)}, f32[1024,128]{1,0:T(8,128)}, f32[1024,128]{1,0:T(8,128)}, f32[1024,128]{1,0:T(8,128)}...) custom-call(s32[4]{0:T(128)} %pad_add_fusion._.where_ref, ...), custom_call_target="tpu_custom_call" | custom-call | flops 1073741824 | bytes 8388608 | tf_op jit(solution)/shard_map/pallas_call | solution.py:147
  8.4 2.6 %collective-permute-start.1 = (f32[1024,128]{1,0:T(8,128)}, f32[1024,128]{1,0:T(8,128)S(1)}, u32[]{:S(2)}, u32[]{:S(2)}) collective-permute-start(f32[1024,128]{1,0:T(8,128)} %get-tuple-element.39), channel_id=1, source_target_pairs={{0,16},{4,68},{8,24},{12,76},{16,0},{20,84},{24,8},{28,92},{32,48}... | collective-permute-start | bytes 1572872 | tf_op jit(solution)/shard_map/ppermute | solution.py:49
  11.0 0.6 broadcast_in_dim.7
  11.7 7.4 %all-to-all-start = ((s32[32,1,256]{2,1,0:T(1,128)}), s32[32,1,256]{2,1,0:T(1,128)S(1)}, u32[]{:S(2)}, u32[]{:S(2)}) async-start(s32[32,1,256]{2,1,0:T(1,128)} %broadcast_in_dim.7), calls=%async_computation | async-start | bytes 65536 | tf_op jit(solution)/shard_map/all_to_all | solution.py:342
  19.1 1.5 collective-permute-start.2
  20.6 0.9 collective-permute-start.4
  21.6 3.5 %collective-permute-start.5 = (f32[1024,128]{1,0:T(8,128)}, f32[1024,128]{1,0:T(8,128)S(1)}, u32[]{:S(2)}, u32[]{:S(2)}) collective-permute-start(f32[1024,128]{1,0:T(8,128)} %get-tuple-element.43), channel_id=1, source_target_pairs={{4,16},{0,68},{12,24},{8,76},{20,0},{16,84},{28,8},{24,92},{36,48}... | collective-permute-start | bytes 1572872 | tf_op jit(solution)/shard_map/ppermute | solution.py:57
  25.1 4.2 %all-to-all-done = s32[32,1,256]{2,1,0:T(1,128)S(1)} async-done(((s32[32,1,256]{2,1,0:T(1,128)}), s32[32,1,256]{2,1,0:T(1,128)S(1)}, u32[]{:S(2)}, u32[]{:S(2)}) %all-to-all-start) | async-done | bytes 32800 | tf_op jit(solution)/shard_map/all_to_all | solution.py:342
  29.4 0.7 fusion.13.index_ref
  30.2 0.7 collective-permute-start.6
  30.9 5.3 %collective-permute-done.5.refs_6_ = f32[1024,128]{1,0:T(8,128)S(1)} collective-permute-done((f32[1024,128]{1,0:T(8,128)}, f32[1024,128]{1,0:T(8,128)S(1)}, u32[]{:S(2)}, u32[]{:S(2)}) %collective-permute-start.5) | collective-permute-done | bytes 524320 | tf_op jit(solution)/shard_map/ppermute | solution.py:57
  36.3 5.5 %collective-permute-done.6.refs_7_ = f32[1024,128]{1,0:T(8,128)S(1)} collective-permute-done((f32[1024,128]{1,0:T(8,128)}, f32[1024,128]{1,0:T(8,128)S(1)}, u32[]{:S(2)}, u32[]{:S(2)}) %collective-permute-start.6) | collective-permute-done | bytes 524320 | tf_op jit(solution)/shard_map/ppermute | solution.py:57
  41.8 0.8 copy-done.6
  42.6 9.3 %shard_map.60 = (f32[4,256,128]{2,1,0:T(8,128)}, f32[4,256,128]{2,1,0:T(8,128)}, f32[4,256,128]{2,1,0:T(8,128)}, f32[4,256,128]{2,1,0:T(8,128)}) custom-call(s32[4]{0:T(128)} %pad_add_fusion._.where_ref, s32[8192]{0:T(1024)} %fusion.13.index_ref, f32[1024,128]{1,0:T(8,128)} %get-tuple-element.33.refs_0_, f32[1024,128]{1,0:T(8,128)} %copy-done, ...), custom_call_target="tpu_custom_call" | custom-call | flops 16777216 | bytes 8388608 | tf_op jit(solution)/shard_map/pallas_call | solution.py:212
  52.0 1.4 collective-permute-start.7
  53.4 3.6 %collective-permute-start.8 = (f32[4,256,128]{2,1,0:T(8,128)}, f32[4,256,128]{2,1,0:T(8,128)S(1)}, u32[]{:S(2)}, u32[]{:S(2)}) collective-permute-start(f32[4,256,128]{2,1,0:T(8,128)} %get-tuple-element.47), channel_id=1, source_target_pairs={{0,64},{4,20},{8,72},{12,28},{16,80},{20,4},{24,88},{28,12},{32,96... | collective-permute-start | bytes 1572872 | tf_op jit(solution)/shard_map/ppermute | solution.py:49
  57.0 9.3 %shard_map.61 = (f32[4,256,128]{2,1,0:T(8,128)}, f32[4,256,128]{2,1,0:T(8,128)}, f32[4,256,128]{2,1,0:T(8,128)}, f32[4,256,128]{2,1,0:T(8,128)}) custom-call(s32[4]{0:T(128)} %pad_add_fusion._.where_ref, s32[8192]{0:T(1024)} %fusion.13.index_ref, f32[1024,128]{1,0:T(8,128)} %get-tuple-element.33.refs_0_, f32[1024,128]{1,0:T(8,128)} %copy-done, ...), custom_call_target="tpu_custom_call" | custom-call | flops 16777216 | bytes 8388608 | tf_op jit(solution)/shard_map/pallas_call | solution.py:212
  66.4 4.7 %collective-permute-start.11 = (f32[4,256,128]{2,1,0:T(8,128)}, f32[4,256,128]{2,1,0:T(8,128)S(1)}, u32[]{:S(2)}, u32[]{:S(2)}) collective-permute-start(f32[4,256,128]{2,1,0:T(8,128)} %get-tuple-element.51), channel_id=1, source_target_pairs={{0,64},{4,20},{8,72},{12,28},{16,80},{20,4},{24,88},{28,12},{32,96... | collective-permute-start | bytes 1572872 | tf_op jit(solution)/shard_map/ppermute | solution.py:49
  71.1 2.1 %collective-permute-done.9 = f32[4,256,128]{2,1,0:T(8,128)S(1)} collective-permute-done((f32[4,256,128]{2,1,0:T(8,128)}, f32[4,256,128]{2,1,0:T(8,128)S(1)}, u32[]{:S(2)}, u32[]{:S(2)}) %collective-permute-start.9) | collective-permute-done | bytes 524320 | tf_op jit(solution)/shard_map/ppermute | solution.py:49
  73.3 11.6 %all_to_all.16.mine_zero.refs_0_ = f32[4,256,128]{2,1,0:T(8,128)S(1)} all-to-all(f32[4,256,128]{2,1,0:T(8,128)S(1)} %add_add_fusion.1), channel_id=1, replica_groups={{0,8,16,24},{4,36,68,100},{32,40,48,56},{12,44,76,108},{64,72,80,88},{2..., dimensions={0} | all-to-all | bytes 1048576 | tf_op jit(solution)/shard_map/all_to_all | solution.py:45
  85.4 1.6 collective-permute-start.14
  87.0 3.2 %collective-permute-done.12 = f32[4,256,128]{2,1,0:T(8,128)S(1)} collective-permute-done((f32[4,256,128]{2,1,0:T(8,128)}, f32[4,256,128]{2,1,0:T(8,128)S(1)}, u32[]{:S(2)}, u32[]{:S(2)}) %collective-permute-start.12) | collective-permute-done | bytes 524320 | tf_op jit(solution)/shard_map/ppermute | solution.py:49
  90.2 1.1 add_add_fusion
  91.3 10.9 %all_to_all.17.mine_one.refs_6_ = f32[4,256,128]{2,1,0:T(8,128)S(1)} all-to-all(f32[4,256,128]{2,1,0:T(8,128)S(1)} %add_add_fusion), channel_id=1, replica_groups={{0,8,16,24},{4,36,68,100},{32,40,48,56},{12,44,76,108},{64,72,80,88},{2..., dimensions={0} | all-to-all | bytes 1048576 | tf_op jit(solution)/shard_map/all_to_all | solution.py:45
  102.8 1.5 collective-permute-start.20
  104.9 1.8 collective-permute-start.17
  106.6 8.7 %collective-permute-done.19.refs_8_ = f32[4,256,128]{2,1,0:T(8,128)S(1)} collective-permute-done((f32[4,256,128]{2,1,0:T(8,128)S(1)}, f32[4,256,128]{2,1,0:T(8,128)S(1)}, u32[]{:S(2)}, u32[]{:S(2)}) %collective-permute-start.19) | collective-permute-done | bytes 524320 | tf_op jit(solution)/shard_map/ppermute | solution.py:61
  115.4 0.8 collective-permute-start.18
  116.2 1.0 collective-permute-done.20.refs_9_
  117.3 1.4 collective-permute-start.21
  118.8 0.8 collective-permute-start.22
  119.9 3.0 %collective-permute-done.18.refs_5_ = f32[2,256,128]{2,1,0:T(8,128)S(1)} collective-permute-done((f32[2,256,128]{2,1,0:T(8,128)S(1)}, f32[2,256,128]{2,1,0:T(8,128)S(1)}, u32[]{:S(2)}, u32[]{:S(2)}) %collective-permute-start.18) | collective-permute-done | bytes 262176 | tf_op jit(solution)/shard_map/ppermute | solution.py:61
  123.0 0.7 collective-permute-done.21.refs_10_
  123.6 2.9 %collective-permute-done.22.refs_11_ = f32[2,256,128]{2,1,0:T(8,128)S(1)} collective-permute-done((f32[2,256,128]{2,1,0:T(8,128)S(1)}, f32[2,256,128]{2,1,0:T(8,128)S(1)}, u32[]{:S(2)}, u32[]{:S(2)}) %collective-permute-start.22) | collective-permute-done | bytes 262176 | tf_op jit(solution)/shard_map/ppermute | solution.py:61
  126.7 0.7 copy-done.23
  127.4 8.3 %shard_map.64 = (f32[4,128,512]{2,1,0:T(8,128)}, f32[4,128,512]{2,1,0:T(8,128)}, f32[4,128,512]{2,1,0:T(8,128)}, f32[4,128,512]{2,1,0:T(8,128)}) custom-call(s32[4]{0:T(128)} %pad_add_fusion._.where_ref, f32[4,256,128]{2,1,0:T(8,128)} %copy-done.7, f32[4,256,128]{2,1,0:T(8,128)} %copy-done.13, f32[4,256,128]{2,1,0:T(8,128)} %copy-done.15, ...), custom_call_target="tpu_custom_call" | custom-call | flops 3221225472 | bytes 8388608 | tf_op jit(solution)/shard_map/pallas_call | solution.py:320
  135.8 5.3 %collective-permute-start.23 = (f32[4,128,512]{2,1,0:T(8,128)}, f32[4,128,512]{2,1,0:T(8,128)S(1)}, u32[]{:S(2)}, u32[]{:S(2)}) collective-permute-start(f32[4,128,512]{2,1,0:T(8,128)} %get-tuple-element.55), channel_id=1, source_target_pairs={{0,8},{4,36},{8,0},{12,44},{16,24},{20,52},{24,16},{28,60},{32,40}... | collective-permute-start | bytes 3145736 | tf_op jit(solution)/shard_map/ppermute | solution.py:49
  141.1 0.6 collective-permute-start.26
  141.7 0.7 collective-permute-start.30
  142.4 1.4 collective-permute-start.33
  143.8 8.5 %shard_map.63 = (f32[2,128,512]{2,1,0:T(8,128)}, f32[2,128,512]{2,1,0:T(8,128)}, f32[2,128,512]{2,1,0:T(8,128)}, f32[2,128,512]{2,1,0:T(8,128)}, f32[4,128,512]{2,1,0:T(8,128)}, /*index=5*/f32[4,128,512]{2,1,0:T(8,128)}) custom-call(s32[4]{0:T(128)} %pad_add_fusion._.where_ref, f32[4,256,128]{2,1,0:T(8,128)} %copy-done.7, f32[4,256,128]{2,1,0:T(8,128)} %copy-done.13, ...), custom_call_target="tpu_custom_call" | custom-call | flops 3221225472 | bytes 8388608 | tf_op jit(solution)/shard_map/pallas_call | solution.py:320
  152.3 1.8 collective-permute-done.23
  154.1 2.0 slice_add_fusion.3
  156.0 0.6 collective-permute-start.24
  156.7 1.9 slice_add_fusion.2
  158.6 2.6 %collective-permute-start.27 = (f32[2,128,512]{2,1,0:T(8,128)}, f32[2,128,512]{2,1,0:T(8,128)}, u32[]{:S(2)}, u32[]{:S(2)}) collective-permute-start(f32[2,128,512]{2,1,0:T(8,128)} %slice_add_fusion.2), channel_id=1, source_target_pairs={{0,8},{4,36},{8,0},{12,44},{16,24},{20,52},{24,16},{28,60},{32,40}... | collective-permute-start | bytes 1572872 | tf_op jit(solution)/shard_map/ppermute | solution.py:49
  161.2 4.1 %collective-permute-done.30 = f32[4,128,512]{2,1,0:T(8,128)S(1)} collective-permute-done((f32[4,128,512]{2,1,0:T(8,128)}, f32[4,128,512]{2,1,0:T(8,128)S(1)}, u32[]{:S(2)}, u32[]{:S(2)}) %collective-permute-start.30) | collective-permute-done | bytes 1048608 | tf_op jit(solution)/shard_map/ppermute | solution.py:49
  165.3 1.1 slice_add_fusion.1
  166.5 0.7 collective-permute-start.31
  167.3 0.9 slice_add_fusion
  168.2 2.4 %collective-permute-start.34 = (f32[2,128,512]{2,1,0:T(8,128)}, f32[2,128,512]{2,1,0:T(8,128)}, u32[]{:S(2)}, u32[]{:S(2)}) collective-permute-start(f32[2,128,512]{2,1,0:T(8,128)} %slice_add_fusion), channel_id=1, source_target_pairs={{0,8},{4,36},{8,0},{12,44},{16,24},{20,52},{24,16},{28,60},{32,40}... | collective-permute-start | bytes 1572872 | tf_op jit(solution)/shard_map/ppermute | solution.py:49
  170.7 3.3 %shard_map.62 = f32[256,1024]{1,0:T(8,128)} custom-call(s32[4]{0:T(128)} %pad_add_fusion._.where_ref, f32[4,256,128]{2,1,0:T(8,128)} %copy-done.7, f32[4,256,128]{2,1,0:T(8,128)} %copy-done.8, f32[4,256,128]{2,1,0:T(8,128)} %copy-done.13, f32[4,256,128]{2,1,0:T(8,128)} %copy-done.14), custom_call_target="tpu_custom_call" | custom-call | flops 16777216 | bytes 8388608 | tf_op jit(solution)/shard_map/pallas_call | solution.py:239
  173.9 1.3 fusion.6
  175.2 1.0 collective-permute-start.25
  176.7 3.3 %collective-permute-start.29 = (f32[128,512]{1,0:T(8,128)S(1)}, f32[128,512]{1,0:T(8,128)S(1)}, u32[]{:S(2)}, u32[]{:S(2)}) collective-permute-start(f32[128,512]{1,0:T(8,128)S(1)} %get-tuple-element.64), channel_id=1, source_target_pairs={{0,96},{4,28},{8,104},{12,20},{16,112},{20,12},{24,120},{28,4},{32... | collective-permute-start | bytes 786440 | tf_op jit(solution)/shard_map/ppermute | solution.py:49
  180.0 1.6 collective-permute-done.31
  181.6 1.3 fusion
  182.9 2.6 %collective-permute-start.32 = (f32[128,512]{1,0:T(8,128)S(1)}, f32[128,512]{1,0:T(8,128)S(1)}, u32[]{:S(2)}, u32[]{:S(2)}) collective-permute-start(f32[128,512]{1,0:T(8,128)S(1)} %get-tuple-element.69), channel_id=1, source_target_pairs={{0,32},{4,12},{8,40},{12,4},{16,48},{20,28},{24,56},{28,20},{32,0}... | collective-permute-start | bytes 786440 | tf_op jit(solution)/shard_map/ppermute | solution.py:49
  185.5 2.8 %collective-permute-start.36 = (f32[128,512]{1,0:T(8,128)S(1)}, f32[128,512]{1,0:T(8,128)S(1)}, u32[]{:S(2)}, u32[]{:S(2)}) collective-permute-start(f32[128,512]{1,0:T(8,128)S(1)} %get-tuple-element.66), channel_id=1, source_target_pairs={{0,96},{4,28},{8,104},{12,20},{16,112},{20,12},{24,120},{28,4},{32... | collective-permute-start | bytes 786440 | tf_op jit(solution)/shard_map/ppermute | solution.py:49
  188.4 1.4 collective-permute-done.32
  189.8 3.6 %collective-permute-done.35 = f32[128,512]{1,0:T(8,128)S(1)} collective-permute-done((f32[128,512]{1,0:T(8,128)S(1)}, f32[128,512]{1,0:T(8,128)S(1)}, u32[]{:S(2)}, u32[]{:S(2)}) %collective-permute-start.35) | collective-permute-done | bytes 262176 | tf_op jit(solution)/shard_map/ppermute | solution.py:49
  193.5 2.4 %collective-permute-done.36 = f32[128,512]{1,0:T(8,128)S(1)} collective-permute-done((f32[128,512]{1,0:T(8,128)S(1)}, f32[128,512]{1,0:T(8,128)S(1)}, u32[]{:S(2)}, u32[]{:S(2)}) %collective-permute-start.36) | collective-permute-done | bytes 262176 | tf_op jit(solution)/shard_map/ppermute | solution.py:49
  196.0 0.8 pad_maximum_fusion
  (86 shorter events, 3.9 us)
Async XLA Ops:
  1.3 9.7 %copy-start.19 = (s32[256]{0:T(256)S(1)}, s32[256]{0:T(256)}, u32[]{:S(2)}) copy-start(s32[256]{0:T(256)} %param.6) | copy-start | bytes 3076
  7.9 22.2 %collective-permute-start = (f32[1024,128]{1,0:T(8,128)}, f32[1024,128]{1,0:T(8,128)S(1)}, u32[]{:S(2)}, u32[]{:S(2)}) collective-permute-start(f32[1024,128]{1,0:T(8,128)} %get-tuple-element.38), channel_id=1, source_target_pairs={{0,8},{4,36},{8,0},{12,44},{16,24},{20,52},{24,16},{28,60},{32,40}... | collective-permute-start | bytes 1572872 | tf_op jit(solution)/shard_map/ppermute | solution.py:49
  8.4 21.8 %collective-permute-start.1 = (f32[1024,128]{1,0:T(8,128)}, f32[1024,128]{1,0:T(8,128)S(1)}, u32[]{:S(2)}, u32[]{:S(2)}) collective-permute-start(f32[1024,128]{1,0:T(8,128)} %get-tuple-element.39), channel_id=1, source_target_pairs={{0,16},{4,68},{8,24},{12,76},{16,0},{20,84},{24,8},{28,92},{32,48}... | collective-permute-start | bytes 1572872 | tf_op jit(solution)/shard_map/ppermute | solution.py:49
  11.7 17.7 %all-to-all-start = ((s32[32,1,256]{2,1,0:T(1,128)}), s32[32,1,256]{2,1,0:T(1,128)S(1)}, u32[]{:S(2)}, u32[]{:S(2)}) async-start(s32[32,1,256]{2,1,0:T(1,128)} %broadcast_in_dim.7), calls=%async_computation | async-start | bytes 65536 | tf_op jit(solution)/shard_map/all_to_all | solution.py:342
  19.1 11.8 %collective-permute-start.2 = (f32[1024,128]{1,0:T(8,128)}, f32[1024,128]{1,0:T(8,128)S(1)}, u32[]{:S(2)}, u32[]{:S(2)}) collective-permute-start(f32[1024,128]{1,0:T(8,128)} %get-tuple-element.40), channel_id=1, source_target_pairs={{0,24},{4,100},{8,16},{12,108},{16,8},{20,116},{24,0},{28,124},{32... | collective-permute-start | bytes 1572872 | tf_op jit(solution)/shard_map/ppermute | solution.py:49
  20.6 10.3 %collective-permute-start.4 = (f32[1024,128]{1,0:T(8,128)}, f32[1024,128]{1,0:T(8,128)S(1)}, u32[]{:S(2)}, u32[]{:S(2)}) collective-permute-start(f32[1024,128]{1,0:T(8,128)} %get-tuple-element.42), channel_id=1, source_target_pairs={{4,8},{0,36},{12,0},{8,44},{20,24},{16,52},{28,16},{24,60},{36,40}... | collective-permute-start | bytes 1572872 | tf_op jit(solution)/shard_map/ppermute | solution.py:57
  21.6 14.7 %collective-permute-start.5 = (f32[1024,128]{1,0:T(8,128)}, f32[1024,128]{1,0:T(8,128)S(1)}, u32[]{:S(2)}, u32[]{:S(2)}) collective-permute-start(f32[1024,128]{1,0:T(8,128)} %get-tuple-element.43), channel_id=1, source_target_pairs={{4,16},{0,68},{12,24},{8,76},{20,0},{16,84},{28,8},{24,92},{36,48}... | collective-permute-start | bytes 1572872 | tf_op jit(solution)/shard_map/ppermute | solution.py:57
  30.1 11.7 %copy-start = (f32[1024,128]{1,0:T(8,128)}, f32[1024,128]{1,0:T(8,128)S(1)}, u32[]{:S(2)}) copy-start(f32[1024,128]{1,0:T(8,128)S(1)} %collective-permute-done.refs_1_) | copy-start | bytes 1572868
  30.1 6.2 %collective-permute-start.3 = (f32[1024,128]{1,0:T(8,128)}, f32[1024,128]{1,0:T(8,128)S(1)}, u32[]{:S(2)}, u32[]{:S(2)}) collective-permute-start(f32[1024,128]{1,0:T(8,128)} %get-tuple-element.41), channel_id=1, source_target_pairs={{4,0},{0,4},{12,8},{8,12},{20,16},{16,20},{28,24},{24,28},{36,32},... | collective-permute-start | bytes 1572872 | tf_op jit(solution)/shard_map/ppermute | solution.py:57
  30.2 11.6 %copy-start.1 = (f32[1024,128]{1,0:T(8,128)}, f32[1024,128]{1,0:T(8,128)S(1)}, u32[]{:S(2)}) copy-start(f32[1024,128]{1,0:T(8,128)S(1)} %collective-permute-done.1.refs_2_) | copy-start | bytes 1572868
  30.2 11.6 %collective-permute-start.6 = (f32[1024,128]{1,0:T(8,128)}, f32[1024,128]{1,0:T(8,128)S(1)}, u32[]{:S(2)}, u32[]{:S(2)}) collective-permute-start(f32[1024,128]{1,0:T(8,128)} %get-tuple-element.44), channel_id=1, source_target_pairs={{4,24},{0,100},{12,16},{8,108},{20,8},{16,116},{28,0},{24,124},{36... | collective-permute-start | bytes 1572872 | tf_op jit(solution)/shard_map/ppermute | solution.py:57
  30.9 10.9 %copy-start.2 = (f32[1024,128]{1,0:T(8,128)}, f32[1024,128]{1,0:T(8,128)S(1)}, u32[]{:S(2)}) copy-start(f32[1024,128]{1,0:T(8,128)S(1)} %collective-permute-done.2.refs_3_) | copy-start | bytes 1572868
  30.9 10.9 %copy-start.3 = (f32[1024,128]{1,0:T(8,128)}, f32[1024,128]{1,0:T(8,128)S(1)}, u32[]{:S(2)}) copy-start(f32[1024,128]{1,0:T(8,128)S(1)} %collective-permute-done.4.refs_5_) | copy-start | bytes 1572868
  36.3 5.5 %copy-start.4 = (f32[1024,128]{1,0:T(8,128)}, f32[1024,128]{1,0:T(8,128)S(1)}, u32[]{:S(2)}) copy-start(f32[1024,128]{1,0:T(8,128)S(1)} %collective-permute-done.5.refs_6_) | copy-start | bytes 1572868
  36.3 5.5 %copy-start.5 = (f32[1024,128]{1,0:T(8,128)}, f32[1024,128]{1,0:T(8,128)S(1)}, u32[]{:S(2)}) copy-start(f32[1024,128]{1,0:T(8,128)S(1)} %collective-permute-done.3.refs_4_) | copy-start | bytes 1572868
  41.8 0.8 copy-start.6
  52.0 21.3 %copy-start.11 = (f32[4,256,128]{2,1,0:T(8,128)S(1)}, f32[4,256,128]{2,1,0:T(8,128)}, u32[]{:S(2)}) copy-start(f32[4,256,128]{2,1,0:T(8,128)} %get-tuple-element.45) | copy-start | bytes 1572868
  52.0 19.1 %collective-permute-start.7 = (f32[4,256,128]{2,1,0:T(8,128)}, f32[4,256,128]{2,1,0:T(8,128)S(1)}, u32[]{:S(2)}, u32[]{:S(2)}) collective-permute-start(f32[4,256,128]{2,1,0:T(8,128)} %get-tuple-element.46), channel_id=1, source_target_pairs={{0,32},{4,12},{8,40},{12,4},{16,48},{20,28},{24,56},{28,20},{32,0}... | collective-permute-start | bytes 1572872 | tf_op jit(solution)/shard_map/ppermute | solution.py:49
  53.4 17.7 %collective-permute-start.8 = (f32[4,256,128]{2,1,0:T(8,128)}, f32[4,256,128]{2,1,0:T(8,128)S(1)}, u32[]{:S(2)}, u32[]{:S(2)}) collective-permute-start(f32[4,256,128]{2,1,0:T(8,128)} %get-tuple-element.47), channel_id=1, source_target_pairs={{0,64},{4,20},{8,72},{12,28},{16,80},{20,4},{24,88},{28,12},{32,96... | collective-permute-start | bytes 1572872 | tf_op jit(solution)/shard_map/ppermute | solution.py:49
  57.0 16.2 %collective-permute-start.9 = (f32[4,256,128]{2,1,0:T(8,128)}, f32[4,256,128]{2,1,0:T(8,128)S(1)}, u32[]{:S(2)}, u32[]{:S(2)}) collective-permute-start(f32[4,256,128]{2,1,0:T(8,128)} %get-tuple-element.48), channel_id=1, source_target_pairs={{0,96},{4,28},{8,104},{12,20},{16,112},{20,12},{24,120},{28,4},{32... | collective-permute-start | bytes 1572872 | tf_op jit(solution)/shard_map/ppermute | solution.py:49
  66.3 20.6 %collective-permute-start.10 = (f32[4,256,128]{2,1,0:T(8,128)}, f32[4,256,128]{2,1,0:T(8,128)S(1)}, u32[]{:S(2)}, u32[]{:S(2)}) collective-permute-start(f32[4,256,128]{2,1,0:T(8,128)} %get-tuple-element.50), channel_id=1, source_target_pairs={{0,32},{4,12},{8,40},{12,4},{16,48},{20,28},{24,56},{28,20},{32,0}... | collective-permute-start | bytes 1572872 | tf_op jit(solution)/shard_map/ppermute | solution.py:49
  66.4 20.5 %collective-permute-start.11 = (f32[4,256,128]{2,1,0:T(8,128)}, f32[4,256,128]{2,1,0:T(8,128)S(1)}, u32[]{:S(2)}, u32[]{:S(2)}) collective-permute-start(f32[4,256,128]{2,1,0:T(8,128)} %get-tuple-element.51), channel_id=1, source_target_pairs={{0,64},{4,20},{8,72},{12,28},{16,80},{20,4},{24,88},{28,12},{32,96... | collective-permute-start | bytes 1572872 | tf_op jit(solution)/shard_map/ppermute | solution.py:49
  71.1 19.0 %collective-permute-start.12 = (f32[4,256,128]{2,1,0:T(8,128)}, f32[4,256,128]{2,1,0:T(8,128)S(1)}, u32[]{:S(2)}, u32[]{:S(2)}) collective-permute-start(f32[4,256,128]{2,1,0:T(8,128)} %get-tuple-element.52), channel_id=1, source_target_pairs={{0,96},{4,28},{8,104},{12,20},{16,112},{20,12},{24,120},{28,4},{32... | collective-permute-start | bytes 1572872 | tf_op jit(solution)/shard_map/ppermute | solution.py:49
  84.9 41.7 %copy-start.7 = (f32[4,256,128]{2,1,0:T(8,128)}, f32[4,256,128]{2,1,0:T(8,128)S(1)}, u32[]{:S(2)}) copy-start(f32[4,256,128]{2,1,0:T(8,128)S(1)} %all_to_all.16.mine_zero.refs_0_) | copy-start | bytes 1572868
  84.9 17.3 %collective-permute-start.13 = (f32[4,256,128]{2,1,0:T(8,128)S(1)}, f32[4,256,128]{2,1,0:T(8,128)S(1)}, u32[]{:S(2)}, u32[]{:S(2)}) collective-permute-start(f32[4,256,128]{2,1,0:T(8,128)S(1)} %all_to_all.16.mine_zero.refs_0_), channel_id=1, source_target_pairs={{0,1},{1,2},{2,3},{3,0},{4,5},{5,6},{6,7},{7,4},{8,9},{9,10},{10,1... | collective-permute-start | bytes 1572872 | tf_op jit(solution)/shard_map/ppermute | solution.py:61
  85.4 16.8 %collective-permute-start.14 = (f32[4,256,128]{2,1,0:T(8,128)S(1)}, f32[4,256,128]{2,1,0:T(8,128)S(1)}, u32[]{:S(2)}, u32[]{:S(2)}) collective-permute-start(f32[4,256,128]{2,1,0:T(8,128)S(1)} %all_to_all.16.mine_zero.refs_0_), channel_id=1, source_target_pairs={{0,3},{1,0},{2,1},{3,2},{4,7},{5,4},{6,5},{7,6},{8,11},{9,8},{10,9... | collective-permute-start | bytes 1572872 | tf_op jit(solution)/shard_map/ppermute | solution.py:61
  102.2 24.4 %copy-start.8 = (f32[4,256,128]{2,1,0:T(8,128)}, f32[4,256,128]{2,1,0:T(8,128)S(1)}, u32[]{:S(2)}) copy-start(f32[4,256,128]{2,1,0:T(8,128)S(1)} %all_to_all.17.mine_one.refs_6_) | copy-start | bytes 1572868
  102.2 24.4 %copy-start.15 = (f32[4,256,128]{2,1,0:T(8,128)}, f32[4,256,128]{2,1,0:T(8,128)S(1)}, u32[]{:S(2)}) copy-start(f32[4,256,128]{2,1,0:T(8,128)S(1)} %collective-permute-done.13.refs_2_) | copy-start | bytes 1572868
  102.2 24.4 %copy-start.16 = (f32[4,256,128]{2,1,0:T(8,128)}, f32[4,256,128]{2,1,0:T(8,128)S(1)}, u32[]{:S(2)}) copy-start(f32[4,256,128]{2,1,0:T(8,128)S(1)} %collective-permute-done.14.refs_3_) | copy-start | bytes 1572868
  102.2 13.1 %collective-permute-start.19 = (f32[4,256,128]{2,1,0:T(8,128)S(1)}, f32[4,256,128]{2,1,0:T(8,128)S(1)}, u32[]{:S(2)}, u32[]{:S(2)}) collective-permute-start(f32[4,256,128]{2,1,0:T(8,128)S(1)} %all_to_all.17.mine_one.refs_6_), channel_id=1, source_target_pairs={{0,1},{1,2},{2,3},{3,0},{4,5},{5,6},{6,7},{7,4},{8,9},{9,10},{10,1... | collective-permute-start | bytes 1572872 | tf_op jit(solution)/shard_map/ppermute | solution.py:61
  102.8 14.5 %collective-permute-start.20 = (f32[4,256,128]{2,1,0:T(8,128)S(1)}, f32[4,256,128]{2,1,0:T(8,128)S(1)}, u32[]{:S(2)}, u32[]{:S(2)}) collective-permute-start(f32[4,256,128]{2,1,0:T(8,128)S(1)} %all_to_all.17.mine_one.refs_6_), channel_id=1, source_target_pairs={{0,3},{1,0},{2,1},{3,2},{4,7},{5,4},{6,5},{7,6},{8,11},{9,8},{10,9... | collective-permute-start | bytes 1572872 | tf_op jit(solution)/shard_map/ppermute | solution.py:61
  104.3 14.4 %collective-permute-start.15 = (f32[4,256,128]{2,1,0:T(8,128)S(1)}, f32[4,256,128]{2,1,0:T(8,128)S(1)}, u32[]{:S(2)}, u32[]{:S(2)}) collective-permute-start(f32[4,256,128]{2,1,0:T(8,128)S(1)} %all_to_all.16.mine_zero.refs_0_), channel_id=1, source_target_pairs={{0,4},{4,0},{8,12},{12,8},{16,20},{20,16},{24,28},{28,24},{32,36},... | collective-permute-start | bytes 1572872 | tf_op jit(solution)/shard_map/ppermute | solution.py:53
  104.3 18.6 %collective-permute-start.16 = (f32[4,256,128]{2,1,0:T(8,128)S(1)}, f32[4,256,128]{2,1,0:T(8,128)S(1)}, u32[]{:S(2)}, u32[]{:S(2)}) collective-permute-start(f32[4,256,128]{2,1,0:T(8,128)S(1)} %all_to_all.17.mine_one.refs_6_), channel_id=1, source_target_pairs={{0,4},{4,0},{8,12},{12,8},{16,20},{20,16},{24,28},{28,24},{32,36},... | collective-permute-start | bytes 1572872 | tf_op jit(solution)/shard_map/ppermute | solution.py:53
  104.9 15.0 %collective-permute-start.17 = (f32[2,256,128]{2,1,0:T(8,128)S(1)}, f32[2,256,128]{2,1,0:T(8,128)S(1)}, u32[]{:S(2)}, u32[]{:S(2)}) collective-permute-start(f32[2,256,128]{2,1,0:T(8,128)S(1)} %slice.128), channel_id=1, source_target_pairs={{0,1},{1,2},{2,3},{3,0},{4,5},{5,6},{6,7},{7,4},{8,9},{9,10},{10,1... | collective-permute-start | bytes 786440 | tf_op jit(solution)/shard_map/ppermute | solution.py:61
  115.4 11.2 %copy-start.17 = (f32[4,256,128]{2,1,0:T(8,128)}, f32[4,256,128]{2,1,0:T(8,128)S(1)}, u32[]{:S(2)}) copy-start(f32[4,256,128]{2,1,0:T(8,128)S(1)} %collective-permute-done.19.refs_8_) | copy-start | bytes 1572868
  115.4 7.6 %collective-permute-start.18 = (f32[2,256,128]{2,1,0:T(8,128)S(1)}, f32[2,256,128]{2,1,0:T(8,128)S(1)}, u32[]{:S(2)}, u32[]{:S(2)}) collective-permute-start(f32[2,256,128]{2,1,0:T(8,128)S(1)} %slice.129), channel_id=1, source_target_pairs={{0,3},{1,0},{2,1},{3,2},{4,7},{5,4},{6,5},{7,6},{8,11},{9,8},{10,9... | collective-permute-start | bytes 786440 | tf_op jit(solution)/shard_map/ppermute | solution.py:61
  117.3 9.4 %copy-start.18 = (f32[4,256,128]{2,1,0:T(8,128)}, f32[4,256,128]{2,1,0:T(8,128)S(1)}, u32[]{:S(2)}) copy-start(f32[4,256,128]{2,1,0:T(8,128)S(1)} %collective-permute-done.20.refs_9_) | copy-start | bytes 1572868
  117.3 6.4 %collective-permute-start.21 = (f32[2,256,128]{2,1,0:T(8,128)S(1)}, f32[2,256,128]{2,1,0:T(8,128)S(1)}, u32[]{:S(2)}, u32[]{:S(2)}) collective-permute-start(f32[2,256,128]{2,1,0:T(8,128)S(1)} %slice.130), channel_id=1, source_target_pairs={{0,1},{1,2},{2,3},{3,0},{4,5},{5,6},{6,7},{7,4},{8,9},{9,10},{10,1... | collective-permute-start | bytes 786440 | tf_op jit(solution)/shard_map/ppermute | solution.py:61
  118.8 7.9 %copy-start.13 = (f32[4,256,128]{2,1,0:T(8,128)}, f32[4,256,128]{2,1,0:T(8,128)S(1)}, u32[]{:S(2)}) copy-start(f32[4,256,128]{2,1,0:T(8,128)S(1)} %collective-permute-done.15.sibling_zero.refs_1_) | copy-start | bytes 1572868
  118.8 7.8 %collective-permute-start.22 = (f32[2,256,128]{2,1,0:T(8,128)S(1)}, f32[2,256,128]{2,1,0:T(8,128)S(1)}, u32[]{:S(2)}, u32[]{:S(2)}) collective-permute-start(f32[2,256,128]{2,1,0:T(8,128)S(1)} %slice.131), channel_id=1, source_target_pairs={{0,3},{1,0},{2,1},{3,2},{4,7},{5,4},{6,5},{7,6},{8,11},{9,8},{10,9... | collective-permute-start | bytes 786440 | tf_op jit(solution)/shard_map/ppermute | solution.py:61
  119.9 6.7 %copy-start.20 = (f32[2,256,128]{2,1,0:T(8,128)}, f32[2,256,128]{2,1,0:T(8,128)S(1)}, u32[]{:S(2)}) copy-start(f32[2,256,128]{2,1,0:T(8,128)S(1)} %collective-permute-done.17.refs_4_) | copy-start | bytes 786436
  123.0 3.7 %copy-start.21 = (f32[2,256,128]{2,1,0:T(8,128)}, f32[2,256,128]{2,1,0:T(8,128)S(1)}, u32[]{:S(2)}) copy-start(f32[2,256,128]{2,1,0:T(8,128)S(1)} %collective-permute-done.18.refs_5_) | copy-start | bytes 786436
  123.0 3.7 %copy-start.14 = (f32[4,256,128]{2,1,0:T(8,128)}, f32[4,256,128]{2,1,0:T(8,128)S(1)}, u32[]{:S(2)}) copy-start(f32[4,256,128]{2,1,0:T(8,128)S(1)} %collective-permute-done.16.sibling_one.refs_7_) | copy-start | bytes 1572868
  123.6 3.0 %copy-start.22 = (f32[2,256,128]{2,1,0:T(8,128)}, f32[2,256,128]{2,1,0:T(8,128)S(1)}, u32[]{:S(2)}) copy-start(f32[2,256,128]{2,1,0:T(8,128)S(1)} %collective-permute-done.21.refs_10_) | copy-start | bytes 786436
  126.7 0.7 copy-start.23
  135.8 18.3 %collective-permute-start.23 = (f32[4,128,512]{2,1,0:T(8,128)}, f32[4,128,512]{2,1,0:T(8,128)S(1)}, u32[]{:S(2)}, u32[]{:S(2)}) collective-permute-start(f32[4,128,512]{2,1,0:T(8,128)} %get-tuple-element.55), channel_id=1, source_target_pairs={{0,8},{4,36},{8,0},{12,44},{16,24},{20,52},{24,16},{28,60},{32,40}... | collective-permute-start | bytes 3145736 | tf_op jit(solution)/shard_map/ppermute | solution.py:49
  141.1 15.6 %collective-permute-start.26 = (f32[4,128,512]{2,1,0:T(8,128)}, f32[4,128,512]{2,1,0:T(8,128)S(1)}, u32[]{:S(2)}, u32[]{:S(2)}) collective-permute-start(f32[4,128,512]{2,1,0:T(8,128)} %get-tuple-element.57), channel_id=1, source_target_pairs={{0,24},{4,100},{8,16},{12,108},{16,8},{20,116},{24,0},{28,124},{32... | collective-permute-start | bytes 3145736 | tf_op jit(solution)/shard_map/ppermute | solution.py:49
  141.7 23.6 %collective-permute-start.30 = (f32[4,128,512]{2,1,0:T(8,128)}, f32[4,128,512]{2,1,0:T(8,128)S(1)}, u32[]{:S(2)}, u32[]{:S(2)}) collective-permute-start(f32[4,128,512]{2,1,0:T(8,128)} %get-tuple-element.60), channel_id=1, source_target_pairs={{0,8},{4,36},{8,0},{12,44},{16,24},{20,52},{24,16},{28,60},{32,40}... | collective-permute-start | bytes 3145736 | tf_op jit(solution)/shard_map/ppermute | solution.py:49
  142.4 24.9 %collective-permute-start.33 = (f32[4,128,512]{2,1,0:T(8,128)}, f32[4,128,512]{2,1,0:T(8,128)S(1)}, u32[]{:S(2)}, u32[]{:S(2)}) collective-permute-start(f32[4,128,512]{2,1,0:T(8,128)} %get-tuple-element.62), channel_id=1, source_target_pairs={{0,24},{4,100},{8,16},{12,108},{16,8},{20,116},{24,0},{28,124},{32... | collective-permute-start | bytes 3145736 | tf_op jit(solution)/shard_map/ppermute | solution.py:49
  152.3 15.0 %copy-start.12 = (f32[2,128,512]{2,1,0:T(8,128)S(1)}, f32[2,128,512]{2,1,0:T(8,128)}, u32[]{:S(2)}) copy-start(f32[2,128,512]{2,1,0:T(8,128)} %get-tuple-element.63) | copy-start | bytes 1572868
  156.0 17.9 %copy-start.10 = (f32[4,128,512]{2,1,0:T(8,128)S(1)}, f32[4,128,512]{2,1,0:T(8,128)}, u32[]{:S(2)}) copy-start(f32[4,128,512]{2,1,0:T(8,128)} %get-tuple-element.54) | copy-start | bytes 3145732
  156.0 17.9 %collective-permute-start.24 = (f32[2,128,512]{2,1,0:T(8,128)}, f32[2,128,512]{2,1,0:T(8,128)S(1)}, u32[]{:S(2)}, u32[]{:S(2)}) collective-permute-start(f32[2,128,512]{2,1,0:T(8,128)} %slice_add_fusion.3), channel_id=1, source_target_pairs={{0,24},{4,100},{8,16},{12,108},{16,8},{20,116},{24,0},{28,124},{32... | collective-permute-start | bytes 1572872 | tf_op jit(solution)/shard_map/ppermute | solution.py:49
  158.6 15.3 %collective-permute-start.27 = (f32[2,128,512]{2,1,0:T(8,128)}, f32[2,128,512]{2,1,0:T(8,128)}, u32[]{:S(2)}, u32[]{:S(2)}) collective-permute-start(f32[2,128,512]{2,1,0:T(8,128)} %slice_add_fusion.2), channel_id=1, source_target_pairs={{0,8},{4,36},{8,0},{12,44},{16,24},{20,52},{24,16},{28,60},{32,40}... | collective-permute-start | bytes 1572872 | tf_op jit(solution)/shard_map/ppermute | solution.py:49
  166.4 15.1 %copy-start.9 = (f32[4,128,512]{2,1,0:T(8,128)S(1)}, f32[4,128,512]{2,1,0:T(8,128)}, u32[]{:S(2)}) copy-start(f32[4,128,512]{2,1,0:T(8,128)} %get-tuple-element.59) | copy-start | bytes 3145732
  166.5 15.1 %collective-permute-start.31 = (f32[2,128,512]{2,1,0:T(8,128)S(1)}, f32[2,128,512]{2,1,0:T(8,128)S(1)}, u32[]{:S(2)}, u32[]{:S(2)}) collective-permute-start(f32[2,128,512]{2,1,0:T(8,128)S(1)} %slice_add_fusion.1), channel_id=1, source_target_pairs={{0,24},{4,100},{8,16},{12,108},{16,8},{20,116},{24,0},{28,124},{32... | collective-permute-start | bytes 1572872 | tf_op jit(solution)/shard_map/ppermute | solution.py:49
  168.2 13.3 %collective-permute-start.34 = (f32[2,128,512]{2,1,0:T(8,128)}, f32[2,128,512]{2,1,0:T(8,128)}, u32[]{:S(2)}, u32[]{:S(2)}) collective-permute-start(f32[2,128,512]{2,1,0:T(8,128)} %slice_add_fusion), channel_id=1, source_target_pairs={{0,8},{4,36},{8,0},{12,44},{16,24},{20,52},{24,16},{28,60},{32,40}... | collective-permute-start | bytes 1572872 | tf_op jit(solution)/shard_map/ppermute | solution.py:49
  175.2 10.3 %collective-permute-start.25 = (f32[128,512]{1,0:T(8,128)S(1)}, f32[128,512]{1,0:T(8,128)S(1)}, u32[]{:S(2)}, u32[]{:S(2)}) collective-permute-start(f32[128,512]{1,0:T(8,128)S(1)} %get-tuple-element.68), channel_id=1, source_target_pairs={{0,32},{4,12},{8,40},{12,4},{16,48},{20,28},{24,56},{28,20},{32,0}... | collective-permute-start | bytes 786440 | tf_op jit(solution)/shard_map/ppermute | solution.py:49
  176.2 12.1 %collective-permute-start.28 = (f32[128,512]{1,0:T(8,128)S(1)}, f32[128,512]{1,0:T(8,128)S(1)}, u32[]{:S(2)}, u32[]{:S(2)}) collective-permute-start(f32[128,512]{1,0:T(8,128)S(1)} %get-tuple-element.65), channel_id=1, source_target_pairs={{0,64},{4,20},{8,72},{12,28},{16,80},{20,4},{24,88},{28,12},{32,96... | collective-permute-start | bytes 786440 | tf_op jit(solution)/shard_map/ppermute | solution.py:49
  176.7 11.5 %collective-permute-start.29 = (f32[128,512]{1,0:T(8,128)S(1)}, f32[128,512]{1,0:T(8,128)S(1)}, u32[]{:S(2)}, u32[]{:S(2)}) collective-permute-start(f32[128,512]{1,0:T(8,128)S(1)} %get-tuple-element.64), channel_id=1, source_target_pairs={{0,96},{4,28},{8,104},{12,20},{16,112},{20,12},{24,120},{28,4},{32... | collective-permute-start | bytes 786440 | tf_op jit(solution)/shard_map/ppermute | solution.py:49
  182.9 7.0 %collective-permute-start.32 = (f32[128,512]{1,0:T(8,128)S(1)}, f32[128,512]{1,0:T(8,128)S(1)}, u32[]{:S(2)}, u32[]{:S(2)}) collective-permute-start(f32[128,512]{1,0:T(8,128)S(1)} %get-tuple-element.69), channel_id=1, source_target_pairs={{0,32},{4,12},{8,40},{12,4},{16,48},{20,28},{24,56},{28,20},{32,0}... | collective-permute-start | bytes 786440 | tf_op jit(solution)/shard_map/ppermute | solution.py:49
  185.5 8.0 %collective-permute-start.35 = (f32[128,512]{1,0:T(8,128)S(1)}, f32[128,512]{1,0:T(8,128)S(1)}, u32[]{:S(2)}, u32[]{:S(2)}) collective-permute-start(f32[128,512]{1,0:T(8,128)S(1)} %get-tuple-element.67), channel_id=1, source_target_pairs={{0,64},{4,20},{8,72},{12,28},{16,80},{20,4},{24,88},{28,12},{32,96... | collective-permute-start | bytes 786440 | tf_op jit(solution)/shard_map/ppermute | solution.py:49
  185.5 10.4 %collective-permute-start.36 = (f32[128,512]{1,0:T(8,128)S(1)}, f32[128,512]{1,0:T(8,128)S(1)}, u32[]{:S(2)}, u32[]{:S(2)}) collective-permute-start(f32[128,512]{1,0:T(8,128)S(1)} %get-tuple-element.66), channel_id=1, source_target_pairs={{0,96},{4,28},{8,104},{12,20},{16,112},{20,12},{24,120},{28,4},{32... | collective-permute-start | bytes 786440 | tf_op jit(solution)/shard_map/ppermute | solution.py:49

commit v4 on v3

--- a/solution.py
+++ b/solution.py
@@ -10,7 +10,7 @@
 
 SIDE = 4
 LANE = 128
-VMEM = 56 * 2**20
+VMEM = 40 * 2**20
 
 
 def place(z, y, c):
@@ -92,7 +92,7 @@
     return jax.ShapeDtypeStruct(shape, jnp.float32)
 
 
-def call(kernel, grid, in_specs, out_specs, out_shape, scalars=0, scratch=(), flops=2**24, moved=2**23):
+def call(kernel, grid, in_specs, out_specs, out_shape, scalars=0, scratch=(), flops=2**24, moved=2**23, vmem=VMEM):
     return pl.pallas_call(
         kernel,
         grid_spec=pltpu.PrefetchScalarGridSpec(
@@ -103,7 +103,7 @@
             scratch_shapes=scratch,
         ),
         out_shape=out_shape,
-        compiler_params=pltpu.CompilerParams(vmem_limit_bytes=VMEM),
+        compiler_params=pltpu.CompilerParams(vmem_limit_bytes=vmem),
         cost_estimate=pl.CostEstimate(flops=flops, bytes_accessed=moved, transcendentals=0),
     )
 
@@ -159,18 +159,17 @@
         scratch=[pltpu.VMEM((SIDE, 2, rows, LANE), jnp.float32), pltpu.SemaphoreType.DMA((SIDE, 2))],
         flops=2**30,
         moved=2**23,
+        vmem=60 * 2**20,
     )(where, table, signs, design, design)
 
 
 def sample_kernel(scale, chunk, owned, where_ref, index_ref, *refs):
     sources, outs = refs[: 2 * SIDE], refs[2 * SIDE : 3 * SIDE]
     mixed_ref, picked_ref, sems = refs[3 * SIDE :]
-    step = pl.program_id(0)
-    block = sources[0].shape[0]
-    rows = block * pl.num_programs(0)
+    rows = sources[0].shape[0]
     size = 32
 
-    @pl.loop(0, block // size)
+    @pl.loop(0, rows // size)
     def _(number):
         here = pl.ds(pl.multiple_of(number * size, size), size)
         sums, differences = [], []
@@ -180,42 +179,38 @@
             differences.append(own - other)
         for core, parts in enumerate((sums, differences)):
             for outer, part in enumerate(butterfly(parts)):
-                at = (outer * 2 + core) * rows + step * block + number * size
+                at = (outer * 2 + core) * rows + number * size
                 mixed_ref[pl.ds(pl.multiple_of(at, size), size), :] = part
                 mixed_ref[pl.ds(pl.multiple_of(2 * SIDE * rows + at, size), size), :] = -part
 
-    @pl.when(step == pl.num_programs(0) - 1)
-    def _():
-        core, second = where_ref[0], where_ref[2]
-        group = 64
-        copies = []
-        for m in (2, 1, 3, 0):
-            for k in range(SIDE):
-                outer, inner = jnp.where(core == 0, second ^ m, k), jnp.where(core == 0, k, second ^ m)
-                start = (outer * 8 + inner * 2 + chunk) * owned
-
-                @pl.loop(0, owned // group)
-                def _(number):
-                    for lane in range(group):
-                        at = number * group + lane
-                        picked_ref[m, k, pl.ds(at, 1), :] = mixed_ref[pl.ds(index_ref[start + at], 1), :]
-
-            copies.append(pltpu.make_async_copy(picked_ref.at[m], outs[m], sems.at[m]))
-            copies[-1].start()
-        for copy in copies:
-            copy.wait()
+    core, second = where_ref[0], where_ref[2]
+    group = 64
+    copies = []
+    for m in (2, 1, 3, 0):
+        for k in range(SIDE):
+            outer, inner = jnp.where(core == 0, second ^ m, k), jnp.where(core == 0, k, second ^ m)
+            start = (outer * 8 + inner * 2 + chunk) * owned
+
+            @pl.loop(0, owned // group)
+            def _(number):
+                for lane in range(group):
+                    at = number * group + lane
+                    picked_ref[m, k, pl.ds(at, 1), :] = mixed_ref[pl.ds(index_ref[start + at], 1), :]
+
+        copies.append(pltpu.make_async_copy(picked_ref.at[m], outs[m], sems.at[m]))
+        copies[-1].start()
+    for copy in copies:
+        copy.wait()
 
 
 def sampled_rows(where, index, sources, scale, chunk, owned):
     rows = sources[0].shape[0]
-    steps = 2
     return call(
         functools.partial(sample_kernel, scale, chunk, owned),
-        (steps,),
-        [pl.BlockSpec((rows // steps, LANE), lambda s, w, i: (s, 0))] * (2 * SIDE),
+        (),
+        [pl.BlockSpec(memory_space=pltpu.SMEM)] * 2 + [pl.BlockSpec(memory_space=pltpu.VMEM)] * (2 * SIDE),
         [pl.BlockSpec(memory_space=pl.ANY)] * SIDE,
         [f32(SIDE, owned, LANE)] * SIDE,
-        scalars=2,
         scratch=[
             pltpu.VMEM((4 * SIDE * rows, LANE), jnp.float32),
             pltpu.VMEM((SIDE, SIDE, owned, LANE), jnp.float32),
@@ -246,63 +241,57 @@
     )(where, *operands)
 
 
-def gram_kernel(plan, where_ref, *refs):
-    inputs, outs = refs[:12], refs[12 : 12 + 2 * len(plan)]
-    right_in, left_in, *held, right_sems, left_sems, out_sems = refs[12 + 2 * len(plan) :]
+def gram_kernel(plan, halves, where_ref, *refs):
+    count = len(plan) * len(halves)
+    inputs, outs = refs[:12], refs[12 : 12 + count]
+    right_in, left_in, *held, out_sems = refs[12 + count :]
     core, first, second, me = (where_ref[i] for i in range(4))
     owned = right_in.shape[0] // 2
     blocks = [(number, block) for number, entries in enumerate(plan) for block in entries]
 
-    def right_copy(chunk, j, side):
-        source = inputs[6 * chunk + side].at[j]
-        block = 2 * j + jnp.where(side == 0, core, 1 - core)
-        rows, lanes = pl.ds(chunk * owned, owned), pl.ds(pl.multiple_of(block * LANE, LANE), LANE)
-        return pltpu.make_async_copy(source, right_in.at[rows, lanes], right_sems.at[chunk, j, side])
-
-    rights = [right_copy(chunk, j, side) for chunk in range(2) for j in range(SIDE) for side in range(2)]
-    for copy in rights:
-        copy.start()
-    lefts = []
-    for slot, (_, (k, m)) in enumerate(blocks):
+    used = [j for half in halves for j in range(CUTS[half] // 256, CUTS[half + 1] // 256)]
+    for chunk in range(2):
+        mine, sibling = inputs[6 * chunk], inputs[6 * chunk + 1]
+        rows = pl.ds(chunk * owned, owned)
+        for j in used:
+            zero = 2 * j * LANE - CUTS[halves[0]]
+            for side, source in enumerate((mine, sibling)):
+                lanes = pl.multiple_of(zero + LANE * jnp.where(side == 0, core, 1 - core), LANE)
+                right_in[rows, pl.ds(lanes, LANE)] = source[j]
+
+    def gather(slot, k, m):
         column = jnp.where(core == 0, second ^ m, first ^ k)
         j = jnp.where(core == 0, first ^ k, second ^ m)
         distance = lax.rem(me + SIDE - column, SIDE)
-        for chunk in range(2):
-            mine, _, right, left, far_a, far_b = inputs[6 * chunk : 6 * chunk + 6]
-            target = left_in.at[slot, pl.ds(chunk * owned, owned), :]
-            sem = left_sems.at[slot, chunk]
-            cases = [(distance == 0, mine, j), (distance == 1, right, j), (distance == 3, left, j)]
-            cases.append(((distance == 2) & (j < 2), far_a, jnp.minimum(j, 1)))
-            cases.append(((distance == 2) & (j >= 2), far_b, jnp.maximum(j, 2) - 2))
-            for chosen, ref, at in cases:
-
-                @pl.when(chosen)
-                def _():
-                    pltpu.make_async_copy(ref.at[at], target, sem).start()
-
-            lefts.append(pltpu.make_async_copy(mine.at[0], target, sem))
+        cases = [(distance == 0, 0, j), (distance == 1, 2, j), (distance == 3, 3, j)]
+        cases.append(((distance == 2) & (j < 2), 4, jnp.minimum(j, 1)))
+        cases.append(((distance == 2) & (j >= 2), 5, jnp.maximum(j, 2) - 2))
+        for chosen, which, at in cases:
+
+            @pl.when(chosen)
+            def _():
+                for chunk in range(2):
+                    left_in[slot, pl.ds(chunk * owned, owned), :] = inputs[6 * chunk + which][at]
 
     def product(a, b):
         return lax.dot_general(a, b, (((0,), (0,)), ((), ())), preferred_element_type=jnp.float32)
 
-    for copy in rights:
-        copy.wait()
     right_high, right_low = split(right_in[...])
     group = 4
     copies = []
     done = [0] * len(plan)
     for base in range(0, len(blocks), group):
-        for copy in lefts[2 * base : 2 * (base + group)]:
-            copy.wait()
+        for i in range(group):
+            gather(base + i, *blocks[base + i][1])
         high, low = split(jnp.concatenate([left_in[base + i] for i in range(group)], axis=1))
-        for half in range(2):
-            here = slice(CUTS[half], CUTS[half + 1])
+        for offset, half in enumerate(halves):
+            here = slice(CUTS[half] - CUTS[halves[0]], CUTS[half + 1] - CUTS[halves[0]])
             value = product(high, right_high[:, here]) + product(low, right_high[:, here])
             value += product(high, right_low[:, here])
             at = list(done)
             for i in range(group):
                 number = blocks[base + i][0]
-                slot = 2 * number + half
+                slot = len(halves) * number + offset
                 held[slot][at[number]] = value[i * LANE : (i + 1) * LANE]
                 at[number] += 1
                 if at[number] == len(plan[number]):
@@ -313,22 +302,20 @@
         copy.wait()
 
 
-def gram_shares(where, operands, plan):
+def gram_shares(where, operands, plan, halves):
     owned = operands[0].shape[1]
-    shapes = [(len(entries), LANE, CUTS[half + 1] - CUTS[half]) for entries in plan for half in range(2)]
+    shapes = [(len(entries), LANE, CUTS[half + 1] - CUTS[half]) for entries in plan for half in halves]
     slots = sum(len(entries) for entries in plan)
     return call(
-        functools.partial(gram_kernel, plan),
+        functools.partial(gram_kernel, plan, halves),
         (),
-        [pl.BlockSpec(memory_space=pltpu.SMEM)] + [pl.BlockSpec(memory_space=pl.ANY)] * len(operands),
+        [pl.BlockSpec(memory_space=pltpu.SMEM)] + [pl.BlockSpec(memory_space=pltpu.VMEM)] * len(operands),
         [pl.BlockSpec(memory_space=pl.ANY)] * len(shapes),
         [f32(*shape) for shape in shapes],
         scratch=[
-            pltpu.VMEM((2 * owned, CUTS[-1]), jnp.float32),
+            pltpu.VMEM((2 * owned, sum(CUTS[half + 1] - CUTS[half] for half in halves)), jnp.float32),
             pltpu.VMEM((slots, 2 * owned, LANE), jnp.float32),
             *[pltpu.VMEM(shape, jnp.float32) for shape in shapes],
-            pltpu.SemaphoreType.DMA((2, SIDE, 2)),
-            pltpu.SemaphoreType.DMA((slots, 2)),
             pltpu.SemaphoreType.DMA((len(shapes),)),
         ],
         flops=3 * 2**30,
@@ -365,7 +352,7 @@
     own, theirs = pieces[:SIDE], list(pieces[SIDE:])
     sample_rows, _ = lax.optimization_barrier((sample_rows, own[0]))
     index = sample_index(sample_rows, z, y, core)
-    index, theirs[0], theirs[3] = lax.optimization_barrier((index, theirs[0], theirs[3]))
+    index, theirs[0] = lax.optimization_barrier((index, theirs[0]))
     sources = [own[0]] + [hop(own[step], FIRST, step) for step in (1, 2, 3)]
     sources += [across(theirs[step], step) for step in range(SIDE)]
 
@@ -379,7 +366,8 @@
             mine, *_ = lax.optimization_barrier((mine, gathered[0][2], gathered[0][3]))
         right, left = around(mine, 1), around(mine, 3)
         far_a, far_b = around(right[: SIDE // 2], 1), around(left[SIDE // 2 :], 3)
-        gathered.append((mine, to_sibling(mine), right, left, far_a, far_b))
+        swapped, *_ = lax.optimization_barrier((mine, right, left))
+        gathered.append((mine, to_sibling(swapped), right, left, far_a, far_b))
 
     sketch = sketch_rows(where, gathered[0][0], gathered[1][0], gathered[0][1], gathered[1][1])
 
@@ -389,11 +377,12 @@
     def blocks(*entries):
         return [(first, second) for first, seconds in entries for second in seconds]
 
-    early = gram_shares(where, operands, [blocks((2, low), (1, low)), blocks((2, high), (3, high))])
-    late = gram_shares(where, operands, [blocks((1, high)), blocks((3, low)), blocks((0, low), (0, high))])
+    early_plan = [blocks((2, low), (1, low)), blocks((2, high), (3, high))]
+    early = [gram_shares(where, operands, early_plan, (half,)) for half in range(2)]
+    late = gram_shares(where, operands, [blocks((1, high)), blocks((3, low)), blocks((0, low), (0, high))], (0, 1))
     parts = []
     for half in range(2):
-        to_one, to_three = early[half::2]
+        to_one, to_three = early[half]
         rest_one, rest_three, here = late[half::2]
         from_one, from_three = hop(to_one, FIRST, 1), hop(to_three, FIRST, 3)
         last_one = hop(rest_one + from_three[:2], FIRST, 1)

time: 199 us -> 190 us (0.955); the launches traced: 197 us -> 190 us
  waiting for transfers between devices: 52.3 us -> 73.8 us
  Pallas kernels: 45.3 us -> 34.8 us
  other arithmetic: 12.2 us -> 2.83 us
  starting transfers between devices: 61.3 us -> 54.1 us
    ppermute x23, waiting for transfers between devices: 20.4 us -> 32.9 us  [hop(): return lax.ppermute(value, 'row', partners(ring, step))]
    pallas_call x4 -> x5, Pallas kernels: 35.5 us -> 26.6 us  [the longest x2 13.8 us: sampled_rows(): call(functools.partial(sample_kernel, scale, chunk, owned), (), [pl.Block...]
    ppermute x8, waiting for transfers between devices: 16.8 us -> 25.1 us  [around(): lax.ppermute(value, 'col', [(i, (i + step) % SIDE) for i in range(SIDE)])]
    ppermute x23, starting transfers between devices: 39 us -> 32.2 us  [hop(): return lax.ppermute(value, 'row', partners(ring, step))]
    add x2, other arithmetic: 3.08 us -> 0.16 us  [shards(): last_three = hop(rest_three + from_one[:2], FIRST, 3)]
    add x2, other arithmetic: 2.81 us -> 0.16 us  [shards(): last_one = hop(rest_one + from_three[:2], FIRST, 1)]
    add x2, other arithmetic: 2.56 us -> 0.49 us  [shards(): here[3] + from_three[3] + last_one[1]]
  transfers between devices with their start and end apart: 38 -> 38, of which waited for: 18 -> 21; matrix products, arithmetic and copies ran while one was open for 6% -> 1% of each run, Pallas kernels for 11% -> 9%
where the time goes in v4:
time: 190 us
  waiting for transfers between devices  73.8 us (39%)
  starting transfers between devices  54.1 us (28%)
  Pallas kernels  34.8 us (18%)
  blocking collectives  21.8 us (11%)
  other arithmetic  2.83 us (1%)
    ppermute x23, waiting for transfers between devices, hop(): return lax.ppermute(value, 'row', partners(ring, step))  32.9 us
    ppermute x23, starting transfers between devices, hop(): return lax.ppermute(value, 'row', partners(ring, step))  32.2 us
    ppermute x8, waiting for transfers between devices, around(): lax.ppermute(value, 'col', [(i, (i + step) % SIDE) for i in range(SIDE)])  25.1 us
    all_to_all x2, blocking collectives, exchange(): lax.all_to_all(value, 'row', 0, 0, tiled=True, axis_index_groups=groups(r...  21.8 us
    pallas_call x2, Pallas kernels, sampled_rows(): call(functools.partial(sample_kernel, scale, chunk, owned), (), [pl.Block...  13.8 us
    pallas_call x3, Pallas kernels, gram_shares(): call(functools.partial(gram_kernel, plan, halves), (), [pl.BlockSpec(memo...  12.8 us
    ppermute x4, waiting for transfers between devices, across(): lax.ppermute(value, 'row', [(i ^ 1, j) for i, j in partners(FIRST, step)])  11.6 us
    ppermute x8, starting transfers between devices, around(): lax.ppermute(value, 'col', [(i, (i + step) % SIDE) for i in range(SIDE)])  9.31 us
  transfers between devices with their start and end apart: 38, of which 21 were waited for; matrix products, arithmetic and copies ran while one was open for 1% of the time, Pallas kernels for 9%

profile of v4, /device:TPU:14, one launch (start us, length us, event | category | flops | bytes accessed | tf_op | source)
XLA Modules:
  0.0 190.0 jit_solution(14828543776496449495)
XLA Ops:
  0.7 0.6 pad_add_fusion._.where_ref
  1.3 6.6 %shard_map.59 = (f32[1024,128]{1,0:T(8,128)}, f32[1024,128]{1,0:T(8,128)}, f32[1024,128]{1,0:T(8,128)}, f32[1024,128]{1,0:T(8,128)}, f32[1024,128]{1,0:T(8,128)}...) custom-call(s32[4]{0:T(128)} %pad_add_fusion._.where_ref, ...), custom_call_target="tpu_custom_call" | custom-call | flops 1073741824 | bytes 8388608 | tf_op jit(solution)/shard_map/pallas_call | solution.py:147
  7.9 0.5 collective-permute-start
  8.4 2.6 %collective-permute-start.1 = (f32[1024,128]{1,0:T(8,128)}, f32[1024,128]{1,0:T(8,128)S(1)}, u32[]{:S(2)}, u32[]{:S(2)}) collective-permute-start(f32[1024,128]{1,0:T(8,128)} %get-tuple-element.39), channel_id=1, source_target_pairs={{0,16},{4,68},{8,24},{12,76},{16,0},{20,84},{24,8},{28,92},{32,48}... | collective-permute-start | bytes 1572872 | tf_op jit(solution)/shard_map/ppermute | solution.py:49
  11.0 0.6 broadcast_in_dim.7
  11.6 7.4 %all-to-all-start = ((s32[32,1,256]{2,1,0:T(1,128)}), s32[32,1,256]{2,1,0:T(1,128)S(1)}, u32[]{:S(2)}, u32[]{:S(2)}) async-start(s32[32,1,256]{2,1,0:T(1,128)} %broadcast_in_dim.7), calls=%async_computation | async-start | bytes 65536 | tf_op jit(solution)/shard_map/all_to_all | solution.py:329
  19.0 1.5 collective-permute-start.2
  20.6 0.9 collective-permute-start.4
  21.5 3.5 %collective-permute-start.5 = (f32[1024,128]{1,0:T(8,128)}, f32[1024,128]{1,0:T(8,128)S(1)}, u32[]{:S(2)}, u32[]{:S(2)}) collective-permute-start(f32[1024,128]{1,0:T(8,128)} %get-tuple-element.43), channel_id=1, source_target_pairs={{4,16},{0,68},{12,24},{8,76},{20,0},{16,84},{28,8},{24,92},{36,48}... | collective-permute-start | bytes 1572872 | tf_op jit(solution)/shard_map/ppermute | solution.py:57
  25.1 4.2 %all-to-all-done = s32[32,1,256]{2,1,0:T(1,128)S(1)} async-done(((s32[32,1,256]{2,1,0:T(1,128)}), s32[32,1,256]{2,1,0:T(1,128)S(1)}, u32[]{:S(2)}, u32[]{:S(2)}) %all-to-all-start) | async-done | bytes 32800 | tf_op jit(solution)/shard_map/all_to_all | solution.py:329
  29.4 0.2 collective-permute-start.6
  29.7 0.4 collective-permute-start.3
  30.1 6.1 %collective-permute-done.5.refs_6_ = f32[1024,128]{1,0:T(8,128)S(1)} collective-permute-done((f32[1024,128]{1,0:T(8,128)}, f32[1024,128]{1,0:T(8,128)S(1)}, u32[]{:S(2)}, u32[]{:S(2)}) %collective-permute-start.5) | collective-permute-done | bytes 524320 | tf_op jit(solution)/shard_map/ppermute | solution.py:57
  36.2 5.5 %collective-permute-done.6.refs_7_ = f32[1024,128]{1,0:T(8,128)S(1)} collective-permute-done((f32[1024,128]{1,0:T(8,128)}, f32[1024,128]{1,0:T(8,128)S(1)}, u32[]{:S(2)}, u32[]{:S(2)}) %collective-permute-start.6) | collective-permute-done | bytes 524320 | tf_op jit(solution)/shard_map/ppermute | solution.py:57
  41.7 1.0 copy-done
  42.8 6.9 %shard_map.60 = (f32[4,256,128]{2,1,0:T(8,128)S(1)}, f32[4,256,128]{2,1,0:T(8,128)S(1)}, f32[4,256,128]{2,1,0:T(8,128)S(1)}, f32[4,256,128]{2,1,0:T(8,128)S(1)}) custom-call(s32[4]{0:T(128)S(1)} %copy-done.1, s32[8192]{0:T(1024)S(1)} %fusion.13.index_ref, f32[1024,128]{1,0:T(8,128)S(1)} %copy-done, f32[1024,128]{1,0:T(8,128)S(1)} %collective-permute-done.refs_1_, ...), custom_call_target="tpu_custom_call" | custom-call | flops 16777216 | bytes 8388608 | tf_op jit(solution)/shard_map/pallas_call | solution.py:208
  49.7 1.4 collective-permute-start.7
  51.2 3.6 %collective-permute-start.8 = (f32[4,256,128]{2,1,0:T(8,128)S(1)}, f32[4,256,128]{2,1,0:T(8,128)S(1)}, u32[]{:S(2)}, u32[]{:S(2)}) collective-permute-start(f32[4,256,128]{2,1,0:T(8,128)S(1)} %get-tuple-element.47), channel_id=1, source_target_pairs={{0,64},{4,20},{8,72},{12,28},{16,80},{20,4},{24,88},{28,12},{32,96... | collective-permute-start | bytes 1572872 | tf_op jit(solution)/shard_map/ppermute | solution.py:49
  54.7 6.9 %shard_map.61 = (f32[4,256,128]{2,1,0:T(8,128)S(1)}, f32[4,256,128]{2,1,0:T(8,128)S(1)}, f32[4,256,128]{2,1,0:T(8,128)S(1)}, f32[4,256,128]{2,1,0:T(8,128)S(1)}) custom-call(s32[4]{0:T(128)S(1)} %copy-done.1, s32[8192]{0:T(1024)S(1)} %fusion.13.index_ref, f32[1024,128]{1,0:T(8,128)S(1)} %copy-done, f32[1024,128]{1,0:T(8,128)S(1)} %collective-permute-done.refs_1_, ...), custom_call_target="tpu_custom_call" | custom-call | flops 16777216 | bytes 8388608 | tf_op jit(solution)/shard_map/pallas_call | solution.py:208
  61.8 4.7 %collective-permute-start.11 = (f32[4,256,128]{2,1,0:T(8,128)S(1)}, f32[4,256,128]{2,1,0:T(8,128)S(1)}, u32[]{:S(2)}, u32[]{:S(2)}) collective-permute-start(f32[4,256,128]{2,1,0:T(8,128)S(1)} %get-tuple-element.51), channel_id=1, source_target_pairs={{0,64},{4,20},{8,72},{12,28},{16,80},{20,4},{24,88},{28,12},{32,96... | collective-permute-start | bytes 1572872 | tf_op jit(solution)/shard_map/ppermute | solution.py:49
  66.5 1.2 collective-permute-done.8
  67.6 3.1 %collective-permute-done.9 = f32[4,256,128]{2,1,0:T(8,128)S(1)} collective-permute-done((f32[4,256,128]{2,1,0:T(8,128)S(1)}, f32[4,256,128]{2,1,0:T(8,128)S(1)}, u32[]{:S(2)}, u32[]{:S(2)}) %collective-permute-start.9) | collective-permute-done | bytes 524320 | tf_op jit(solution)/shard_map/ppermute | solution.py:49
  70.8 10.9 %all_to_all.16.mine_zero.refs_0_ = f32[4,256,128]{2,1,0:T(8,128)S(1)} all-to-all(f32[4,256,128]{2,1,0:T(8,128)S(1)} %add_add_fusion.1), channel_id=1, replica_groups={{0,8,16,24},{4,36,68,100},{32,40,48,56},{12,44,76,108},{64,72,80,88},{2..., dimensions={0} | all-to-all | bytes 1048576 | tf_op jit(solution)/shard_map/all_to_all | solution.py:45
  81.7 0.5 collective-permute-start.13
  82.2 1.5 collective-permute-start.14
  83.8 1.5 collective-permute-done.12
  85.4 10.9 %all_to_all.17.mine_one.refs_6_ = f32[4,256,128]{2,1,0:T(8,128)S(1)} all-to-all(f32[4,256,128]{2,1,0:T(8,128)S(1)} %add_add_fusion), channel_id=1, replica_groups={{0,8,16,24},{4,36,68,100},{32,40,48,56},{12,44,76,108},{64,72,80,88},{2..., dimensions={0} | all-to-all | bytes 1048576 | tf_op jit(solution)/shard_map/all_to_all | solution.py:45
  96.3 1.3 collective-permute-done.14.refs_3_
  97.6 0.3 collective-permute-start.16
  97.9 1.8 collective-permute-start.17
  99.6 1.6 collective-permute-start.19
  101.2 11.1 %collective-permute-done.16.refs_8_ = f32[4,256,128]{2,1,0:T(8,128)S(1)} collective-permute-done((f32[4,256,128]{2,1,0:T(8,128)S(1)}, f32[4,256,128]{2,1,0:T(8,128)S(1)}, u32[]{:S(2)}, u32[]{:S(2)}) %collective-permute-start.16) | collective-permute-done | bytes 524320 | tf_op jit(solution)/shard_map/ppermute | solution.py:61
  112.3 0.8 collective-permute-done.17.refs_9_
  113.1 0.6 collective-permute-start.20
  113.8 2.8 %collective-permute-start.21 = (f32[2,256,128]{2,1,0:T(8,128)S(1)}, f32[2,256,128]{2,1,0:T(8,128)S(1)}, u32[]{:S(2)}, u32[]{:S(2)}) collective-permute-start(f32[2,256,128]{2,1,0:T(8,128)S(1)} %slice.130), channel_id=1, source_target_pairs={{0,1},{1,2},{2,3},{3,0},{4,5},{5,6},{6,7},{7,4},{8,9},{9,10},{10,1... | collective-permute-start | bytes 786440 | tf_op jit(solution)/shard_map/ppermute | solution.py:61
  116.6 1.4 collective-permute-done.19.refs_4_
  117.9 0.3 collective-permute-start.22
  118.2 5.3 %collective-permute-done.20.refs_5_ = f32[2,256,128]{2,1,0:T(8,128)S(1)} collective-permute-done((f32[2,256,128]{2,1,0:T(8,128)S(1)}, f32[2,256,128]{2,1,0:T(8,128)S(1)}, u32[]{:S(2)}, u32[]{:S(2)}) %collective-permute-start.20) | collective-permute-done | bytes 262176 | tf_op jit(solution)/shard_map/ppermute | solution.py:61
  123.5 5.2 %collective-permute-done.22.refs_11_ = f32[2,256,128]{2,1,0:T(8,128)S(1)} collective-permute-done((f32[2,256,128]{2,1,0:T(8,128)S(1)}, f32[2,256,128]{2,1,0:T(8,128)S(1)}, u32[]{:S(2)}, u32[]{:S(2)}) %collective-permute-start.22) | collective-permute-done | bytes 262176 | tf_op jit(solution)/shard_map/ppermute | solution.py:61
  128.8 3.4 %shard_map.64 = (f32[4,128,512]{2,1,0:T(8,128)S(1)}, f32[4,128,512]{2,1,0:T(8,128)S(1)}) custom-call(s32[4]{0:T(128)S(1)} %copy-done.1, f32[4,256,128]{2,1,0:T(8,128)S(1)} %all_to_all.16.mine_zero.refs_0_, f32[4,256,128]{2,1,0:T(8,128)S(1)} %collective-permute-done.15.sibling_zero.refs_1_, f32[4,256,128]{2,1,0:T(8,128)S(1)} %collective-permute-done.13.refs_2_, ...), custom_call_target="tpu_custom_call" | custom-call | flops 3221225472 | bytes 8388608 | tf_op jit(solution)/shard_map/pallas_call | solution.py:309
  132.2 2.2 %collective-permute-start.23 = (f32[4,128,512]{2,1,0:T(8,128)S(1)}, f32[4,128,512]{2,1,0:T(8,128)S(1)}, u32[]{:S(2)}, u32[]{:S(2)}) collective-permute-start(f32[4,128,512]{2,1,0:T(8,128)S(1)} %get-tuple-element.57), channel_id=1, source_target_pairs={{0,8},{4,36},{8,0},{12,44},{16,24},{20,52},{24,16},{28,60},{32,40}... | collective-permute-start | bytes 3145736 | tf_op jit(solution)/shard_map/ppermute | solution.py:49
  134.3 3.4 %shard_map.65 = (f32[4,128,512]{2,1,0:T(8,128)S(1)}, f32[4,128,512]{2,1,0:T(8,128)S(1)}) custom-call(s32[4]{0:T(128)S(1)} %copy-done.1, f32[4,256,128]{2,1,0:T(8,128)S(1)} %all_to_all.16.mine_zero.refs_0_, f32[4,256,128]{2,1,0:T(8,128)S(1)} %collective-permute-done.15.sibling_zero.refs_1_, f32[4,256,128]{2,1,0:T(8,128)S(1)} %collective-permute-done.13.refs_2_, ...), custom_call_target="tpu_custom_call" | custom-call | flops 3221225472 | bytes 8388608 | tf_op jit(solution)/shard_map/pallas_call | solution.py:309
  137.7 0.8 collective-permute-start.30
  138.6 2.0 %collective-permute-start.33 = (f32[4,128,512]{2,1,0:T(8,128)S(1)}, f32[4,128,512]{2,1,0:T(8,128)S(1)}, u32[]{:S(2)}, u32[]{:S(2)}) collective-permute-start(f32[4,128,512]{2,1,0:T(8,128)S(1)} %get-tuple-element.64), channel_id=1, source_target_pairs={{0,24},{4,100},{8,16},{12,108},{16,8},{20,116},{24,0},{28,124},{32... | collective-permute-start | bytes 3145736 | tf_op jit(solution)/shard_map/ppermute | solution.py:49
  140.5 6.0 %shard_map.63 = (f32[2,128,512]{2,1,0:T(8,128)S(1)}, f32[2,128,512]{2,1,0:T(8,128)S(1)}, f32[2,128,512]{2,1,0:T(8,128)S(1)}, f32[2,128,512]{2,1,0:T(8,128)S(1)},...) custom-call(s32[4]{0:T(128)S(1)} %copy-done.1, f32[4,256,128]{2,1,0:T(8,128)S(1)} %all_to_all.16.mine_zero.refs_0_, ...), custom_call_target="tpu_custom_call" | custom-call | flops 3221225472 | bytes 8388608 | tf_op jit(solution)/shard_map/pallas_call | solution.py:309
  146.5 0.6 collective-permute-done.23
  147.4 1.7 collective-permute-done.26
  149.2 1.4 collective-permute-start.27
  150.6 7.7 %collective-permute-done.30 = f32[4,128,512]{2,1,0:T(8,128)S(1)} collective-permute-done((f32[4,128,512]{2,1,0:T(8,128)S(1)}, f32[4,128,512]{2,1,0:T(8,128)S(1)}, u32[]{:S(2)}, u32[]{:S(2)}) %collective-permute-start.30) | collective-permute-done | bytes 1048608 | tf_op jit(solution)/shard_map/ppermute | solution.py:49
  158.7 1.7 collective-permute-done.33
  160.4 1.4 collective-permute-start.34
  161.8 1.6 shard_map.62
  163.5 2.5 %collective-permute-done.24 = f32[2,128,512]{2,1,0:T(8,128)S(1)} collective-permute-done((f32[2,128,512]{2,1,0:T(8,128)S(1)}, f32[2,128,512]{2,1,0:T(8,128)S(1)}, u32[]{:S(2)}, u32[]{:S(2)}) %collective-permute-start.24) | collective-permute-done | bytes 524320 | tf_op jit(solution)/shard_map/ppermute | solution.py:49
  166.0 0.2 fusion.6
  166.3 2.0 %collective-permute-start.28 = (f32[128,512]{1,0:T(8,128)S(1)}, f32[128,512]{1,0:T(8,128)S(1)}, u32[]{:S(2)}, u32[]{:S(2)}) collective-permute-start(f32[128,512]{1,0:T(8,128)S(1)} %get-tuple-element.67), channel_id=1, source_target_pairs={{0,64},{4,20},{8,72},{12,28},{16,80},{20,4},{24,88},{28,12},{32,96... | collective-permute-start | bytes 786440 | tf_op jit(solution)/shard_map/ppermute | solution.py:49
  168.3 2.7 %collective-permute-start.29 = (f32[128,512]{1,0:T(8,128)S(1)}, f32[128,512]{1,0:T(8,128)S(1)}, u32[]{:S(2)}, u32[]{:S(2)}) collective-permute-start(f32[128,512]{1,0:T(8,128)S(1)} %get-tuple-element.66), channel_id=1, source_target_pairs={{0,96},{4,28},{8,104},{12,20},{16,112},{20,12},{24,120},{28,4},{32... | collective-permute-start | bytes 786440 | tf_op jit(solution)/shard_map/ppermute | solution.py:49
  171.0 6.1 %collective-permute-done.31 = f32[2,128,512]{2,1,0:T(8,128)S(1)} collective-permute-done((f32[2,128,512]{2,1,0:T(8,128)S(1)}, f32[2,128,512]{2,1,0:T(8,128)S(1)}, u32[]{:S(2)}, u32[]{:S(2)}) %collective-permute-start.31) | collective-permute-done | bytes 524320 | tf_op jit(solution)/shard_map/ppermute | solution.py:49
  177.1 0.2 fusion
  177.5 1.6 collective-permute-start.35
  179.0 3.1 %collective-permute-start.36 = (f32[128,512]{1,0:T(8,128)S(1)}, f32[128,512]{1,0:T(8,128)S(1)}, u32[]{:S(2)}, u32[]{:S(2)}) collective-permute-start(f32[128,512]{1,0:T(8,128)S(1)} %get-tuple-element.68), channel_id=1, source_target_pairs={{0,96},{4,28},{8,104},{12,20},{16,112},{20,12},{24,120},{28,4},{32... | collective-permute-start | bytes 786440 | tf_op jit(solution)/shard_map/ppermute | solution.py:49
  182.3 1.5 collective-permute-done.32
  183.8 2.5 %collective-permute-done.35 = f32[128,512]{1,0:T(8,128)S(1)} collective-permute-done((f32[128,512]{1,0:T(8,128)S(1)}, f32[128,512]{1,0:T(8,128)S(1)}, u32[]{:S(2)}, u32[]{:S(2)}) %collective-permute-start.35) | collective-permute-done | bytes 262176 | tf_op jit(solution)/shard_map/ppermute | solution.py:49
  186.3 2.7 %collective-permute-done.36 = f32[128,512]{1,0:T(8,128)S(1)} collective-permute-done((f32[128,512]{1,0:T(8,128)S(1)}, f32[128,512]{1,0:T(8,128)S(1)}, u32[]{:S(2)}, u32[]{:S(2)}) %collective-permute-start.36) | collective-permute-done | bytes 262176 | tf_op jit(solution)/shard_map/ppermute | solution.py:49
  189.2 0.8 pad_maximum_fusion
  (45 shorter events, 1.8 us)
Async XLA Ops:
  1.3 9.7 %copy-start.2 = (s32[256]{0:T(256)S(1)}, s32[256]{0:T(256)}, u32[]{:S(2)}) copy-start(s32[256]{0:T(256)} %param.6) | copy-start | bytes 3076
  1.3 40.5 %copy-start.1 = (s32[4]{0:T(128)S(1)}, s32[4]{0:T(128)}, u32[]{:S(2)}) copy-start(s32[4]{0:T(128)} %pad_add_fusion._.where_ref) | copy-start | bytes 52
  7.9 21.6 %collective-permute-start = (f32[1024,128]{1,0:T(8,128)}, f32[1024,128]{1,0:T(8,128)S(1)}, u32[]{:S(2)}, u32[]{:S(2)}) collective-permute-start(f32[1024,128]{1,0:T(8,128)} %get-tuple-element.38), channel_id=1, source_target_pairs={{0,8},{4,36},{8,0},{12,44},{16,24},{20,52},{24,16},{28,60},{32,40}... | collective-permute-start | bytes 1572872 | tf_op jit(solution)/shard_map/ppermute | solution.py:49
  8.4 21.3 %collective-permute-start.1 = (f32[1024,128]{1,0:T(8,128)}, f32[1024,128]{1,0:T(8,128)S(1)}, u32[]{:S(2)}, u32[]{:S(2)}) collective-permute-start(f32[1024,128]{1,0:T(8,128)} %get-tuple-element.39), channel_id=1, source_target_pairs={{0,16},{4,68},{8,24},{12,76},{16,0},{20,84},{24,8},{28,92},{32,48}... | collective-permute-start | bytes 1572872 | tf_op jit(solution)/shard_map/ppermute | solution.py:49
  11.6 17.7 %all-to-all-start = ((s32[32,1,256]{2,1,0:T(1,128)}), s32[32,1,256]{2,1,0:T(1,128)S(1)}, u32[]{:S(2)}, u32[]{:S(2)}) async-start(s32[32,1,256]{2,1,0:T(1,128)} %broadcast_in_dim.7), calls=%async_computation | async-start | bytes 65536 | tf_op jit(solution)/shard_map/all_to_all | solution.py:329
  19.0 11.1 %collective-permute-start.2 = (f32[1024,128]{1,0:T(8,128)}, f32[1024,128]{1,0:T(8,128)S(1)}, u32[]{:S(2)}, u32[]{:S(2)}) collective-permute-start(f32[1024,128]{1,0:T(8,128)} %get-tuple-element.40), channel_id=1, source_target_pairs={{0,24},{4,100},{8,16},{12,108},{16,8},{20,116},{24,0},{28,124},{32... | collective-permute-start | bytes 1572872 | tf_op jit(solution)/shard_map/ppermute | solution.py:49
  20.6 9.5 %collective-permute-start.4 = (f32[1024,128]{1,0:T(8,128)}, f32[1024,128]{1,0:T(8,128)S(1)}, u32[]{:S(2)}, u32[]{:S(2)}) collective-permute-start(f32[1024,128]{1,0:T(8,128)} %get-tuple-element.42), channel_id=1, source_target_pairs={{4,8},{0,36},{12,0},{8,44},{20,24},{16,52},{28,16},{24,60},{36,40}... | collective-permute-start | bytes 1572872 | tf_op jit(solution)/shard_map/ppermute | solution.py:57
  21.5 14.7 %collective-permute-start.5 = (f32[1024,128]{1,0:T(8,128)}, f32[1024,128]{1,0:T(8,128)S(1)}, u32[]{:S(2)}, u32[]{:S(2)}) collective-permute-start(f32[1024,128]{1,0:T(8,128)} %get-tuple-element.43), channel_id=1, source_target_pairs={{4,16},{0,68},{12,24},{8,76},{20,0},{16,84},{28,8},{24,92},{36,48}... | collective-permute-start | bytes 1572872 | tf_op jit(solution)/shard_map/ppermute | solution.py:57
  29.4 12.3 %collective-permute-start.6 = (f32[1024,128]{1,0:T(8,128)}, f32[1024,128]{1,0:T(8,128)S(1)}, u32[]{:S(2)}, u32[]{:S(2)}) collective-permute-start(f32[1024,128]{1,0:T(8,128)} %get-tuple-element.44), channel_id=1, source_target_pairs={{4,24},{0,100},{12,16},{8,108},{20,8},{16,116},{28,0},{24,124},{36... | collective-permute-start | bytes 1572872 | tf_op jit(solution)/shard_map/ppermute | solution.py:57
  29.7 12.0 %collective-permute-start.3 = (f32[1024,128]{1,0:T(8,128)}, f32[1024,128]{1,0:T(8,128)S(1)}, u32[]{:S(2)}, u32[]{:S(2)}) collective-permute-start(f32[1024,128]{1,0:T(8,128)} %get-tuple-element.41), channel_id=1, source_target_pairs={{4,0},{0,4},{12,8},{8,12},{20,16},{16,20},{28,24},{24,28},{36,32},... | collective-permute-start | bytes 1572872 | tf_op jit(solution)/shard_map/ppermute | solution.py:57
  41.7 1.0 copy-start
  49.7 16.7 %collective-permute-start.7 = (f32[4,256,128]{2,1,0:T(8,128)S(1)}, f32[4,256,128]{2,1,0:T(8,128)S(1)}, u32[]{:S(2)}, u32[]{:S(2)}) collective-permute-start(f32[4,256,128]{2,1,0:T(8,128)S(1)} %get-tuple-element.46), channel_id=1, source_target_pairs={{0,32},{4,12},{8,40},{12,4},{16,48},{20,28},{24,56},{28,20},{32,0}... | collective-permute-start | bytes 1572872 | tf_op jit(solution)/shard_map/ppermute | solution.py:49
  51.2 16.5 %collective-permute-start.8 = (f32[4,256,128]{2,1,0:T(8,128)S(1)}, f32[4,256,128]{2,1,0:T(8,128)S(1)}, u32[]{:S(2)}, u32[]{:S(2)}) collective-permute-start(f32[4,256,128]{2,1,0:T(8,128)S(1)} %get-tuple-element.47), channel_id=1, source_target_pairs={{0,64},{4,20},{8,72},{12,28},{16,80},{20,4},{24,88},{28,12},{32,96... | collective-permute-start | bytes 1572872 | tf_op jit(solution)/shard_map/ppermute | solution.py:49
  54.7 16.0 %collective-permute-start.9 = (f32[4,256,128]{2,1,0:T(8,128)S(1)}, f32[4,256,128]{2,1,0:T(8,128)S(1)}, u32[]{:S(2)}, u32[]{:S(2)}) collective-permute-start(f32[4,256,128]{2,1,0:T(8,128)S(1)} %get-tuple-element.48), channel_id=1, source_target_pairs={{0,96},{4,28},{8,104},{12,20},{16,112},{20,12},{24,120},{28,4},{32... | collective-permute-start | bytes 1572872 | tf_op jit(solution)/shard_map/ppermute | solution.py:49
  61.7 22.1 %collective-permute-start.10 = (f32[4,256,128]{2,1,0:T(8,128)S(1)}, f32[4,256,128]{2,1,0:T(8,128)S(1)}, u32[]{:S(2)}, u32[]{:S(2)}) collective-permute-start(f32[4,256,128]{2,1,0:T(8,128)S(1)} %get-tuple-element.50), channel_id=1, source_target_pairs={{0,32},{4,12},{8,40},{12,4},{16,48},{20,28},{24,56},{28,20},{32,0}... | collective-permute-start | bytes 1572872 | tf_op jit(solution)/shard_map/ppermute | solution.py:49
  61.8 22.0 %collective-permute-start.11 = (f32[4,256,128]{2,1,0:T(8,128)S(1)}, f32[4,256,128]{2,1,0:T(8,128)S(1)}, u32[]{:S(2)}, u32[]{:S(2)}) collective-permute-start(f32[4,256,128]{2,1,0:T(8,128)S(1)} %get-tuple-element.51), channel_id=1, source_target_pairs={{0,64},{4,20},{8,72},{12,28},{16,80},{20,4},{24,88},{28,12},{32,96... | collective-permute-start | bytes 1572872 | tf_op jit(solution)/shard_map/ppermute | solution.py:49
  66.4 18.8 %collective-permute-start.12 = (f32[4,256,128]{2,1,0:T(8,128)S(1)}, f32[4,256,128]{2,1,0:T(8,128)S(1)}, u32[]{:S(2)}, u32[]{:S(2)}) collective-permute-start(f32[4,256,128]{2,1,0:T(8,128)S(1)} %get-tuple-element.52), channel_id=1, source_target_pairs={{0,96},{4,28},{8,104},{12,20},{16,112},{20,12},{24,120},{28,4},{32... | collective-permute-start | bytes 1572872 | tf_op jit(solution)/shard_map/ppermute | solution.py:49
  81.7 14.5 %collective-permute-start.13 = (f32[4,256,128]{2,1,0:T(8,128)S(1)}, f32[4,256,128]{2,1,0:T(8,128)S(1)}, u32[]{:S(2)}, u32[]{:S(2)}) collective-permute-start(f32[4,256,128]{2,1,0:T(8,128)S(1)} %all_to_all.16.mine_zero.refs_0_), channel_id=1, source_target_pairs={{0,1},{1,2},{2,3},{3,0},{4,5},{5,6},{6,7},{7,4},{8,9},{9,10},{10,1... | collective-permute-start | bytes 1572872 | tf_op jit(solution)/shard_map/ppermute | solution.py:61
  82.2 15.3 %collective-permute-start.14 = (f32[4,256,128]{2,1,0:T(8,128)S(1)}, f32[4,256,128]{2,1,0:T(8,128)S(1)}, u32[]{:S(2)}, u32[]{:S(2)}) collective-permute-start(f32[4,256,128]{2,1,0:T(8,128)S(1)} %all_to_all.16.mine_zero.refs_0_), channel_id=1, source_target_pairs={{0,3},{1,0},{2,1},{3,2},{4,7},{5,4},{6,5},{7,6},{8,11},{9,8},{10,9... | collective-permute-start | bytes 1572872 | tf_op jit(solution)/shard_map/ppermute | solution.py:61
  97.6 14.7 %collective-permute-start.16 = (f32[4,256,128]{2,1,0:T(8,128)S(1)}, f32[4,256,128]{2,1,0:T(8,128)S(1)}, u32[]{:S(2)}, u32[]{:S(2)}) collective-permute-start(f32[4,256,128]{2,1,0:T(8,128)S(1)} %all_to_all.17.mine_one.refs_6_), channel_id=1, source_target_pairs={{0,1},{1,2},{2,3},{3,0},{4,5},{5,6},{6,7},{7,4},{8,9},{9,10},{10,1... | collective-permute-start | bytes 1572872 | tf_op jit(solution)/shard_map/ppermute | solution.py:61
  97.9 15.3 %collective-permute-start.17 = (f32[4,256,128]{2,1,0:T(8,128)S(1)}, f32[4,256,128]{2,1,0:T(8,128)S(1)}, u32[]{:S(2)}, u32[]{:S(2)}) collective-permute-start(f32[4,256,128]{2,1,0:T(8,128)S(1)} %all_to_all.17.mine_one.refs_6_), channel_id=1, source_target_pairs={{0,3},{1,0},{2,1},{3,2},{4,7},{5,4},{6,5},{7,6},{8,11},{9,8},{10,9... | collective-permute-start | bytes 1572872 | tf_op jit(solution)/shard_map/ppermute | solution.py:61
  99.6 23.9 %collective-permute-start.15 = (f32[4,256,128]{2,1,0:T(8,128)S(1)}, f32[4,256,128]{2,1,0:T(8,128)S(1)}, u32[]{:S(2)}, u32[]{:S(2)}) collective-permute-start(f32[4,256,128]{2,1,0:T(8,128)S(1)} %all_to_all.16.mine_zero.refs_0_), channel_id=1, source_target_pairs={{0,4},{4,0},{8,12},{12,8},{16,20},{20,16},{24,28},{28,24},{32,36},... | collective-permute-start | bytes 1572872 | tf_op jit(solution)/shard_map/ppermute | solution.py:53
  99.6 18.3 %collective-permute-start.19 = (f32[2,256,128]{2,1,0:T(8,128)S(1)}, f32[2,256,128]{2,1,0:T(8,128)S(1)}, u32[]{:S(2)}, u32[]{:S(2)}) collective-permute-start(f32[2,256,128]{2,1,0:T(8,128)S(1)} %slice.128), channel_id=1, source_target_pairs={{0,1},{1,2},{2,3},{3,0},{4,5},{5,6},{6,7},{7,4},{8,9},{9,10},{10,1... | collective-permute-start | bytes 786440 | tf_op jit(solution)/shard_map/ppermute | solution.py:61
  113.1 15.6 %collective-permute-start.18 = (f32[4,256,128]{2,1,0:T(8,128)S(1)}, f32[4,256,128]{2,1,0:T(8,128)S(1)}, u32[]{:S(2)}, u32[]{:S(2)}) collective-permute-start(f32[4,256,128]{2,1,0:T(8,128)S(1)} %all_to_all.17.mine_one.refs_6_), channel_id=1, source_target_pairs={{0,4},{4,0},{8,12},{12,8},{16,20},{20,16},{24,28},{28,24},{32,36},... | collective-permute-start | bytes 1572872 | tf_op jit(solution)/shard_map/ppermute | solution.py:53
  113.1 10.4 %collective-permute-start.20 = (f32[2,256,128]{2,1,0:T(8,128)S(1)}, f32[2,256,128]{2,1,0:T(8,128)S(1)}, u32[]{:S(2)}, u32[]{:S(2)}) collective-permute-start(f32[2,256,128]{2,1,0:T(8,128)S(1)} %slice.129), channel_id=1, source_target_pairs={{0,3},{1,0},{2,1},{3,2},{4,7},{5,4},{6,5},{7,6},{8,11},{9,8},{10,9... | collective-permute-start | bytes 786440 | tf_op jit(solution)/shard_map/ppermute | solution.py:61
  113.8 9.8 %collective-permute-start.21 = (f32[2,256,128]{2,1,0:T(8,128)S(1)}, f32[2,256,128]{2,1,0:T(8,128)S(1)}, u32[]{:S(2)}, u32[]{:S(2)}) collective-permute-start(f32[2,256,128]{2,1,0:T(8,128)S(1)} %slice.130), channel_id=1, source_target_pairs={{0,1},{1,2},{2,3},{3,0},{4,5},{5,6},{6,7},{7,4},{8,9},{9,10},{10,1... | collective-permute-start | bytes 786440 | tf_op jit(solution)/shard_map/ppermute | solution.py:61
  117.9 10.8 %collective-permute-start.22 = (f32[2,256,128]{2,1,0:T(8,128)S(1)}, f32[2,256,128]{2,1,0:T(8,128)S(1)}, u32[]{:S(2)}, u32[]{:S(2)}) collective-permute-start(f32[2,256,128]{2,1,0:T(8,128)S(1)} %slice.131), channel_id=1, source_target_pairs={{0,3},{1,0},{2,1},{3,2},{4,7},{5,4},{6,5},{7,6},{8,11},{9,8},{10,9... | collective-permute-start | bytes 786440 | tf_op jit(solution)/shard_map/ppermute | solution.py:61
  132.2 14.9 %collective-permute-start.23 = (f32[4,128,512]{2,1,0:T(8,128)S(1)}, f32[4,128,512]{2,1,0:T(8,128)S(1)}, u32[]{:S(2)}, u32[]{:S(2)}) collective-permute-start(f32[4,128,512]{2,1,0:T(8,128)S(1)} %get-tuple-element.57), channel_id=1, source_target_pairs={{0,8},{4,36},{8,0},{12,44},{16,24},{20,52},{24,16},{28,60},{32,40}... | collective-permute-start | bytes 3145736 | tf_op jit(solution)/shard_map/ppermute | solution.py:49
  134.3 14.8 %collective-permute-start.26 = (f32[4,128,512]{2,1,0:T(8,128)S(1)}, f32[4,128,512]{2,1,0:T(8,128)S(1)}, u32[]{:S(2)}, u32[]{:S(2)}) collective-permute-start(f32[4,128,512]{2,1,0:T(8,128)S(1)} %get-tuple-element.59), channel_id=1, source_target_pairs={{0,24},{4,100},{8,16},{12,108},{16,8},{20,116},{24,0},{28,124},{32... | collective-permute-start | bytes 3145736 | tf_op jit(solution)/shard_map/ppermute | solution.py:49
  137.7 20.6 %collective-permute-start.30 = (f32[4,128,512]{2,1,0:T(8,128)S(1)}, f32[4,128,512]{2,1,0:T(8,128)S(1)}, u32[]{:S(2)}, u32[]{:S(2)}) collective-permute-start(f32[4,128,512]{2,1,0:T(8,128)S(1)} %get-tuple-element.62), channel_id=1, source_target_pairs={{0,8},{4,36},{8,0},{12,44},{16,24},{20,52},{24,16},{28,60},{32,40}... | collective-permute-start | bytes 3145736 | tf_op jit(solution)/shard_map/ppermute | solution.py:49
  138.6 21.8 %collective-permute-start.33 = (f32[4,128,512]{2,1,0:T(8,128)S(1)}, f32[4,128,512]{2,1,0:T(8,128)S(1)}, u32[]{:S(2)}, u32[]{:S(2)}) collective-permute-start(f32[4,128,512]{2,1,0:T(8,128)S(1)} %get-tuple-element.64), channel_id=1, source_target_pairs={{0,24},{4,100},{8,16},{12,108},{16,8},{20,116},{24,0},{28,124},{32... | collective-permute-start | bytes 3145736 | tf_op jit(solution)/shard_map/ppermute | solution.py:49
  147.2 18.8 %collective-permute-start.24 = (f32[2,128,512]{2,1,0:T(8,128)S(1)}, f32[2,128,512]{2,1,0:T(8,128)S(1)}, u32[]{:S(2)}, u32[]{:S(2)}) collective-permute-start(f32[2,128,512]{2,1,0:T(8,128)S(1)} %slice_add_fusion.3), channel_id=1, source_target_pairs={{0,24},{4,100},{8,16},{12,108},{16,8},{20,116},{24,0},{28,124},{32... | collective-permute-start | bytes 1572872 | tf_op jit(solution)/shard_map/ppermute | solution.py:49
  149.2 16.8 %collective-permute-start.27 = (f32[2,128,512]{2,1,0:T(8,128)S(1)}, f32[2,128,512]{2,1,0:T(8,128)S(1)}, u32[]{:S(2)}, u32[]{:S(2)}) collective-permute-start(f32[2,128,512]{2,1,0:T(8,128)S(1)} %slice_add_fusion.2), channel_id=1, source_target_pairs={{0,8},{4,36},{8,0},{12,44},{16,24},{20,52},{24,16},{28,60},{32,40}... | collective-permute-start | bytes 1572872 | tf_op jit(solution)/shard_map/ppermute | solution.py:49
  158.4 18.7 %collective-permute-start.31 = (f32[2,128,512]{2,1,0:T(8,128)S(1)}, f32[2,128,512]{2,1,0:T(8,128)S(1)}, u32[]{:S(2)}, u32[]{:S(2)}) collective-permute-start(f32[2,128,512]{2,1,0:T(8,128)S(1)} %slice_add_fusion.1), channel_id=1, source_target_pairs={{0,24},{4,100},{8,16},{12,108},{16,8},{20,116},{24,0},{28,124},{32... | collective-permute-start | bytes 1572872 | tf_op jit(solution)/shard_map/ppermute | solution.py:49
  160.4 16.7 %collective-permute-start.34 = (f32[2,128,512]{2,1,0:T(8,128)S(1)}, f32[2,128,512]{2,1,0:T(8,128)S(1)}, u32[]{:S(2)}, u32[]{:S(2)}) collective-permute-start(f32[2,128,512]{2,1,0:T(8,128)S(1)} %slice_add_fusion), channel_id=1, source_target_pairs={{0,8},{4,36},{8,0},{12,44},{16,24},{20,52},{24,16},{28,60},{32,40}... | collective-permute-start | bytes 1572872 | tf_op jit(solution)/shard_map/ppermute | solution.py:49
  166.2 12.8 %collective-permute-start.25 = (f32[128,512]{1,0:T(8,128)S(1)}, f32[128,512]{1,0:T(8,128)S(1)}, u32[]{:S(2)}, u32[]{:S(2)}) collective-permute-start(f32[128,512]{1,0:T(8,128)S(1)} %get-tuple-element.70), channel_id=1, source_target_pairs={{0,32},{4,12},{8,40},{12,4},{16,48},{20,28},{24,56},{28,20},{32,0}... | collective-permute-start | bytes 786440 | tf_op jit(solution)/shard_map/ppermute | solution.py:49
  166.3 15.8 %collective-permute-start.28 = (f32[128,512]{1,0:T(8,128)S(1)}, f32[128,512]{1,0:T(8,128)S(1)}, u32[]{:S(2)}, u32[]{:S(2)}) collective-permute-start(f32[128,512]{1,0:T(8,128)S(1)} %get-tuple-element.67), channel_id=1, source_target_pairs={{0,64},{4,20},{8,72},{12,28},{16,80},{20,4},{24,88},{28,12},{32,96... | collective-permute-start | bytes 786440 | tf_op jit(solution)/shard_map/ppermute | solution.py:49
  168.3 13.9 %collective-permute-start.29 = (f32[128,512]{1,0:T(8,128)S(1)}, f32[128,512]{1,0:T(8,128)S(1)}, u32[]{:S(2)}, u32[]{:S(2)}) collective-permute-start(f32[128,512]{1,0:T(8,128)S(1)} %get-tuple-element.66), channel_id=1, source_target_pairs={{0,96},{4,28},{8,104},{12,20},{16,112},{20,12},{24,120},{28,4},{32... | collective-permute-start | bytes 786440 | tf_op jit(solution)/shard_map/ppermute | solution.py:49
  177.4 6.5 %collective-permute-start.32 = (f32[128,512]{1,0:T(8,128)S(1)}, f32[128,512]{1,0:T(8,128)S(1)}, u32[]{:S(2)}, u32[]{:S(2)}) collective-permute-start(f32[128,512]{1,0:T(8,128)S(1)} %get-tuple-element.71), channel_id=1, source_target_pairs={{0,32},{4,12},{8,40},{12,4},{16,48},{20,28},{24,56},{28,20},{32,0}... | collective-permute-start | bytes 786440 | tf_op jit(solution)/shard_map/ppermute | solution.py:49
  177.5 8.8 %collective-permute-start.35 = (f32[128,512]{1,0:T(8,128)S(1)}, f32[128,512]{1,0:T(8,128)S(1)}, u32[]{:S(2)}, u32[]{:S(2)}) collective-permute-start(f32[128,512]{1,0:T(8,128)S(1)} %get-tuple-element.69), channel_id=1, source_target_pairs={{0,64},{4,20},{8,72},{12,28},{16,80},{20,4},{24,88},{28,12},{32,96... | collective-permute-start | bytes 786440 | tf_op jit(solution)/shard_map/ppermute | solution.py:49
  179.0 10.0 %collective-permute-start.36 = (f32[128,512]{1,0:T(8,128)S(1)}, f32[128,512]{1,0:T(8,128)S(1)}, u32[]{:S(2)}, u32[]{:S(2)}) collective-permute-start(f32[128,512]{1,0:T(8,128)S(1)} %get-tuple-element.68), channel_id=1, source_target_pairs={{0,96},{4,28},{8,104},{12,20},{16,112},{20,12},{24,120},{28,4},{32... | collective-permute-start | bytes 786440 | tf_op jit(solution)/shard_map/ppermute | solution.py:49

commit v5 on v4

--- a/solution.py
+++ b/solution.py
@@ -108,59 +108,61 @@
     )
 
 
-def local_kernel(_, table_ref, signs_ref, own_ref, other_ref, *refs):
-    outs, held_ref, sems = refs[:-2], refs[-2], refs[-1]
-    step = pl.program_id(0)
+def local_kernel(where_ref, table_ref, signs_ref, design_ref, *refs):
+    outs, (taken_ref, parts_ref, held_ref, in_sems, sems) = refs[:-5], refs[-5:]
     size = table_ref.shape[0]
-    parts = []
-    for number in range(own_ref.shape[0] // size):
+    count = design_ref.shape[0] // size
+    arrivals = []
+    for number in range(count):
         rows = pl.ds(number * size, size)
-        signed_table = table_ref[...] * signs_ref[:, rows].astype(jnp.bfloat16)
-        high, low = split(jnp.concatenate([own_ref[rows, :], other_ref[rows, :]], axis=1))
+        arrivals.append(pltpu.make_async_copy(design_ref.at[rows, :], taken_ref.at[number], in_sems.at[number]))
+        arrivals[-1].start()
+    for number, arrival in enumerate(arrivals):
+        signed_table = table_ref[...] * signs_ref[:, pl.ds(number * size, size)].astype(jnp.bfloat16)
+        arrival.wait()
+        high, low = split(taken_ref[number])
         part = jnp.dot(signed_table, high, preferred_element_type=jnp.float32)
-        parts.append(part + jnp.dot(signed_table, low, preferred_element_type=jnp.float32))
-    for number, part in enumerate(butterfly(parts)):
-        rows = pl.ds(number * size, size)
-        held_ref[step, 0, rows, :] = part[:, :LANE]
-        held_ref[step, 1, rows, :] = part[:, LANE:]
-
-    def copy(k, side):
-        return pltpu.make_async_copy(held_ref.at[k, side], outs[SIDE * side + k], sems.at[k, side])
-
+        parts_ref[number] = part + jnp.dot(signed_table, low, preferred_element_type=jnp.float32)
+    copies = []
     for k in range(SIDE):
-
-        @pl.when(step == k)
-        def _():
-            copy(k, 0).start()
-            copy(k, 1).start()
-
-    @pl.when(step == SIDE - 1)
-    def _():
-        for k in range(SIDE):
-            copy(k, 0).wait()
-            copy(k, 1).wait()
+        blocks = (2 * (where_ref[1] ^ k) + where_ref[0], 2 * (where_ref[2] ^ k) + 1 - where_ref[0])
+        for side, block in enumerate(blocks):
+            lanes = pl.ds(pl.multiple_of(block * LANE, LANE), LANE)
+            parts = butterfly([parts_ref[number, :, lanes] for number in range(count)])
+            for number, part in enumerate(parts):
+                held_ref[k, side, pl.ds(number * size, size), :] = part
+            copies.append(pltpu.make_async_copy(held_ref.at[k, side], outs[SIDE * side + k], sems.at[k, side]))
+            copies[-1].start()
+    for copy in copies:
+        copy.wait()
 
 
 def local_transform(where, design, signs, table):
-    rows = design.shape[0]
+    rows, width = design.shape
     size = table.shape[0]
+    count = rows // size
     return call(
         local_kernel,
-        (SIDE,),
+        (),
         [
-            fixed((size, size)),
-            fixed((1, rows)),
-            pl.BlockSpec((rows, LANE), lambda k, w: (0, 2 * (w[1] ^ k) + w[0])),
-            pl.BlockSpec((rows, LANE), lambda k, w: (0, 2 * (w[2] ^ k) + 1 - w[0])),
+            pl.BlockSpec(memory_space=pltpu.SMEM),
+            pl.BlockSpec(memory_space=pltpu.VMEM),
+            pl.BlockSpec(memory_space=pltpu.VMEM),
+            pl.BlockSpec(memory_space=pl.ANY),
         ],
         [pl.BlockSpec(memory_space=pl.ANY)] * (2 * SIDE),
         [f32(rows, LANE)] * (2 * SIDE),
-        scalars=1,
-        scratch=[pltpu.VMEM((SIDE, 2, rows, LANE), jnp.float32), pltpu.SemaphoreType.DMA((SIDE, 2))],
+        scratch=[
+            pltpu.VMEM((count, size, width), jnp.float32),
+            pltpu.VMEM((count, size, width), jnp.float32),
+            pltpu.VMEM((SIDE, 2, rows, LANE), jnp.float32),
+            pltpu.SemaphoreType.DMA((count,)),
+            pltpu.SemaphoreType.DMA((SIDE, 2)),
+        ],
         flops=2**30,
         moved=2**23,
         vmem=60 * 2**20,
-    )(where, table, signs, design, design)
+    )(where, table, signs, design)
 
 
 def sample_kernel(scale, chunk, owned, where_ref, index_ref, *refs):
@@ -363,10 +365,12 @@
         sums = (picked[0] + arrived[0]) + (arrived[1] + arrived[2])
         mine = exchange(sums, FIRST)
         if gathered:
-            mine, *_ = lax.optimization_barrier((mine, gathered[0][2], gathered[0][3]))
+            mine, *_ = lax.optimization_barrier((mine, *gathered[0][1:4]))
         right, left = around(mine, 1), around(mine, 3)
-        far_a, far_b = around(right[: SIDE // 2], 1), around(left[SIDE // 2 :], 3)
-        swapped, *_ = lax.optimization_barrier((mine, right, left))
+        swapped, onward, back = mine, right, left
+        if gathered:
+            swapped, onward, back, *_ = lax.optimization_barrier((mine, right, left, *gathered[0][4:]))
+        far_a, far_b = around(onward[: SIDE // 2], 1), around(back[SIDE // 2 :], 3)
         gathered.append((mine, to_sibling(swapped), right, left, far_a, far_b))
 
     sketch = sketch_rows(where, gathered[0][0], gathered[1][0], gathered[0][1], gathered[1][1])

time: 190 us -> 190 us (level)
    ppermute x23, waiting for transfers between devices: 32.9 us -> 30.4 us  [hop(): return lax.ppermute(value, 'row', partners(ring, step))]
    ppermute x2, starting transfers between devices: 0.01 us -> 1.97 us  [to_sibling(): return lax.ppermute(value, 'row', [(i, i ^ 1) for i in range(32)])]
  transfers between devices with their start and end apart: 38 -> 38, of which waited for: 21 -> 20; matrix products, arithmetic and copies ran while one was open for 1% -> 1% of each run, Pallas kernels for 9% -> 9%
where the time goes in v5:
time: 190 us
  waiting for transfers between devices  72 us (38%)
  starting transfers between devices  55.9 us (29%)
  Pallas kernels  34.5 us (18%)
  blocking collectives  21.8 us (11%)
  other arithmetic  2.83 us (1%)
    ppermute x23, starting transfers between devices, hop(): return lax.ppermute(value, 'row', partners(ring, step))  33 us
    ppermute x23, waiting for transfers between devices, hop(): return lax.ppermute(value, 'row', partners(ring, step))  30.4 us
    ppermute x8, waiting for transfers between devices, around(): lax.ppermute(value, 'col', [(i, (i + step) % SIDE) for i in range(SIDE)])  25.7 us
    all_to_all x2, blocking collectives, exchange(): lax.all_to_all(value, 'row', 0, 0, tiled=True, axis_index_groups=groups(r...  21.8 us
    pallas_call x2, Pallas kernels, sampled_rows(): call(functools.partial(sample_kernel, scale, chunk, owned), (), [pl.Block...  13.8 us
    pallas_call x3, Pallas kernels, gram_shares(): call(functools.partial(gram_kernel, plan, halves), (), [pl.BlockSpec(memo...  12.8 us
    ppermute x4, waiting for transfers between devices, across(): lax.ppermute(value, 'row', [(i ^ 1, j) for i, j in partners(FIRST, step)])  11.6 us
    ppermute x8, starting transfers between devices, around(): lax.ppermute(value, 'col', [(i, (i + step) % SIDE) for i in range(SIDE)])  8.41 us
  transfers between devices with their start and end apart: 38, of which 20 were waited for; matrix products, arithmetic and copies ran while one was open for 1% of the time, Pallas kernels for 9%

profile of v5, /device:TPU:14, one launch (start us, length us, event | category | flops | bytes accessed | tf_op | source)
XLA Modules:
  0.0 189.7 jit_solution(2029401744394190802)
XLA Ops:
  0.7 0.6 pad_add_fusion.where_ref
  1.3 6.3 %shard_map.59 = (f32[1024,128]{1,0:T(8,128)}, f32[1024,128]{1,0:T(8,128)}, f32[1024,128]{1,0:T(8,128)}, f32[1024,128]{1,0:T(8,128)}, f32[1024,128]{1,0:T(8,128)}...) custom-call(s32[4]{0:T(128)} %pad_add_fusion.where_ref, ...), custom_call_target="tpu_custom_call" | custom-call | flops 1073741824 | bytes 8388608 | tf_op jit(solution)/shard_map/pallas_call | solution.py:144
  7.6 0.5 collective-permute-start
  8.1 2.6 %collective-permute-start.1 = (f32[1024,128]{1,0:T(8,128)}, f32[1024,128]{1,0:T(8,128)S(1)}, u32[]{:S(2)}, u32[]{:S(2)}) collective-permute-start(f32[1024,128]{1,0:T(8,128)} %get-tuple-element.40), channel_id=1, source_target_pairs={{0,16},{4,68},{8,24},{12,76},{16,0},{20,84},{24,8},{28,92},{32,48}... | collective-permute-start | bytes 1572872 | tf_op jit(solution)/shard_map/ppermute | solution.py:49
  10.7 0.6 broadcast_in_dim.7
  11.3 7.4 %all-to-all-start = ((s32[32,1,256]{2,1,0:T(1,128)}), s32[32,1,256]{2,1,0:T(1,128)S(1)}, u32[]{:S(2)}, u32[]{:S(2)}) async-start(s32[32,1,256]{2,1,0:T(1,128)} %broadcast_in_dim.7), calls=%async_computation | async-start | bytes 65536 | tf_op jit(solution)/shard_map/all_to_all | solution.py:331
  18.8 1.5 collective-permute-start.2
  20.3 0.9 collective-permute-start.4
  21.2 3.5 %collective-permute-start.5 = (f32[1024,128]{1,0:T(8,128)}, f32[1024,128]{1,0:T(8,128)S(1)}, u32[]{:S(2)}, u32[]{:S(2)}) collective-permute-start(f32[1024,128]{1,0:T(8,128)} %get-tuple-element.44), channel_id=1, source_target_pairs={{4,16},{0,68},{12,24},{8,76},{20,0},{16,84},{28,8},{24,92},{36,48}... | collective-permute-start | bytes 1572872 | tf_op jit(solution)/shard_map/ppermute | solution.py:57
  24.8 4.3 %all-to-all-done = s32[32,1,256]{2,1,0:T(1,128)S(1)} async-done(((s32[32,1,256]{2,1,0:T(1,128)}), s32[32,1,256]{2,1,0:T(1,128)S(1)}, u32[]{:S(2)}, u32[]{:S(2)}) %all-to-all-start) | async-done | bytes 32800 | tf_op jit(solution)/shard_map/all_to_all | solution.py:331
  29.4 0.4 collective-permute-start.3
  29.9 6.1 %collective-permute-done.5.refs_6_ = f32[1024,128]{1,0:T(8,128)S(1)} collective-permute-done((f32[1024,128]{1,0:T(8,128)}, f32[1024,128]{1,0:T(8,128)S(1)}, u32[]{:S(2)}, u32[]{:S(2)}) %collective-permute-start.5) | collective-permute-done | bytes 524320 | tf_op jit(solution)/shard_map/ppermute | solution.py:57
  35.9 5.5 %collective-permute-done.6.refs_7_ = f32[1024,128]{1,0:T(8,128)S(1)} collective-permute-done((f32[1024,128]{1,0:T(8,128)}, f32[1024,128]{1,0:T(8,128)S(1)}, u32[]{:S(2)}, u32[]{:S(2)}) %collective-permute-start.6) | collective-permute-done | bytes 524320 | tf_op jit(solution)/shard_map/ppermute | solution.py:57
  41.5 1.0 copy-done
  42.5 6.9 %shard_map.60 = (f32[4,256,128]{2,1,0:T(8,128)S(1)}, f32[4,256,128]{2,1,0:T(8,128)S(1)}, f32[4,256,128]{2,1,0:T(8,128)S(1)}, f32[4,256,128]{2,1,0:T(8,128)S(1)}) custom-call(s32[4]{0:T(128)S(1)} %copy-done.1, s32[8192]{0:T(1024)S(1)} %fusion.13.index_ref, f32[1024,128]{1,0:T(8,128)S(1)} %copy-done, f32[1024,128]{1,0:T(8,128)S(1)} %collective-permute-done.refs_1_, ...), custom_call_target="tpu_custom_call" | custom-call | flops 16777216 | bytes 8388608 | tf_op jit(solution)/shard_map/pallas_call | solution.py:210
  49.4 1.4 collective-permute-start.7
  50.9 3.6 %collective-permute-start.8 = (f32[4,256,128]{2,1,0:T(8,128)S(1)}, f32[4,256,128]{2,1,0:T(8,128)S(1)}, u32[]{:S(2)}, u32[]{:S(2)}) collective-permute-start(f32[4,256,128]{2,1,0:T(8,128)S(1)} %get-tuple-element.48), channel_id=1, source_target_pairs={{0,64},{4,20},{8,72},{12,28},{16,80},{20,4},{24,88},{28,12},{32,96... | collective-permute-start | bytes 1572872 | tf_op jit(solution)/shard_map/ppermute | solution.py:49
  54.5 6.9 %shard_map.61 = (f32[4,256,128]{2,1,0:T(8,128)S(1)}, f32[4,256,128]{2,1,0:T(8,128)S(1)}, f32[4,256,128]{2,1,0:T(8,128)S(1)}, f32[4,256,128]{2,1,0:T(8,128)S(1)}) custom-call(s32[4]{0:T(128)S(1)} %copy-done.1, s32[8192]{0:T(1024)S(1)} %fusion.13.index_ref, f32[1024,128]{1,0:T(8,128)S(1)} %copy-done, f32[1024,128]{1,0:T(8,128)S(1)} %collective-permute-done.refs_1_, ...), custom_call_target="tpu_custom_call" | custom-call | flops 16777216 | bytes 8388608 | tf_op jit(solution)/shard_map/pallas_call | solution.py:210
  61.5 4.7 %collective-permute-start.11 = (f32[4,256,128]{2,1,0:T(8,128)S(1)}, f32[4,256,128]{2,1,0:T(8,128)S(1)}, u32[]{:S(2)}, u32[]{:S(2)}) collective-permute-start(f32[4,256,128]{2,1,0:T(8,128)S(1)} %get-tuple-element.52), channel_id=1, source_target_pairs={{0,64},{4,20},{8,72},{12,28},{16,80},{20,4},{24,88},{28,12},{32,96... | collective-permute-start | bytes 1572872 | tf_op jit(solution)/shard_map/ppermute | solution.py:49
  66.2 1.2 collective-permute-done.8
  67.3 3.1 %collective-permute-done.9 = f32[4,256,128]{2,1,0:T(8,128)S(1)} collective-permute-done((f32[4,256,128]{2,1,0:T(8,128)S(1)}, f32[4,256,128]{2,1,0:T(8,128)S(1)}, u32[]{:S(2)}, u32[]{:S(2)}) %collective-permute-start.9) | collective-permute-done | bytes 524320 | tf_op jit(solution)/shard_map/ppermute | solution.py:49
  70.6 10.9 %all_to_all.16.mine_zero.refs_0_ = f32[4,256,128]{2,1,0:T(8,128)S(1)} all-to-all(f32[4,256,128]{2,1,0:T(8,128)S(1)} %add_add_fusion.1), channel_id=1, replica_groups={{0,8,16,24},{4,36,68,100},{32,40,48,56},{12,44,76,108},{64,72,80,88},{2..., dimensions={0} | all-to-all | bytes 1048576 | tf_op jit(solution)/shard_map/all_to_all | solution.py:45
  81.5 2.0 %collective-permute-start.13 = (f32[4,256,128]{2,1,0:T(8,128)S(1)}, f32[4,256,128]{2,1,0:T(8,128)S(1)}, u32[]{:S(2)}, u32[]{:S(2)}) collective-permute-start(f32[4,256,128]{2,1,0:T(8,128)S(1)} %all_to_all.16.mine_zero.refs_0_), channel_id=1, source_target_pairs={{0,4},{4,0},{8,12},{12,8},{16,20},{20,16},{24,28},{28,24},{32,36},... | collective-permute-start | bytes 1572872 | tf_op jit(solution)/shard_map/ppermute | solution.py:53
  83.4 0.5 collective-permute-start.14
  83.9 1.5 collective-permute-start.15
  85.6 10.9 %all_to_all.17.mine_one.refs_6_ = f32[4,256,128]{2,1,0:T(8,128)S(1)} all-to-all(f32[4,256,128]{2,1,0:T(8,128)S(1)} %add_add_fusion), channel_id=1, replica_groups={{0,8,16,24},{4,36,68,100},{32,40,48,56},{12,44,76,108},{64,72,80,88},{2..., dimensions={0} | all-to-all | bytes 1048576 | tf_op jit(solution)/shard_map/all_to_all | solution.py:45
  96.5 0.8 collective-permute-done.14.refs_2_
  97.3 1.4 collective-permute-done.15.refs_3_
  98.7 0.3 collective-permute-start.16
  99.0 1.8 collective-permute-start.17
  100.8 1.5 collective-permute-start.18
  102.3 0.6 collective-permute-start.19
  102.9 14.0 %collective-permute-done.18.refs_4_ = f32[2,256,128]{2,1,0:T(8,128)S(1)} collective-permute-done((f32[2,256,128]{2,1,0:T(8,128)S(1)}, f32[2,256,128]{2,1,0:T(8,128)S(1)}, u32[]{:S(2)}, u32[]{:S(2)}) %collective-permute-start.18) | collective-permute-done | bytes 262176 | tf_op jit(solution)/shard_map/ppermute | solution.py:61
  117.0 1.5 collective-permute-done.19.refs_5_
  118.5 0.4 collective-permute-start.21
  119.0 1.7 collective-permute-start.22
  120.7 6.6 %collective-permute-done.21.refs_10_ = f32[2,256,128]{2,1,0:T(8,128)S(1)} collective-permute-done((f32[2,256,128]{2,1,0:T(8,128)S(1)}, f32[2,256,128]{2,1,0:T(8,128)S(1)}, u32[]{:S(2)}, u32[]{:S(2)}) %collective-permute-start.21) | collective-permute-done | bytes 262176 | tf_op jit(solution)/shard_map/ppermute | solution.py:61
  127.3 1.4 collective-permute-done.22.refs_11_
  128.7 3.4 %shard_map.64 = (f32[4,128,512]{2,1,0:T(8,128)S(1)}, f32[4,128,512]{2,1,0:T(8,128)S(1)}) custom-call(s32[4]{0:T(128)S(1)} %copy-done.1, f32[4,256,128]{2,1,0:T(8,128)S(1)} %all_to_all.16.mine_zero.refs_0_, f32[4,256,128]{2,1,0:T(8,128)S(1)} %collective-permute-done.13.sibling_zero.refs_1_, f32[4,256,128]{2,1,0:T(8,128)S(1)} %collective-permute-done.14.refs_2_, ...), custom_call_target="tpu_custom_call" | custom-call | flops 3221225472 | bytes 8388608 | tf_op jit(solution)/shard_map/pallas_call | solution.py:311
  132.1 2.0 %collective-permute-start.23 = (f32[4,128,512]{2,1,0:T(8,128)S(1)}, f32[4,128,512]{2,1,0:T(8,128)S(1)}, u32[]{:S(2)}, u32[]{:S(2)}) collective-permute-start(f32[4,128,512]{2,1,0:T(8,128)S(1)} %get-tuple-element.59), channel_id=1, source_target_pairs={{0,8},{4,36},{8,0},{12,44},{16,24},{20,52},{24,16},{28,60},{32,40}... | collective-permute-start | bytes 3145736 | tf_op jit(solution)/shard_map/ppermute | solution.py:49
  134.2 3.4 %shard_map.65 = (f32[4,128,512]{2,1,0:T(8,128)S(1)}, f32[4,128,512]{2,1,0:T(8,128)S(1)}) custom-call(s32[4]{0:T(128)S(1)} %copy-done.1, f32[4,256,128]{2,1,0:T(8,128)S(1)} %all_to_all.16.mine_zero.refs_0_, f32[4,256,128]{2,1,0:T(8,128)S(1)} %collective-permute-done.13.sibling_zero.refs_1_, f32[4,256,128]{2,1,0:T(8,128)S(1)} %collective-permute-done.14.refs_2_, ...), custom_call_target="tpu_custom_call" | custom-call | flops 3221225472 | bytes 8388608 | tf_op jit(solution)/shard_map/pallas_call | solution.py:311
  137.6 1.1 collective-permute-start.30
  138.7 1.6 collective-permute-start.33
  140.3 6.0 %shard_map.63 = (f32[2,128,512]{2,1,0:T(8,128)S(1)}, f32[2,128,512]{2,1,0:T(8,128)S(1)}, f32[2,128,512]{2,1,0:T(8,128)S(1)}, f32[2,128,512]{2,1,0:T(8,128)S(1)},...) custom-call(s32[4]{0:T(128)S(1)} %copy-done.1, f32[4,256,128]{2,1,0:T(8,128)S(1)} %all_to_all.16.mine_zero.refs_0_, ...), custom_call_target="tpu_custom_call" | custom-call | flops 3221225472 | bytes 8388608 | tf_op jit(solution)/shard_map/pallas_call | solution.py:311
  146.3 0.7 collective-permute-done.23
  147.1 0.5 collective-permute-start.24
  147.6 1.3 collective-permute-done.26
  149.0 1.6 collective-permute-start.27
  150.6 7.6 %collective-permute-done.30 = f32[4,128,512]{2,1,0:T(8,128)S(1)} collective-permute-done((f32[4,128,512]{2,1,0:T(8,128)S(1)}, f32[4,128,512]{2,1,0:T(8,128)S(1)}, u32[]{:S(2)}, u32[]{:S(2)}) %collective-permute-start.30) | collective-permute-done | bytes 1048608 | tf_op jit(solution)/shard_map/ppermute | solution.py:49
  158.3 0.5 collective-permute-start.31
  158.8 1.3 collective-permute-done.33
  160.2 1.4 collective-permute-start.34
  161.6 1.6 shard_map.62
  163.2 2.5 %collective-permute-done.24 = f32[2,128,512]{2,1,0:T(8,128)S(1)} collective-permute-done((f32[2,128,512]{2,1,0:T(8,128)S(1)}, f32[2,128,512]{2,1,0:T(8,128)S(1)}, u32[]{:S(2)}, u32[]{:S(2)}) %collective-permute-start.24) | collective-permute-done | bytes 524320 | tf_op jit(solution)/shard_map/ppermute | solution.py:49
  165.7 0.2 fusion.6
  166.1 1.5 collective-permute-start.28
  167.5 3.2 %collective-permute-start.29 = (f32[128,512]{1,0:T(8,128)S(1)}, f32[128,512]{1,0:T(8,128)S(1)}, u32[]{:S(2)}, u32[]{:S(2)}) collective-permute-start(f32[128,512]{1,0:T(8,128)S(1)} %get-tuple-element.68), channel_id=1, source_target_pairs={{0,96},{4,28},{8,104},{12,20},{16,112},{20,12},{24,120},{28,4},{32... | collective-permute-start | bytes 786440 | tf_op jit(solution)/shard_map/ppermute | solution.py:49
  170.8 6.4 %collective-permute-done.31 = f32[2,128,512]{2,1,0:T(8,128)S(1)} collective-permute-done((f32[2,128,512]{2,1,0:T(8,128)S(1)}, f32[2,128,512]{2,1,0:T(8,128)S(1)}, u32[]{:S(2)}, u32[]{:S(2)}) %collective-permute-start.31) | collective-permute-done | bytes 524320 | tf_op jit(solution)/shard_map/ppermute | solution.py:49
  177.6 1.2 collective-permute-start.35
  178.7 3.5 %collective-permute-start.36 = (f32[128,512]{1,0:T(8,128)S(1)}, f32[128,512]{1,0:T(8,128)S(1)}, u32[]{:S(2)}, u32[]{:S(2)}) collective-permute-start(f32[128,512]{1,0:T(8,128)S(1)} %get-tuple-element.70), channel_id=1, source_target_pairs={{0,96},{4,28},{8,104},{12,20},{16,112},{20,12},{24,120},{28,4},{32... | collective-permute-start | bytes 786440 | tf_op jit(solution)/shard_map/ppermute | solution.py:49
  182.4 1.5 collective-permute-done.32
  183.9 2.1 %collective-permute-done.35 = f32[128,512]{1,0:T(8,128)S(1)} collective-permute-done((f32[128,512]{1,0:T(8,128)S(1)}, f32[128,512]{1,0:T(8,128)S(1)}, u32[]{:S(2)}, u32[]{:S(2)}) %collective-permute-start.35) | collective-permute-done | bytes 262176 | tf_op jit(solution)/shard_map/ppermute | solution.py:49
  186.0 2.7 %collective-permute-done.36 = f32[128,512]{1,0:T(8,128)S(1)} collective-permute-done((f32[128,512]{1,0:T(8,128)S(1)}, f32[128,512]{1,0:T(8,128)S(1)}, u32[]{:S(2)}, u32[]{:S(2)}) %collective-permute-start.36) | collective-permute-done | bytes 262176 | tf_op jit(solution)/shard_map/ppermute | solution.py:49
  188.8 0.8 pad_maximum_fusion
  (45 shorter events, 1.9 us)
Async XLA Ops:
  0.6 10.1 %copy-start.2 = (s32[256]{0:T(256)S(1)}, s32[256]{0:T(256)}, u32[]{:S(2)}) copy-start(s32[256]{0:T(256)} %param.6) | copy-start | bytes 3076
  1.3 40.2 %copy-start.1 = (s32[4]{0:T(128)S(1)}, s32[4]{0:T(128)}, u32[]{:S(2)}) copy-start(s32[4]{0:T(128)} %pad_add_fusion.where_ref) | copy-start | bytes 52
  7.6 21.6 %collective-permute-start = (f32[1024,128]{1,0:T(8,128)}, f32[1024,128]{1,0:T(8,128)S(1)}, u32[]{:S(2)}, u32[]{:S(2)}) collective-permute-start(f32[1024,128]{1,0:T(8,128)} %get-tuple-element.39), channel_id=1, source_target_pairs={{0,8},{4,36},{8,0},{12,44},{16,24},{20,52},{24,16},{28,60},{32,40}... | collective-permute-start | bytes 1572872 | tf_op jit(solution)/shard_map/ppermute | solution.py:49
  8.1 21.3 %collective-permute-start.1 = (f32[1024,128]{1,0:T(8,128)}, f32[1024,128]{1,0:T(8,128)S(1)}, u32[]{:S(2)}, u32[]{:S(2)}) collective-permute-start(f32[1024,128]{1,0:T(8,128)} %get-tuple-element.40), channel_id=1, source_target_pairs={{0,16},{4,68},{8,24},{12,76},{16,0},{20,84},{24,8},{28,92},{32,48}... | collective-permute-start | bytes 1572872 | tf_op jit(solution)/shard_map/ppermute | solution.py:49
  11.3 17.7 %all-to-all-start = ((s32[32,1,256]{2,1,0:T(1,128)}), s32[32,1,256]{2,1,0:T(1,128)S(1)}, u32[]{:S(2)}, u32[]{:S(2)}) async-start(s32[32,1,256]{2,1,0:T(1,128)} %broadcast_in_dim.7), calls=%async_computation | async-start | bytes 65536 | tf_op jit(solution)/shard_map/all_to_all | solution.py:331
  18.8 11.1 %collective-permute-start.2 = (f32[1024,128]{1,0:T(8,128)}, f32[1024,128]{1,0:T(8,128)S(1)}, u32[]{:S(2)}, u32[]{:S(2)}) collective-permute-start(f32[1024,128]{1,0:T(8,128)} %get-tuple-element.41), channel_id=1, source_target_pairs={{0,24},{4,100},{8,16},{12,108},{16,8},{20,116},{24,0},{28,124},{32... | collective-permute-start | bytes 1572872 | tf_op jit(solution)/shard_map/ppermute | solution.py:49
  20.3 9.6 %collective-permute-start.4 = (f32[1024,128]{1,0:T(8,128)}, f32[1024,128]{1,0:T(8,128)S(1)}, u32[]{:S(2)}, u32[]{:S(2)}) collective-permute-start(f32[1024,128]{1,0:T(8,128)} %get-tuple-element.43), channel_id=1, source_target_pairs={{4,8},{0,36},{12,0},{8,44},{20,24},{16,52},{28,16},{24,60},{36,40}... | collective-permute-start | bytes 1572872 | tf_op jit(solution)/shard_map/ppermute | solution.py:57
  21.2 14.7 %collective-permute-start.5 = (f32[1024,128]{1,0:T(8,128)}, f32[1024,128]{1,0:T(8,128)S(1)}, u32[]{:S(2)}, u32[]{:S(2)}) collective-permute-start(f32[1024,128]{1,0:T(8,128)} %get-tuple-element.44), channel_id=1, source_target_pairs={{4,16},{0,68},{12,24},{8,76},{20,0},{16,84},{28,8},{24,92},{36,48}... | collective-permute-start | bytes 1572872 | tf_op jit(solution)/shard_map/ppermute | solution.py:57
  29.2 12.3 %collective-permute-start.6 = (f32[1024,128]{1,0:T(8,128)}, f32[1024,128]{1,0:T(8,128)S(1)}, u32[]{:S(2)}, u32[]{:S(2)}) collective-permute-start(f32[1024,128]{1,0:T(8,128)} %get-tuple-element.45), channel_id=1, source_target_pairs={{4,24},{0,100},{12,16},{8,108},{20,8},{16,116},{28,0},{24,124},{36... | collective-permute-start | bytes 1572872 | tf_op jit(solution)/shard_map/ppermute | solution.py:57
  29.4 12.0 %collective-permute-start.3 = (f32[1024,128]{1,0:T(8,128)}, f32[1024,128]{1,0:T(8,128)S(1)}, u32[]{:S(2)}, u32[]{:S(2)}) collective-permute-start(f32[1024,128]{1,0:T(8,128)} %get-tuple-element.42), channel_id=1, source_target_pairs={{4,0},{0,4},{12,8},{8,12},{20,16},{16,20},{28,24},{24,28},{36,32},... | collective-permute-start | bytes 1572872 | tf_op jit(solution)/shard_map/ppermute | solution.py:57
  41.5 1.0 copy-start
  49.4 16.8 %collective-permute-start.7 = (f32[4,256,128]{2,1,0:T(8,128)S(1)}, f32[4,256,128]{2,1,0:T(8,128)S(1)}, u32[]{:S(2)}, u32[]{:S(2)}) collective-permute-start(f32[4,256,128]{2,1,0:T(8,128)S(1)} %get-tuple-element.47), channel_id=1, source_target_pairs={{0,32},{4,12},{8,40},{12,4},{16,48},{20,28},{24,56},{28,20},{32,0}... | collective-permute-start | bytes 1572872 | tf_op jit(solution)/shard_map/ppermute | solution.py:49
  50.9 16.5 %collective-permute-start.8 = (f32[4,256,128]{2,1,0:T(8,128)S(1)}, f32[4,256,128]{2,1,0:T(8,128)S(1)}, u32[]{:S(2)}, u32[]{:S(2)}) collective-permute-start(f32[4,256,128]{2,1,0:T(8,128)S(1)} %get-tuple-element.48), channel_id=1, source_target_pairs={{0,64},{4,20},{8,72},{12,28},{16,80},{20,4},{24,88},{28,12},{32,96... | collective-permute-start | bytes 1572872 | tf_op jit(solution)/shard_map/ppermute | solution.py:49
  54.5 16.0 %collective-permute-start.9 = (f32[4,256,128]{2,1,0:T(8,128)S(1)}, f32[4,256,128]{2,1,0:T(8,128)S(1)}, u32[]{:S(2)}, u32[]{:S(2)}) collective-permute-start(f32[4,256,128]{2,1,0:T(8,128)S(1)} %get-tuple-element.49), channel_id=1, source_target_pairs={{0,96},{4,28},{8,104},{12,20},{16,112},{20,12},{24,120},{28,4},{32... | collective-permute-start | bytes 1572872 | tf_op jit(solution)/shard_map/ppermute | solution.py:49
  61.4 22.5 %collective-permute-start.10 = (f32[4,256,128]{2,1,0:T(8,128)S(1)}, f32[4,256,128]{2,1,0:T(8,128)S(1)}, u32[]{:S(2)}, u32[]{:S(2)}) collective-permute-start(f32[4,256,128]{2,1,0:T(8,128)S(1)} %get-tuple-element.51), channel_id=1, source_target_pairs={{0,32},{4,12},{8,40},{12,4},{16,48},{20,28},{24,56},{28,20},{32,0}... | collective-permute-start | bytes 1572872 | tf_op jit(solution)/shard_map/ppermute | solution.py:49
  61.5 24.0 %collective-permute-start.11 = (f32[4,256,128]{2,1,0:T(8,128)S(1)}, f32[4,256,128]{2,1,0:T(8,128)S(1)}, u32[]{:S(2)}, u32[]{:S(2)}) collective-permute-start(f32[4,256,128]{2,1,0:T(8,128)S(1)} %get-tuple-element.52), channel_id=1, source_target_pairs={{0,64},{4,20},{8,72},{12,28},{16,80},{20,4},{24,88},{28,12},{32,96... | collective-permute-start | bytes 1572872 | tf_op jit(solution)/shard_map/ppermute | solution.py:49
  66.2 19.3 %collective-permute-start.12 = (f32[4,256,128]{2,1,0:T(8,128)S(1)}, f32[4,256,128]{2,1,0:T(8,128)S(1)}, u32[]{:S(2)}, u32[]{:S(2)}) collective-permute-start(f32[4,256,128]{2,1,0:T(8,128)S(1)} %get-tuple-element.53), channel_id=1, source_target_pairs={{0,96},{4,28},{8,104},{12,20},{16,112},{20,12},{24,120},{28,4},{32... | collective-permute-start | bytes 1572872 | tf_op jit(solution)/shard_map/ppermute | solution.py:49
  81.5 15.0 %collective-permute-start.13 = (f32[4,256,128]{2,1,0:T(8,128)S(1)}, f32[4,256,128]{2,1,0:T(8,128)S(1)}, u32[]{:S(2)}, u32[]{:S(2)}) collective-permute-start(f32[4,256,128]{2,1,0:T(8,128)S(1)} %all_to_all.16.mine_zero.refs_0_), channel_id=1, source_target_pairs={{0,4},{4,0},{8,12},{12,8},{16,20},{20,16},{24,28},{28,24},{32,36},... | collective-permute-start | bytes 1572872 | tf_op jit(solution)/shard_map/ppermute | solution.py:53
  83.4 13.8 %collective-permute-start.14 = (f32[4,256,128]{2,1,0:T(8,128)S(1)}, f32[4,256,128]{2,1,0:T(8,128)S(1)}, u32[]{:S(2)}, u32[]{:S(2)}) collective-permute-start(f32[4,256,128]{2,1,0:T(8,128)S(1)} %all_to_all.16.mine_zero.refs_0_), channel_id=1, source_target_pairs={{0,1},{1,2},{2,3},{3,0},{4,5},{5,6},{6,7},{7,4},{8,9},{9,10},{10,1... | collective-permute-start | bytes 1572872 | tf_op jit(solution)/shard_map/ppermute | solution.py:61
  83.9 14.8 %collective-permute-start.15 = (f32[4,256,128]{2,1,0:T(8,128)S(1)}, f32[4,256,128]{2,1,0:T(8,128)S(1)}, u32[]{:S(2)}, u32[]{:S(2)}) collective-permute-start(f32[4,256,128]{2,1,0:T(8,128)S(1)} %all_to_all.16.mine_zero.refs_0_), channel_id=1, source_target_pairs={{0,3},{1,0},{2,1},{3,2},{4,7},{5,4},{6,5},{7,6},{8,11},{9,8},{10,9... | collective-permute-start | bytes 1572872 | tf_op jit(solution)/shard_map/ppermute | solution.py:61
  98.7 19.8 %collective-permute-start.16 = (f32[4,256,128]{2,1,0:T(8,128)S(1)}, f32[4,256,128]{2,1,0:T(8,128)S(1)}, u32[]{:S(2)}, u32[]{:S(2)}) collective-permute-start(f32[4,256,128]{2,1,0:T(8,128)S(1)} %all_to_all.17.mine_one.refs_6_), channel_id=1, source_target_pairs={{0,1},{1,2},{2,3},{3,0},{4,5},{5,6},{6,7},{7,4},{8,9},{9,10},{10,1... | collective-permute-start | bytes 1572872 | tf_op jit(solution)/shard_map/ppermute | solution.py:61
  99.0 19.5 %collective-permute-start.17 = (f32[4,256,128]{2,1,0:T(8,128)S(1)}, f32[4,256,128]{2,1,0:T(8,128)S(1)}, u32[]{:S(2)}, u32[]{:S(2)}) collective-permute-start(f32[4,256,128]{2,1,0:T(8,128)S(1)} %all_to_all.17.mine_one.refs_6_), channel_id=1, source_target_pairs={{0,3},{1,0},{2,1},{3,2},{4,7},{5,4},{6,5},{7,6},{8,11},{9,8},{10,9... | collective-permute-start | bytes 1572872 | tf_op jit(solution)/shard_map/ppermute | solution.py:61
  100.8 16.2 %collective-permute-start.18 = (f32[2,256,128]{2,1,0:T(8,128)S(1)}, f32[2,256,128]{2,1,0:T(8,128)S(1)}, u32[]{:S(2)}, u32[]{:S(2)}) collective-permute-start(f32[2,256,128]{2,1,0:T(8,128)S(1)} %slice.128), channel_id=1, source_target_pairs={{0,1},{1,2},{2,3},{3,0},{4,5},{5,6},{6,7},{7,4},{8,9},{9,10},{10,1... | collective-permute-start | bytes 786440 | tf_op jit(solution)/shard_map/ppermute | solution.py:61
  102.3 16.2 %collective-permute-start.19 = (f32[2,256,128]{2,1,0:T(8,128)S(1)}, f32[2,256,128]{2,1,0:T(8,128)S(1)}, u32[]{:S(2)}, u32[]{:S(2)}) collective-permute-start(f32[2,256,128]{2,1,0:T(8,128)S(1)} %slice.129), channel_id=1, source_target_pairs={{0,3},{1,0},{2,1},{3,2},{4,7},{5,4},{6,5},{7,6},{8,11},{9,8},{10,9... | collective-permute-start | bytes 786440 | tf_op jit(solution)/shard_map/ppermute | solution.py:61
  118.5 10.2 %collective-permute-start.20 = (f32[4,256,128]{2,1,0:T(8,128)S(1)}, f32[4,256,128]{2,1,0:T(8,128)S(1)}, u32[]{:S(2)}, u32[]{:S(2)}) collective-permute-start(f32[4,256,128]{2,1,0:T(8,128)S(1)} %all_to_all.17.mine_one.refs_6_), channel_id=1, source_target_pairs={{0,4},{4,0},{8,12},{12,8},{16,20},{20,16},{24,28},{28,24},{32,36},... | collective-permute-start | bytes 1572872 | tf_op jit(solution)/shard_map/ppermute | solution.py:53
  118.5 8.8 %collective-permute-start.21 = (f32[2,256,128]{2,1,0:T(8,128)S(1)}, f32[2,256,128]{2,1,0:T(8,128)S(1)}, u32[]{:S(2)}, u32[]{:S(2)}) collective-permute-start(f32[2,256,128]{2,1,0:T(8,128)S(1)} %slice.98), channel_id=1, source_target_pairs={{0,1},{1,2},{2,3},{3,0},{4,5},{5,6},{6,7},{7,4},{8,9},{9,10},{10,1... | collective-permute-start | bytes 786440 | tf_op jit(solution)/shard_map/ppermute | solution.py:61
  119.0 9.7 %collective-permute-start.22 = (f32[2,256,128]{2,1,0:T(8,128)S(1)}, f32[2,256,128]{2,1,0:T(8,128)S(1)}, u32[]{:S(2)}, u32[]{:S(2)}) collective-permute-start(f32[2,256,128]{2,1,0:T(8,128)S(1)} %slice.99), channel_id=1, source_target_pairs={{0,3},{1,0},{2,1},{3,2},{4,7},{5,4},{6,5},{7,6},{8,11},{9,8},{10,9... | collective-permute-start | bytes 786440 | tf_op jit(solution)/shard_map/ppermute | solution.py:61
  132.1 14.9 %collective-permute-start.23 = (f32[4,128,512]{2,1,0:T(8,128)S(1)}, f32[4,128,512]{2,1,0:T(8,128)S(1)}, u32[]{:S(2)}, u32[]{:S(2)}) collective-permute-start(f32[4,128,512]{2,1,0:T(8,128)S(1)} %get-tuple-element.59), channel_id=1, source_target_pairs={{0,8},{4,36},{8,0},{12,44},{16,24},{20,52},{24,16},{28,60},{32,40}... | collective-permute-start | bytes 3145736 | tf_op jit(solution)/shard_map/ppermute | solution.py:49
  134.1 14.8 %collective-permute-start.26 = (f32[4,128,512]{2,1,0:T(8,128)S(1)}, f32[4,128,512]{2,1,0:T(8,128)S(1)}, u32[]{:S(2)}, u32[]{:S(2)}) collective-permute-start(f32[4,128,512]{2,1,0:T(8,128)S(1)} %get-tuple-element.61), channel_id=1, source_target_pairs={{0,24},{4,100},{8,16},{12,108},{16,8},{20,116},{24,0},{28,124},{32... | collective-permute-start | bytes 3145736 | tf_op jit(solution)/shard_map/ppermute | solution.py:49
  137.6 20.6 %collective-permute-start.30 = (f32[4,128,512]{2,1,0:T(8,128)S(1)}, f32[4,128,512]{2,1,0:T(8,128)S(1)}, u32[]{:S(2)}, u32[]{:S(2)}) collective-permute-start(f32[4,128,512]{2,1,0:T(8,128)S(1)} %get-tuple-element.64), channel_id=1, source_target_pairs={{0,8},{4,36},{8,0},{12,44},{16,24},{20,52},{24,16},{28,60},{32,40}... | collective-permute-start | bytes 3145736 | tf_op jit(solution)/shard_map/ppermute | solution.py:49
  138.7 21.4 %collective-permute-start.33 = (f32[4,128,512]{2,1,0:T(8,128)S(1)}, f32[4,128,512]{2,1,0:T(8,128)S(1)}, u32[]{:S(2)}, u32[]{:S(2)}) collective-permute-start(f32[4,128,512]{2,1,0:T(8,128)S(1)} %get-tuple-element.66), channel_id=1, source_target_pairs={{0,24},{4,100},{8,16},{12,108},{16,8},{20,116},{24,0},{28,124},{32... | collective-permute-start | bytes 3145736 | tf_op jit(solution)/shard_map/ppermute | solution.py:49
  147.1 18.7 %collective-permute-start.24 = (f32[2,128,512]{2,1,0:T(8,128)S(1)}, f32[2,128,512]{2,1,0:T(8,128)S(1)}, u32[]{:S(2)}, u32[]{:S(2)}) collective-permute-start(f32[2,128,512]{2,1,0:T(8,128)S(1)} %slice_add_fusion.3), channel_id=1, source_target_pairs={{0,24},{4,100},{8,16},{12,108},{16,8},{20,116},{24,0},{28,124},{32... | collective-permute-start | bytes 1572872 | tf_op jit(solution)/shard_map/ppermute | solution.py:49
  149.0 16.8 %collective-permute-start.27 = (f32[2,128,512]{2,1,0:T(8,128)S(1)}, f32[2,128,512]{2,1,0:T(8,128)S(1)}, u32[]{:S(2)}, u32[]{:S(2)}) collective-permute-start(f32[2,128,512]{2,1,0:T(8,128)S(1)} %slice_add_fusion.2), channel_id=1, source_target_pairs={{0,8},{4,36},{8,0},{12,44},{16,24},{20,52},{24,16},{28,60},{32,40}... | collective-permute-start | bytes 1572872 | tf_op jit(solution)/shard_map/ppermute | solution.py:49
  158.3 18.9 %collective-permute-start.31 = (f32[2,128,512]{2,1,0:T(8,128)S(1)}, f32[2,128,512]{2,1,0:T(8,128)S(1)}, u32[]{:S(2)}, u32[]{:S(2)}) collective-permute-start(f32[2,128,512]{2,1,0:T(8,128)S(1)} %slice_add_fusion.1), channel_id=1, source_target_pairs={{0,24},{4,100},{8,16},{12,108},{16,8},{20,116},{24,0},{28,124},{32... | collective-permute-start | bytes 1572872 | tf_op jit(solution)/shard_map/ppermute | solution.py:49
  160.2 17.0 %collective-permute-start.34 = (f32[2,128,512]{2,1,0:T(8,128)S(1)}, f32[2,128,512]{2,1,0:T(8,128)S(1)}, u32[]{:S(2)}, u32[]{:S(2)}) collective-permute-start(f32[2,128,512]{2,1,0:T(8,128)S(1)} %slice_add_fusion), channel_id=1, source_target_pairs={{0,8},{4,36},{8,0},{12,44},{16,24},{20,52},{24,16},{28,60},{32,40}... | collective-permute-start | bytes 1572872 | tf_op jit(solution)/shard_map/ppermute | solution.py:49
  166.0 12.8 %collective-permute-start.25 = (f32[128,512]{1,0:T(8,128)S(1)}, f32[128,512]{1,0:T(8,128)S(1)}, u32[]{:S(2)}, u32[]{:S(2)}) collective-permute-start(f32[128,512]{1,0:T(8,128)S(1)} %get-tuple-element.72), channel_id=1, source_target_pairs={{0,32},{4,12},{8,40},{12,4},{16,48},{20,28},{24,56},{28,20},{32,0}... | collective-permute-start | bytes 786440 | tf_op jit(solution)/shard_map/ppermute | solution.py:49
  166.1 16.2 %collective-permute-start.28 = (f32[128,512]{1,0:T(8,128)S(1)}, f32[128,512]{1,0:T(8,128)S(1)}, u32[]{:S(2)}, u32[]{:S(2)}) collective-permute-start(f32[128,512]{1,0:T(8,128)S(1)} %get-tuple-element.69), channel_id=1, source_target_pairs={{0,64},{4,20},{8,72},{12,28},{16,80},{20,4},{24,88},{28,12},{32,96... | collective-permute-start | bytes 786440 | tf_op jit(solution)/shard_map/ppermute | solution.py:49
  167.5 14.7 %collective-permute-start.29 = (f32[128,512]{1,0:T(8,128)S(1)}, f32[128,512]{1,0:T(8,128)S(1)}, u32[]{:S(2)}, u32[]{:S(2)}) collective-permute-start(f32[128,512]{1,0:T(8,128)S(1)} %get-tuple-element.68), channel_id=1, source_target_pairs={{0,96},{4,28},{8,104},{12,20},{16,112},{20,12},{24,120},{28,4},{32... | collective-permute-start | bytes 786440 | tf_op jit(solution)/shard_map/ppermute | solution.py:49
  177.5 6.5 %collective-permute-start.32 = (f32[128,512]{1,0:T(8,128)S(1)}, f32[128,512]{1,0:T(8,128)S(1)}, u32[]{:S(2)}, u32[]{:S(2)}) collective-permute-start(f32[128,512]{1,0:T(8,128)S(1)} %get-tuple-element.73), channel_id=1, source_target_pairs={{0,32},{4,12},{8,40},{12,4},{16,48},{20,28},{24,56},{28,20},{32,0}... | collective-permute-start | bytes 786440 | tf_op jit(solution)/shard_map/ppermute | solution.py:49
  177.6 8.4 %collective-permute-start.35 = (f32[128,512]{1,0:T(8,128)S(1)}, f32[128,512]{1,0:T(8,128)S(1)}, u32[]{:S(2)}, u32[]{:S(2)}) collective-permute-start(f32[128,512]{1,0:T(8,128)S(1)} %get-tuple-element.71), channel_id=1, source_target_pairs={{0,64},{4,20},{8,72},{12,28},{16,80},{20,4},{24,88},{28,12},{32,96... | collective-permute-start | bytes 786440 | tf_op jit(solution)/shard_map/ppermute | solution.py:49
  178.7 10.0 %collective-permute-start.36 = (f32[128,512]{1,0:T(8,128)S(1)}, f32[128,512]{1,0:T(8,128)S(1)}, u32[]{:S(2)}, u32[]{:S(2)}) collective-permute-start(f32[128,512]{1,0:T(8,128)S(1)} %get-tuple-element.70), channel_id=1, source_target_pairs={{0,96},{4,28},{8,104},{12,20},{16,112},{20,12},{24,120},{28,4},{32... | collective-permute-start | bytes 786440 | tf_op jit(solution)/shard_map/ppermute | solution.py:49

commit v6 on v5

--- a/solution.py
+++ b/solution.py
@@ -30,6 +30,11 @@
 
 FIRST, SECOND = 0, 1
 CUTS = (0, 512, 1024)
+
+
+def ring_places(index):
+    z, y, core = index // 8, index // 2 % 4, index % 2
+    return core, jnp.where(core == 0, y, z), jnp.where(core == 0, z, y)
 
 
 def groups(ring):
@@ -108,7 +113,8 @@
     )
 
 
-def local_kernel(where_ref, table_ref, signs_ref, design_ref, *refs):
+def local_kernel(table_ref, signs_ref, design_ref, *refs):
+    core, first, second = ring_places(lax.axis_index("row"))
     outs, (taken_ref, parts_ref, held_ref, in_sems, sems) = refs[:-5], refs[-5:]
     size = table_ref.shape[0]
     count = design_ref.shape[0] // size
@@ -125,7 +131,7 @@
         parts_ref[number] = part + jnp.dot(signed_table, low, preferred_element_type=jnp.float32)
     copies = []
     for k in range(SIDE):
-        blocks = (2 * (where_ref[1] ^ k) + where_ref[0], 2 * (where_ref[2] ^ k) + 1 - where_ref[0])
+        blocks = (2 * (first ^ k) + core, 2 * (second ^ k) + 1 - core)
         for side, block in enumerate(blocks):
             lanes = pl.ds(pl.multiple_of(block * LANE, LANE), LANE)
             parts = butterfly([parts_ref[number, :, lanes] for number in range(count)])
@@ -137,7 +143,7 @@
         copy.wait()
 
 
-def local_transform(where, design, signs, table):
+def local_transform(design, signs, table):
     rows, width = design.shape
     size = table.shape[0]
     count = rows // size
@@ -145,7 +151,6 @@
         local_kernel,
         (),
         [
-            pl.BlockSpec(memory_space=pltpu.SMEM),
             pl.BlockSpec(memory_space=pltpu.VMEM),
             pl.BlockSpec(memory_space=pltpu.VMEM),
             pl.BlockSpec(memory_space=pl.ANY),
@@ -162,7 +167,7 @@
         flops=2**30,
         moved=2**23,
         vmem=60 * 2**20,
-    )(where, table, signs, design)
+    )(table, signs, design)
 
 
 def sample_kernel(scale, chunk, owned, where_ref, index_ref, *refs):
@@ -350,7 +355,7 @@
     scale = float(np.float32(1.0) / np.sqrt(np.float32(total)))
 
     table = jnp.asarray(hadamard(256), jnp.bfloat16)
-    pieces = local_transform(where, design, signs[None, :], table)
+    pieces = local_transform(design, signs[None, :], table)
     own, theirs = pieces[:SIDE], list(pieces[SIDE:])
     sample_rows, _ = lax.optimization_barrier((sample_rows, own[0]))
     index = sample_index(sample_rows, z, y, core)

time: 190 us -> 189 us (level)
  no operation moved by 1% of the time
where the time goes in v6:
time: 189 us
  waiting for transfers between devices  71.9 us (38%)
  starting transfers between devices  55.9 us (30%)
  Pallas kernels  34.5 us (18%)
  blocking collectives  21.8 us (12%)
  other arithmetic  2.35 us (1%)
    ppermute x23, starting transfers between devices, hop(): return lax.ppermute(value, 'row', partners(ring, step))  33 us
    ppermute x23, waiting for transfers between devices, hop(): return lax.ppermute(value, 'row', partners(ring, step))  30.4 us
    ppermute x8, waiting for transfers between devices, around(): lax.ppermute(value, 'col', [(i, (i + step) % SIDE) for i in range(SIDE)])  25.7 us
    all_to_all x2, blocking collectives, exchange(): lax.all_to_all(value, 'row', 0, 0, tiled=True, axis_index_groups=groups(r...  21.8 us
    pallas_call x2, Pallas kernels, sampled_rows(): call(functools.partial(sample_kernel, scale, chunk, owned), (), [pl.Block...  13.9 us
    pallas_call x3, Pallas kernels, gram_shares(): call(functools.partial(gram_kernel, plan, halves), (), [pl.BlockSpec(memo...  12.8 us
    ppermute x4, waiting for transfers between devices, across(): lax.ppermute(value, 'row', [(i ^ 1, j) for i, j in partners(FIRST, step)])  11.5 us
    ppermute x8, starting transfers between devices, around(): lax.ppermute(value, 'col', [(i, (i + step) % SIDE) for i in range(SIDE)])  8.41 us
  transfers between devices with their start and end apart: 38, of which 20 were waited for; matrix products, arithmetic and copies ran while one was open for 1% of the time, Pallas kernels for 9%

profile of v6, /device:TPU:14, one launch (start us, length us, event | category | flops | bytes accessed | tf_op | source)
XLA Modules:
  0.0 189.0 jit_solution(9625010616653723413)
XLA Ops:
  0.6 6.3 %shard_map.59 = (f32[1024,128]{1,0:T(8,128)}, f32[1024,128]{1,0:T(8,128)}, f32[1024,128]{1,0:T(8,128)}, f32[1024,128]{1,0:T(8,128)}, f32[1024,128]{1,0:T(8,128)}...) custom-call(bf16[256,256]{1,0:T(8,128)(2,1)} %constant.110.clone.table_ref, s32[1,1024]{1,0:T(1,128)} %bitcast.31, ...), custom_call_target="tpu_custom_call" | custom-call | flops 1073741824 | bytes 8388608 | tf_op jit(solution)/shard_map/pallas_call | solution.py:150
  7.0 0.5 collective-permute-start
  7.5 2.6 %collective-permute-start.1 = (f32[1024,128]{1,0:T(8,128)}, f32[1024,128]{1,0:T(8,128)S(1)}, u32[]{:S(2)}, u32[]{:S(2)}) collective-permute-start(f32[1024,128]{1,0:T(8,128)} %get-tuple-element.40), channel_id=1, source_target_pairs={{0,16},{4,68},{8,24},{12,76},{16,0},{20,84},{24,8},{28,92},{32,48}... | collective-permute-start | bytes 1572872 | tf_op jit(solution)/shard_map/ppermute | solution.py:54
  10.1 0.6 broadcast_in_dim.7
  10.7 7.4 %all-to-all-start = ((s32[32,1,256]{2,1,0:T(1,128)}), s32[32,1,256]{2,1,0:T(1,128)S(1)}, u32[]{:S(2)}, u32[]{:S(2)}) async-start(s32[32,1,256]{2,1,0:T(1,128)} %broadcast_in_dim.7), calls=%async_computation | async-start | bytes 65536 | tf_op jit(solution)/shard_map/all_to_all | solution.py:336
  18.1 1.5 collective-permute-start.2
  19.7 0.9 collective-permute-start.4
  20.6 3.5 %collective-permute-start.5 = (f32[1024,128]{1,0:T(8,128)}, f32[1024,128]{1,0:T(8,128)S(1)}, u32[]{:S(2)}, u32[]{:S(2)}) collective-permute-start(f32[1024,128]{1,0:T(8,128)} %get-tuple-element.44), channel_id=1, source_target_pairs={{4,16},{0,68},{12,24},{8,76},{20,0},{16,84},{28,8},{24,92},{36,48}... | collective-permute-start | bytes 1572872 | tf_op jit(solution)/shard_map/ppermute | solution.py:62
  24.2 4.2 %all-to-all-done = s32[32,1,256]{2,1,0:T(1,128)S(1)} async-done(((s32[32,1,256]{2,1,0:T(1,128)}), s32[32,1,256]{2,1,0:T(1,128)S(1)}, u32[]{:S(2)}, u32[]{:S(2)}) %all-to-all-start) | async-done | bytes 32800 | tf_op jit(solution)/shard_map/all_to_all | solution.py:336
  28.8 0.4 collective-permute-start.3
  29.3 6.0 %collective-permute-done.5.refs_6_ = f32[1024,128]{1,0:T(8,128)S(1)} collective-permute-done((f32[1024,128]{1,0:T(8,128)}, f32[1024,128]{1,0:T(8,128)S(1)}, u32[]{:S(2)}, u32[]{:S(2)}) %collective-permute-start.5) | collective-permute-done | bytes 524320 | tf_op jit(solution)/shard_map/ppermute | solution.py:62
  35.3 5.5 %collective-permute-done.6.refs_7_ = f32[1024,128]{1,0:T(8,128)S(1)} collective-permute-done((f32[1024,128]{1,0:T(8,128)}, f32[1024,128]{1,0:T(8,128)S(1)}, u32[]{:S(2)}, u32[]{:S(2)}) %collective-permute-start.6) | collective-permute-done | bytes 524320 | tf_op jit(solution)/shard_map/ppermute | solution.py:62
  40.8 1.0 copy-done
  41.9 6.9 %shard_map.60 = (f32[4,256,128]{2,1,0:T(8,128)S(1)}, f32[4,256,128]{2,1,0:T(8,128)S(1)}, f32[4,256,128]{2,1,0:T(8,128)S(1)}, f32[4,256,128]{2,1,0:T(8,128)S(1)}) custom-call(s32[4]{0:T(128)S(1)} %pad_add_fusion.where_ref, s32[8192]{0:T(1024)S(1)} %fusion.13.index_ref, f32[1024,128]{1,0:T(8,128)S(1)} %copy-done, ...), custom_call_target="tpu_custom_call" | custom-call | flops 16777216 | bytes 8388608 | tf_op jit(solution)/shard_map/pallas_call | solution.py:215
  48.8 1.4 collective-permute-start.7
  50.2 3.6 %collective-permute-start.8 = (f32[4,256,128]{2,1,0:T(8,128)S(1)}, f32[4,256,128]{2,1,0:T(8,128)S(1)}, u32[]{:S(2)}, u32[]{:S(2)}) collective-permute-start(f32[4,256,128]{2,1,0:T(8,128)S(1)} %get-tuple-element.48), channel_id=1, source_target_pairs={{0,64},{4,20},{8,72},{12,28},{16,80},{20,4},{24,88},{28,12},{32,96... | collective-permute-start | bytes 1572872 | tf_op jit(solution)/shard_map/ppermute | solution.py:54
  53.8 6.9 %shard_map.61 = (f32[4,256,128]{2,1,0:T(8,128)S(1)}, f32[4,256,128]{2,1,0:T(8,128)S(1)}, f32[4,256,128]{2,1,0:T(8,128)S(1)}, f32[4,256,128]{2,1,0:T(8,128)S(1)}) custom-call(s32[4]{0:T(128)S(1)} %pad_add_fusion.where_ref, s32[8192]{0:T(1024)S(1)} %fusion.13.index_ref, f32[1024,128]{1,0:T(8,128)S(1)} %copy-done, ...), custom_call_target="tpu_custom_call" | custom-call | flops 16777216 | bytes 8388608 | tf_op jit(solution)/shard_map/pallas_call | solution.py:215
  60.9 4.7 %collective-permute-start.11 = (f32[4,256,128]{2,1,0:T(8,128)S(1)}, f32[4,256,128]{2,1,0:T(8,128)S(1)}, u32[]{:S(2)}, u32[]{:S(2)}) collective-permute-start(f32[4,256,128]{2,1,0:T(8,128)S(1)} %get-tuple-element.52), channel_id=1, source_target_pairs={{0,64},{4,20},{8,72},{12,28},{16,80},{20,4},{24,88},{28,12},{32,96... | collective-permute-start | bytes 1572872 | tf_op jit(solution)/shard_map/ppermute | solution.py:54
  65.5 1.1 collective-permute-done.8
  66.7 3.1 %collective-permute-done.9 = f32[4,256,128]{2,1,0:T(8,128)S(1)} collective-permute-done((f32[4,256,128]{2,1,0:T(8,128)S(1)}, f32[4,256,128]{2,1,0:T(8,128)S(1)}, u32[]{:S(2)}, u32[]{:S(2)}) %collective-permute-start.9) | collective-permute-done | bytes 524320 | tf_op jit(solution)/shard_map/ppermute | solution.py:54
  69.9 10.9 %all_to_all.16.mine_zero.refs_0_ = f32[4,256,128]{2,1,0:T(8,128)S(1)} all-to-all(f32[4,256,128]{2,1,0:T(8,128)S(1)} %add_add_fusion.1), channel_id=1, replica_groups={{0,8,16,24},{4,36,68,100},{32,40,48,56},{12,44,76,108},{64,72,80,88},{2..., dimensions={0} | all-to-all | bytes 1048576 | tf_op jit(solution)/shard_map/all_to_all | solution.py:50
  80.8 2.0 %collective-permute-start.13 = (f32[4,256,128]{2,1,0:T(8,128)S(1)}, f32[4,256,128]{2,1,0:T(8,128)S(1)}, u32[]{:S(2)}, u32[]{:S(2)}) collective-permute-start(f32[4,256,128]{2,1,0:T(8,128)S(1)} %all_to_all.16.mine_zero.refs_0_), channel_id=1, source_target_pairs={{0,4},{4,0},{8,12},{12,8},{16,20},{20,16},{24,28},{28,24},{32,36},... | collective-permute-start | bytes 1572872 | tf_op jit(solution)/shard_map/ppermute | solution.py:58
  82.8 0.5 collective-permute-start.14
  83.3 1.5 collective-permute-start.15
  85.0 10.9 %all_to_all.17.mine_one.refs_6_ = f32[4,256,128]{2,1,0:T(8,128)S(1)} all-to-all(f32[4,256,128]{2,1,0:T(8,128)S(1)} %add_add_fusion), channel_id=1, replica_groups={{0,8,16,24},{4,36,68,100},{32,40,48,56},{12,44,76,108},{64,72,80,88},{2..., dimensions={0} | all-to-all | bytes 1048576 | tf_op jit(solution)/shard_map/all_to_all | solution.py:50
  95.9 0.8 collective-permute-done.14.refs_2_
  96.6 1.4 collective-permute-done.15.refs_3_
  98.1 0.3 collective-permute-start.16
  98.3 1.8 collective-permute-start.17
  100.1 1.5 collective-permute-start.18
  101.7 0.6 collective-permute-start.19
  102.3 14.0 %collective-permute-done.18.refs_4_ = f32[2,256,128]{2,1,0:T(8,128)S(1)} collective-permute-done((f32[2,256,128]{2,1,0:T(8,128)S(1)}, f32[2,256,128]{2,1,0:T(8,128)S(1)}, u32[]{:S(2)}, u32[]{:S(2)}) %collective-permute-start.18) | collective-permute-done | bytes 262176 | tf_op jit(solution)/shard_map/ppermute | solution.py:66
  116.3 1.5 collective-permute-done.19.refs_5_
  117.9 0.4 collective-permute-start.21
  118.4 1.7 collective-permute-start.22
  120.1 6.6 %collective-permute-done.21.refs_10_ = f32[2,256,128]{2,1,0:T(8,128)S(1)} collective-permute-done((f32[2,256,128]{2,1,0:T(8,128)S(1)}, f32[2,256,128]{2,1,0:T(8,128)S(1)}, u32[]{:S(2)}, u32[]{:S(2)}) %collective-permute-start.21) | collective-permute-done | bytes 262176 | tf_op jit(solution)/shard_map/ppermute | solution.py:66
  126.7 1.4 collective-permute-done.22.refs_11_
  128.1 3.4 %shard_map.64 = (f32[4,128,512]{2,1,0:T(8,128)S(1)}, f32[4,128,512]{2,1,0:T(8,128)S(1)}) custom-call(s32[4]{0:T(128)S(1)} %pad_add_fusion.where_ref, f32[4,256,128]{2,1,0:T(8,128)S(1)} %all_to_all.16.mine_zero.refs_0_, f32[4,256,128]{2,1,0:T(8,128)S(1)} %collective-permute-done.13.sibling_zero.refs_1_, f32[4,256,128]{2,1,0:T(8,128)S(1)} %collective-permute-done.14.refs_2_, ...), custom_call_target="tpu_custom_call" | custom-call | flops 3221225472 | bytes 8388608 | tf_op jit(solution)/shard_map/pallas_call | solution.py:316
  131.5 2.0 %collective-permute-start.23 = (f32[4,128,512]{2,1,0:T(8,128)S(1)}, f32[4,128,512]{2,1,0:T(8,128)S(1)}, u32[]{:S(2)}, u32[]{:S(2)}) collective-permute-start(f32[4,128,512]{2,1,0:T(8,128)S(1)} %get-tuple-element.59), channel_id=1, source_target_pairs={{0,8},{4,36},{8,0},{12,44},{16,24},{20,52},{24,16},{28,60},{32,40}... | collective-permute-start | bytes 3145736 | tf_op jit(solution)/shard_map/ppermute | solution.py:54
  133.6 3.4 %shard_map.65 = (f32[4,128,512]{2,1,0:T(8,128)S(1)}, f32[4,128,512]{2,1,0:T(8,128)S(1)}) custom-call(s32[4]{0:T(128)S(1)} %pad_add_fusion.where_ref, f32[4,256,128]{2,1,0:T(8,128)S(1)} %all_to_all.16.mine_zero.refs_0_, f32[4,256,128]{2,1,0:T(8,128)S(1)} %collective-permute-done.13.sibling_zero.refs_1_, f32[4,256,128]{2,1,0:T(8,128)S(1)} %collective-permute-done.14.refs_2_, ...), custom_call_target="tpu_custom_call" | custom-call | flops 3221225472 | bytes 8388608 | tf_op jit(solution)/shard_map/pallas_call | solution.py:316
  137.0 1.1 collective-permute-start.30
  138.1 1.6 collective-permute-start.33
  139.7 6.0 %shard_map.63 = (f32[2,128,512]{2,1,0:T(8,128)S(1)}, f32[2,128,512]{2,1,0:T(8,128)S(1)}, f32[2,128,512]{2,1,0:T(8,128)S(1)}, f32[2,128,512]{2,1,0:T(8,128)S(1)},...) custom-call(s32[4]{0:T(128)S(1)} %pad_add_fusion.where_ref, f32[4,256,128]{2,1,0:T(8,128)S(1)} %all_to_all.16.mine_zero.refs_0_, ...), custom_call_target="tpu_custom_call" | custom-call | flops 3221225472 | bytes 8388608 | tf_op jit(solution)/shard_map/pallas_call | solution.py:316
  145.7 0.7 collective-permute-done.23
  146.4 0.5 collective-permute-start.24
  147.0 1.3 collective-permute-done.26
  148.3 1.6 collective-permute-start.27
  150.0 7.6 %collective-permute-done.30 = f32[4,128,512]{2,1,0:T(8,128)S(1)} collective-permute-done((f32[4,128,512]{2,1,0:T(8,128)S(1)}, f32[4,128,512]{2,1,0:T(8,128)S(1)}, u32[]{:S(2)}, u32[]{:S(2)}) %collective-permute-start.30) | collective-permute-done | bytes 1048608 | tf_op jit(solution)/shard_map/ppermute | solution.py:54
  157.7 0.5 collective-permute-start.31
  158.2 1.3 collective-permute-done.33
  159.6 1.4 collective-permute-start.34
  161.0 1.6 shard_map.62
  162.6 2.5 %collective-permute-done.24 = f32[2,128,512]{2,1,0:T(8,128)S(1)} collective-permute-done((f32[2,128,512]{2,1,0:T(8,128)S(1)}, f32[2,128,512]{2,1,0:T(8,128)S(1)}, u32[]{:S(2)}, u32[]{:S(2)}) %collective-permute-start.24) | collective-permute-done | bytes 524320 | tf_op jit(solution)/shard_map/ppermute | solution.py:54
  165.1 0.2 fusion.6
  165.4 1.5 collective-permute-start.28
  166.9 3.2 %collective-permute-start.29 = (f32[128,512]{1,0:T(8,128)S(1)}, f32[128,512]{1,0:T(8,128)S(1)}, u32[]{:S(2)}, u32[]{:S(2)}) collective-permute-start(f32[128,512]{1,0:T(8,128)S(1)} %get-tuple-element.68), channel_id=1, source_target_pairs={{0,96},{4,28},{8,104},{12,20},{16,112},{20,12},{24,120},{28,4},{32... | collective-permute-start | bytes 786440 | tf_op jit(solution)/shard_map/ppermute | solution.py:54
  170.1 6.4 %collective-permute-done.31 = f32[2,128,512]{2,1,0:T(8,128)S(1)} collective-permute-done((f32[2,128,512]{2,1,0:T(8,128)S(1)}, f32[2,128,512]{2,1,0:T(8,128)S(1)}, u32[]{:S(2)}, u32[]{:S(2)}) %collective-permute-start.31) | collective-permute-done | bytes 524320 | tf_op jit(solution)/shard_map/ppermute | solution.py:54
  176.6 0.2 fusion
  176.9 1.2 collective-permute-start.35
  178.1 3.5 %collective-permute-start.36 = (f32[128,512]{1,0:T(8,128)S(1)}, f32[128,512]{1,0:T(8,128)S(1)}, u32[]{:S(2)}, u32[]{:S(2)}) collective-permute-start(f32[128,512]{1,0:T(8,128)S(1)} %get-tuple-element.70), channel_id=1, source_target_pairs={{0,96},{4,28},{8,104},{12,20},{16,112},{20,12},{24,120},{28,4},{32... | collective-permute-start | bytes 786440 | tf_op jit(solution)/shard_map/ppermute | solution.py:54
  181.8 1.5 collective-permute-done.32
  183.3 2.1 %collective-permute-done.35 = f32[128,512]{1,0:T(8,128)S(1)} collective-permute-done((f32[128,512]{1,0:T(8,128)S(1)}, f32[128,512]{1,0:T(8,128)S(1)}, u32[]{:S(2)}, u32[]{:S(2)}) %collective-permute-start.35) | collective-permute-done | bytes 262176 | tf_op jit(solution)/shard_map/ppermute | solution.py:54
  185.4 2.7 %collective-permute-done.36 = f32[128,512]{1,0:T(8,128)S(1)} collective-permute-done((f32[128,512]{1,0:T(8,128)S(1)}, f32[128,512]{1,0:T(8,128)S(1)}, u32[]{:S(2)}, u32[]{:S(2)}) %collective-permute-start.36) | collective-permute-done | bytes 262176 | tf_op jit(solution)/shard_map/ppermute | solution.py:54
  188.2 0.8 pad_maximum_fusion
  (43 shorter events, 1.8 us)
Async XLA Ops:
  0.6 9.5 %copy-start.1 = (s32[256]{0:T(256)S(1)}, s32[256]{0:T(256)}, u32[]{:S(2)}) copy-start(s32[256]{0:T(256)} %param.6) | copy-start | bytes 3076
  7.0 21.6 %collective-permute-start = (f32[1024,128]{1,0:T(8,128)}, f32[1024,128]{1,0:T(8,128)S(1)}, u32[]{:S(2)}, u32[]{:S(2)}) collective-permute-start(f32[1024,128]{1,0:T(8,128)} %get-tuple-element.39), channel_id=1, source_target_pairs={{0,8},{4,36},{8,0},{12,44},{16,24},{20,52},{24,16},{28,60},{32,40}... | collective-permute-start | bytes 1572872 | tf_op jit(solution)/shard_map/ppermute | solution.py:54
  7.5 21.3 %collective-permute-start.1 = (f32[1024,128]{1,0:T(8,128)}, f32[1024,128]{1,0:T(8,128)S(1)}, u32[]{:S(2)}, u32[]{:S(2)}) collective-permute-start(f32[1024,128]{1,0:T(8,128)} %get-tuple-element.40), channel_id=1, source_target_pairs={{0,16},{4,68},{8,24},{12,76},{16,0},{20,84},{24,8},{28,92},{32,48}... | collective-permute-start | bytes 1572872 | tf_op jit(solution)/shard_map/ppermute | solution.py:54
  10.7 17.7 %all-to-all-start = ((s32[32,1,256]{2,1,0:T(1,128)}), s32[32,1,256]{2,1,0:T(1,128)S(1)}, u32[]{:S(2)}, u32[]{:S(2)}) async-start(s32[32,1,256]{2,1,0:T(1,128)} %broadcast_in_dim.7), calls=%async_computation | async-start | bytes 65536 | tf_op jit(solution)/shard_map/all_to_all | solution.py:336
  18.1 11.2 %collective-permute-start.2 = (f32[1024,128]{1,0:T(8,128)}, f32[1024,128]{1,0:T(8,128)S(1)}, u32[]{:S(2)}, u32[]{:S(2)}) collective-permute-start(f32[1024,128]{1,0:T(8,128)} %get-tuple-element.41), channel_id=1, source_target_pairs={{0,24},{4,100},{8,16},{12,108},{16,8},{20,116},{24,0},{28,124},{32... | collective-permute-start | bytes 1572872 | tf_op jit(solution)/shard_map/ppermute | solution.py:54
  19.7 9.6 %collective-permute-start.4 = (f32[1024,128]{1,0:T(8,128)}, f32[1024,128]{1,0:T(8,128)S(1)}, u32[]{:S(2)}, u32[]{:S(2)}) collective-permute-start(f32[1024,128]{1,0:T(8,128)} %get-tuple-element.43), channel_id=1, source_target_pairs={{4,8},{0,36},{12,0},{8,44},{20,24},{16,52},{28,16},{24,60},{36,40}... | collective-permute-start | bytes 1572872 | tf_op jit(solution)/shard_map/ppermute | solution.py:62
  20.6 14.7 %collective-permute-start.5 = (f32[1024,128]{1,0:T(8,128)}, f32[1024,128]{1,0:T(8,128)S(1)}, u32[]{:S(2)}, u32[]{:S(2)}) collective-permute-start(f32[1024,128]{1,0:T(8,128)} %get-tuple-element.44), channel_id=1, source_target_pairs={{4,16},{0,68},{12,24},{8,76},{20,0},{16,84},{28,8},{24,92},{36,48}... | collective-permute-start | bytes 1572872 | tf_op jit(solution)/shard_map/ppermute | solution.py:62
  28.5 12.3 %collective-permute-start.6 = (f32[1024,128]{1,0:T(8,128)}, f32[1024,128]{1,0:T(8,128)S(1)}, u32[]{:S(2)}, u32[]{:S(2)}) collective-permute-start(f32[1024,128]{1,0:T(8,128)} %get-tuple-element.45), channel_id=1, source_target_pairs={{4,24},{0,100},{12,16},{8,108},{20,8},{16,116},{28,0},{24,124},{36... | collective-permute-start | bytes 1572872 | tf_op jit(solution)/shard_map/ppermute | solution.py:62
  28.8 12.0 %collective-permute-start.3 = (f32[1024,128]{1,0:T(8,128)}, f32[1024,128]{1,0:T(8,128)}, u32[]{:S(2)}, u32[]{:S(2)}) collective-permute-start(f32[1024,128]{1,0:T(8,128)} %get-tuple-element.42), channel_id=1, source_target_pairs={{4,0},{0,4},{12,8},{8,12},{20,16},{16,20},{28,24},{24,28},{36,32},... | collective-permute-start | bytes 1572872 | tf_op jit(solution)/shard_map/ppermute | solution.py:62
  40.8 1.0 copy-start
  48.8 16.7 %collective-permute-start.7 = (f32[4,256,128]{2,1,0:T(8,128)S(1)}, f32[4,256,128]{2,1,0:T(8,128)S(1)}, u32[]{:S(2)}, u32[]{:S(2)}) collective-permute-start(f32[4,256,128]{2,1,0:T(8,128)S(1)} %get-tuple-element.47), channel_id=1, source_target_pairs={{0,32},{4,12},{8,40},{12,4},{16,48},{20,28},{24,56},{28,20},{32,0}... | collective-permute-start | bytes 1572872 | tf_op jit(solution)/shard_map/ppermute | solution.py:54
  50.2 16.5 %collective-permute-start.8 = (f32[4,256,128]{2,1,0:T(8,128)S(1)}, f32[4,256,128]{2,1,0:T(8,128)S(1)}, u32[]{:S(2)}, u32[]{:S(2)}) collective-permute-start(f32[4,256,128]{2,1,0:T(8,128)S(1)} %get-tuple-element.48), channel_id=1, source_target_pairs={{0,64},{4,20},{8,72},{12,28},{16,80},{20,4},{24,88},{28,12},{32,96... | collective-permute-start | bytes 1572872 | tf_op jit(solution)/shard_map/ppermute | solution.py:54
  53.8 16.0 %collective-permute-start.9 = (f32[4,256,128]{2,1,0:T(8,128)S(1)}, f32[4,256,128]{2,1,0:T(8,128)S(1)}, u32[]{:S(2)}, u32[]{:S(2)}) collective-permute-start(f32[4,256,128]{2,1,0:T(8,128)S(1)} %get-tuple-element.49), channel_id=1, source_target_pairs={{0,96},{4,28},{8,104},{12,20},{16,112},{20,12},{24,120},{28,4},{32... | collective-permute-start | bytes 1572872 | tf_op jit(solution)/shard_map/ppermute | solution.py:54
  60.8 22.5 %collective-permute-start.10 = (f32[4,256,128]{2,1,0:T(8,128)S(1)}, f32[4,256,128]{2,1,0:T(8,128)S(1)}, u32[]{:S(2)}, u32[]{:S(2)}) collective-permute-start(f32[4,256,128]{2,1,0:T(8,128)S(1)} %get-tuple-element.51), channel_id=1, source_target_pairs={{0,32},{4,12},{8,40},{12,4},{16,48},{20,28},{24,56},{28,20},{32,0}... | collective-permute-start | bytes 1572872 | tf_op jit(solution)/shard_map/ppermute | solution.py:54
  60.9 24.0 %collective-permute-start.11 = (f32[4,256,128]{2,1,0:T(8,128)S(1)}, f32[4,256,128]{2,1,0:T(8,128)S(1)}, u32[]{:S(2)}, u32[]{:S(2)}) collective-permute-start(f32[4,256,128]{2,1,0:T(8,128)S(1)} %get-tuple-element.52), channel_id=1, source_target_pairs={{0,64},{4,20},{8,72},{12,28},{16,80},{20,4},{24,88},{28,12},{32,96... | collective-permute-start | bytes 1572872 | tf_op jit(solution)/shard_map/ppermute | solution.py:54
  65.5 19.3 %collective-permute-start.12 = (f32[4,256,128]{2,1,0:T(8,128)S(1)}, f32[4,256,128]{2,1,0:T(8,128)S(1)}, u32[]{:S(2)}, u32[]{:S(2)}) collective-permute-start(f32[4,256,128]{2,1,0:T(8,128)S(1)} %get-tuple-element.53), channel_id=1, source_target_pairs={{0,96},{4,28},{8,104},{12,20},{16,112},{20,12},{24,120},{28,4},{32... | collective-permute-start | bytes 1572872 | tf_op jit(solution)/shard_map/ppermute | solution.py:54
  80.8 15.0 %collective-permute-start.13 = (f32[4,256,128]{2,1,0:T(8,128)S(1)}, f32[4,256,128]{2,1,0:T(8,128)S(1)}, u32[]{:S(2)}, u32[]{:S(2)}) collective-permute-start(f32[4,256,128]{2,1,0:T(8,128)S(1)} %all_to_all.16.mine_zero.refs_0_), channel_id=1, source_target_pairs={{0,4},{4,0},{8,12},{12,8},{16,20},{20,16},{24,28},{28,24},{32,36},... | collective-permute-start | bytes 1572872 | tf_op jit(solution)/shard_map/ppermute | solution.py:58
  82.8 13.8 %collective-permute-start.14 = (f32[4,256,128]{2,1,0:T(8,128)S(1)}, f32[4,256,128]{2,1,0:T(8,128)S(1)}, u32[]{:S(2)}, u32[]{:S(2)}) collective-permute-start(f32[4,256,128]{2,1,0:T(8,128)S(1)} %all_to_all.16.mine_zero.refs_0_), channel_id=1, source_target_pairs={{0,1},{1,2},{2,3},{3,0},{4,5},{5,6},{6,7},{7,4},{8,9},{9,10},{10,1... | collective-permute-start | bytes 1572872 | tf_op jit(solution)/shard_map/ppermute | solution.py:66
  83.3 14.8 %collective-permute-start.15 = (f32[4,256,128]{2,1,0:T(8,128)S(1)}, f32[4,256,128]{2,1,0:T(8,128)S(1)}, u32[]{:S(2)}, u32[]{:S(2)}) collective-permute-start(f32[4,256,128]{2,1,0:T(8,128)S(1)} %all_to_all.16.mine_zero.refs_0_), channel_id=1, source_target_pairs={{0,3},{1,0},{2,1},{3,2},{4,7},{5,4},{6,5},{7,6},{8,11},{9,8},{10,9... | collective-permute-start | bytes 1572872 | tf_op jit(solution)/shard_map/ppermute | solution.py:66
  98.1 19.8 %collective-permute-start.16 = (f32[4,256,128]{2,1,0:T(8,128)S(1)}, f32[4,256,128]{2,1,0:T(8,128)S(1)}, u32[]{:S(2)}, u32[]{:S(2)}) collective-permute-start(f32[4,256,128]{2,1,0:T(8,128)S(1)} %all_to_all.17.mine_one.refs_6_), channel_id=1, source_target_pairs={{0,1},{1,2},{2,3},{3,0},{4,5},{5,6},{6,7},{7,4},{8,9},{9,10},{10,1... | collective-permute-start | bytes 1572872 | tf_op jit(solution)/shard_map/ppermute | solution.py:66
  98.3 19.5 %collective-permute-start.17 = (f32[4,256,128]{2,1,0:T(8,128)S(1)}, f32[4,256,128]{2,1,0:T(8,128)S(1)}, u32[]{:S(2)}, u32[]{:S(2)}) collective-permute-start(f32[4,256,128]{2,1,0:T(8,128)S(1)} %all_to_all.17.mine_one.refs_6_), channel_id=1, source_target_pairs={{0,3},{1,0},{2,1},{3,2},{4,7},{5,4},{6,5},{7,6},{8,11},{9,8},{10,9... | collective-permute-start | bytes 1572872 | tf_op jit(solution)/shard_map/ppermute | solution.py:66
  100.1 16.2 %collective-permute-start.18 = (f32[2,256,128]{2,1,0:T(8,128)S(1)}, f32[2,256,128]{2,1,0:T(8,128)S(1)}, u32[]{:S(2)}, u32[]{:S(2)}) collective-permute-start(f32[2,256,128]{2,1,0:T(8,128)S(1)} %slice.128), channel_id=1, source_target_pairs={{0,1},{1,2},{2,3},{3,0},{4,5},{5,6},{6,7},{7,4},{8,9},{9,10},{10,1... | collective-permute-start | bytes 786440 | tf_op jit(solution)/shard_map/ppermute | solution.py:66
  101.7 16.2 %collective-permute-start.19 = (f32[2,256,128]{2,1,0:T(8,128)S(1)}, f32[2,256,128]{2,1,0:T(8,128)S(1)}, u32[]{:S(2)}, u32[]{:S(2)}) collective-permute-start(f32[2,256,128]{2,1,0:T(8,128)S(1)} %slice.129), channel_id=1, source_target_pairs={{0,3},{1,0},{2,1},{3,2},{4,7},{5,4},{6,5},{7,6},{8,11},{9,8},{10,9... | collective-permute-start | bytes 786440 | tf_op jit(solution)/shard_map/ppermute | solution.py:66
  117.9 10.2 %collective-permute-start.20 = (f32[4,256,128]{2,1,0:T(8,128)S(1)}, f32[4,256,128]{2,1,0:T(8,128)S(1)}, u32[]{:S(2)}, u32[]{:S(2)}) collective-permute-start(f32[4,256,128]{2,1,0:T(8,128)S(1)} %all_to_all.17.mine_one.refs_6_), channel_id=1, source_target_pairs={{0,4},{4,0},{8,12},{12,8},{16,20},{20,16},{24,28},{28,24},{32,36},... | collective-permute-start | bytes 1572872 | tf_op jit(solution)/shard_map/ppermute | solution.py:58
  117.9 8.8 %collective-permute-start.21 = (f32[2,256,128]{2,1,0:T(8,128)S(1)}, f32[2,256,128]{2,1,0:T(8,128)S(1)}, u32[]{:S(2)}, u32[]{:S(2)}) collective-permute-start(f32[2,256,128]{2,1,0:T(8,128)S(1)} %slice.98), channel_id=1, source_target_pairs={{0,1},{1,2},{2,3},{3,0},{4,5},{5,6},{6,7},{7,4},{8,9},{9,10},{10,1... | collective-permute-start | bytes 786440 | tf_op jit(solution)/shard_map/ppermute | solution.py:66
  118.4 9.7 %collective-permute-start.22 = (f32[2,256,128]{2,1,0:T(8,128)S(1)}, f32[2,256,128]{2,1,0:T(8,128)S(1)}, u32[]{:S(2)}, u32[]{:S(2)}) collective-permute-start(f32[2,256,128]{2,1,0:T(8,128)S(1)} %slice.99), channel_id=1, source_target_pairs={{0,3},{1,0},{2,1},{3,2},{4,7},{5,4},{6,5},{7,6},{8,11},{9,8},{10,9... | collective-permute-start | bytes 786440 | tf_op jit(solution)/shard_map/ppermute | solution.py:66
  131.5 14.9 %collective-permute-start.23 = (f32[4,128,512]{2,1,0:T(8,128)S(1)}, f32[4,128,512]{2,1,0:T(8,128)S(1)}, u32[]{:S(2)}, u32[]{:S(2)}) collective-permute-start(f32[4,128,512]{2,1,0:T(8,128)S(1)} %get-tuple-element.59), channel_id=1, source_target_pairs={{0,8},{4,36},{8,0},{12,44},{16,24},{20,52},{24,16},{28,60},{32,40}... | collective-permute-start | bytes 3145736 | tf_op jit(solution)/shard_map/ppermute | solution.py:54
  133.4 14.8 %collective-permute-start.26 = (f32[4,128,512]{2,1,0:T(8,128)S(1)}, f32[4,128,512]{2,1,0:T(8,128)S(1)}, u32[]{:S(2)}, u32[]{:S(2)}) collective-permute-start(f32[4,128,512]{2,1,0:T(8,128)S(1)} %get-tuple-element.61), channel_id=1, source_target_pairs={{0,24},{4,100},{8,16},{12,108},{16,8},{20,116},{24,0},{28,124},{32... | collective-permute-start | bytes 3145736 | tf_op jit(solution)/shard_map/ppermute | solution.py:54
  137.0 20.6 %collective-permute-start.30 = (f32[4,128,512]{2,1,0:T(8,128)S(1)}, f32[4,128,512]{2,1,0:T(8,128)S(1)}, u32[]{:S(2)}, u32[]{:S(2)}) collective-permute-start(f32[4,128,512]{2,1,0:T(8,128)S(1)} %get-tuple-element.64), channel_id=1, source_target_pairs={{0,8},{4,36},{8,0},{12,44},{16,24},{20,52},{24,16},{28,60},{32,40}... | collective-permute-start | bytes 3145736 | tf_op jit(solution)/shard_map/ppermute | solution.py:54
  138.1 21.4 %collective-permute-start.33 = (f32[4,128,512]{2,1,0:T(8,128)S(1)}, f32[4,128,512]{2,1,0:T(8,128)S(1)}, u32[]{:S(2)}, u32[]{:S(2)}) collective-permute-start(f32[4,128,512]{2,1,0:T(8,128)S(1)} %get-tuple-element.66), channel_id=1, source_target_pairs={{0,24},{4,100},{8,16},{12,108},{16,8},{20,116},{24,0},{28,124},{32... | collective-permute-start | bytes 3145736 | tf_op jit(solution)/shard_map/ppermute | solution.py:54
  146.4 18.7 %collective-permute-start.24 = (f32[2,128,512]{2,1,0:T(8,128)S(1)}, f32[2,128,512]{2,1,0:T(8,128)S(1)}, u32[]{:S(2)}, u32[]{:S(2)}) collective-permute-start(f32[2,128,512]{2,1,0:T(8,128)S(1)} %slice_add_fusion.3), channel_id=1, source_target_pairs={{0,24},{4,100},{8,16},{12,108},{16,8},{20,116},{24,0},{28,124},{32... | collective-permute-start | bytes 1572872 | tf_op jit(solution)/shard_map/ppermute | solution.py:54
  148.3 16.8 %collective-permute-start.27 = (f32[2,128,512]{2,1,0:T(8,128)S(1)}, f32[2,128,512]{2,1,0:T(8,128)S(1)}, u32[]{:S(2)}, u32[]{:S(2)}) collective-permute-start(f32[2,128,512]{2,1,0:T(8,128)S(1)} %slice_add_fusion.2), channel_id=1, source_target_pairs={{0,8},{4,36},{8,0},{12,44},{16,24},{20,52},{24,16},{28,60},{32,40}... | collective-permute-start | bytes 1572872 | tf_op jit(solution)/shard_map/ppermute | solution.py:54
  157.7 18.9 %collective-permute-start.31 = (f32[2,128,512]{2,1,0:T(8,128)S(1)}, f32[2,128,512]{2,1,0:T(8,128)S(1)}, u32[]{:S(2)}, u32[]{:S(2)}) collective-permute-start(f32[2,128,512]{2,1,0:T(8,128)S(1)} %slice_add_fusion.1), channel_id=1, source_target_pairs={{0,24},{4,100},{8,16},{12,108},{16,8},{20,116},{24,0},{28,124},{32... | collective-permute-start | bytes 1572872 | tf_op jit(solution)/shard_map/ppermute | solution.py:54
  159.6 17.0 %collective-permute-start.34 = (f32[2,128,512]{2,1,0:T(8,128)S(1)}, f32[2,128,512]{2,1,0:T(8,128)S(1)}, u32[]{:S(2)}, u32[]{:S(2)}) collective-permute-start(f32[2,128,512]{2,1,0:T(8,128)S(1)} %slice_add_fusion), channel_id=1, source_target_pairs={{0,8},{4,36},{8,0},{12,44},{16,24},{20,52},{24,16},{28,60},{32,40}... | collective-permute-start | bytes 1572872 | tf_op jit(solution)/shard_map/ppermute | solution.py:54
  165.3 12.8 %collective-permute-start.25 = (f32[128,512]{1,0:T(8,128)S(1)}, f32[128,512]{1,0:T(8,128)S(1)}, u32[]{:S(2)}, u32[]{:S(2)}) collective-permute-start(f32[128,512]{1,0:T(8,128)S(1)} %get-tuple-element.72), channel_id=1, source_target_pairs={{0,32},{4,12},{8,40},{12,4},{16,48},{20,28},{24,56},{28,20},{32,0}... | collective-permute-start | bytes 786440 | tf_op jit(solution)/shard_map/ppermute | solution.py:54
  165.4 16.2 %collective-permute-start.28 = (f32[128,512]{1,0:T(8,128)S(1)}, f32[128,512]{1,0:T(8,128)S(1)}, u32[]{:S(2)}, u32[]{:S(2)}) collective-permute-start(f32[128,512]{1,0:T(8,128)S(1)} %get-tuple-element.69), channel_id=1, source_target_pairs={{0,64},{4,20},{8,72},{12,28},{16,80},{20,4},{24,88},{28,12},{32,96... | collective-permute-start | bytes 786440 | tf_op jit(solution)/shard_map/ppermute | solution.py:54
  166.9 14.7 %collective-permute-start.29 = (f32[128,512]{1,0:T(8,128)S(1)}, f32[128,512]{1,0:T(8,128)S(1)}, u32[]{:S(2)}, u32[]{:S(2)}) collective-permute-start(f32[128,512]{1,0:T(8,128)S(1)} %get-tuple-element.68), channel_id=1, source_target_pairs={{0,96},{4,28},{8,104},{12,20},{16,112},{20,12},{24,120},{28,4},{32... | collective-permute-start | bytes 786440 | tf_op jit(solution)/shard_map/ppermute | solution.py:54
  176.8 6.5 %collective-permute-start.32 = (f32[128,512]{1,0:T(8,128)S(1)}, f32[128,512]{1,0:T(8,128)S(1)}, u32[]{:S(2)}, u32[]{:S(2)}) collective-permute-start(f32[128,512]{1,0:T(8,128)S(1)} %get-tuple-element.73), channel_id=1, source_target_pairs={{0,32},{4,12},{8,40},{12,4},{16,48},{20,28},{24,56},{28,20},{32,0}... | collective-permute-start | bytes 786440 | tf_op jit(solution)/shard_map/ppermute | solution.py:54
  176.9 8.4 %collective-permute-start.35 = (f32[128,512]{1,0:T(8,128)S(1)}, f32[128,512]{1,0:T(8,128)S(1)}, u32[]{:S(2)}, u32[]{:S(2)}) collective-permute-start(f32[128,512]{1,0:T(8,128)S(1)} %get-tuple-element.71), channel_id=1, source_target_pairs={{0,64},{4,20},{8,72},{12,28},{16,80},{20,4},{24,88},{28,12},{32,96... | collective-permute-start | bytes 786440 | tf_op jit(solution)/shard_map/ppermute | solution.py:54
  178.1 10.0 %collective-permute-start.36 = (f32[128,512]{1,0:T(8,128)S(1)}, f32[128,512]{1,0:T(8,128)S(1)}, u32[]{:S(2)}, u32[]{:S(2)}) collective-permute-start(f32[128,512]{1,0:T(8,128)S(1)} %get-tuple-element.70), channel_id=1, source_target_pairs={{0,96},{4,28},{8,104},{12,20},{16,112},{20,12},{24,120},{28,4},{32... | collective-permute-start | bytes 786440 | tf_op jit(solution)/shard_map/ppermute | solution.py:54

commit v7 on v6

--- a/solution.py
+++ b/solution.py
@@ -10,7 +10,7 @@
 
 SIDE = 4
 LANE = 128
-VMEM = 40 * 2**20
+VMEM = 28 * 2**20
 
 
 def place(z, y, c):

time: 189 us -> 189 us (level)
  no operation moved by 1% of the time
where the time goes in v7:
time: 189 us
  waiting for transfers between devices  71.9 us (38%)
  starting transfers between devices  55.9 us (30%)
  Pallas kernels  34.5 us (18%)
  blocking collectives  21.8 us (12%)
  other arithmetic  2.35 us (1%)
    ppermute x23, starting transfers between devices, hop(): return lax.ppermute(value, 'row', partners(ring, step))  33 us
    ppermute x23, waiting for transfers between devices, hop(): return lax.ppermute(value, 'row', partners(ring, step))  30.4 us
    ppermute x8, waiting for transfers between devices, around(): lax.ppermute(value, 'col', [(i, (i + step) % SIDE) for i in range(SIDE)])  25.7 us
    all_to_all x2, blocking collectives, exchange(): lax.all_to_all(value, 'row', 0, 0, tiled=True, axis_index_groups=groups(r...  21.8 us
    pallas_call x2, Pallas kernels, sampled_rows(): call(functools.partial(sample_kernel, scale, chunk, owned), (), [pl.Block...  13.9 us
    pallas_call x3, Pallas kernels, gram_shares(): call(functools.partial(gram_kernel, plan, halves), (), [pl.BlockSpec(memo...  12.8 us
    ppermute x4, waiting for transfers between devices, across(): lax.ppermute(value, 'row', [(i ^ 1, j) for i, j in partners(FIRST, step)])  11.5 us
    ppermute x8, starting transfers between devices, around(): lax.ppermute(value, 'col', [(i, (i + step) % SIDE) for i in range(SIDE)])  8.41 us
  transfers between devices with their start and end apart: 38, of which 20 were waited for; matrix products, arithmetic and copies ran while one was open for 1% of the time, Pallas kernels for 9%

profile of v7, /device:TPU:14, one launch (start us, length us, event | category | flops | bytes accessed | tf_op | source)
XLA Modules:
  0.0 189.0 jit_solution(6737967655983101687)
XLA Ops:
  0.6 6.3 %shard_map.59 = (f32[1024,128]{1,0:T(8,128)}, f32[1024,128]{1,0:T(8,128)}, f32[1024,128]{1,0:T(8,128)}, f32[1024,128]{1,0:T(8,128)}, f32[1024,128]{1,0:T(8,128)}...) custom-call(bf16[256,256]{1,0:T(8,128)(2,1)} %constant.110.clone.table_ref, s32[1,1024]{1,0:T(1,128)} %bitcast.31, ...), custom_call_target="tpu_custom_call" | custom-call | flops 1073741824 | bytes 8388608 | tf_op jit(solution)/shard_map/pallas_call | solution.py:150
  7.0 0.5 collective-permute-start
  7.5 2.6 %collective-permute-start.1 = (f32[1024,128]{1,0:T(8,128)}, f32[1024,128]{1,0:T(8,128)S(1)}, u32[]{:S(2)}, u32[]{:S(2)}) collective-permute-start(f32[1024,128]{1,0:T(8,128)} %get-tuple-element.40), channel_id=1, source_target_pairs={{0,16},{4,68},{8,24},{12,76},{16,0},{20,84},{24,8},{28,92},{32,48}... | collective-permute-start | bytes 1572872 | tf_op jit(solution)/shard_map/ppermute | solution.py:54
  10.1 0.6 broadcast_in_dim.7
  10.7 7.4 %all-to-all-start = ((s32[32,1,256]{2,1,0:T(1,128)}), s32[32,1,256]{2,1,0:T(1,128)S(1)}, u32[]{:S(2)}, u32[]{:S(2)}) async-start(s32[32,1,256]{2,1,0:T(1,128)} %broadcast_in_dim.7), calls=%async_computation | async-start | bytes 65536 | tf_op jit(solution)/shard_map/all_to_all | solution.py:336
  18.1 1.5 collective-permute-start.2
  19.7 0.9 collective-permute-start.4
  20.6 3.5 %collective-permute-start.5 = (f32[1024,128]{1,0:T(8,128)}, f32[1024,128]{1,0:T(8,128)S(1)}, u32[]{:S(2)}, u32[]{:S(2)}) collective-permute-start(f32[1024,128]{1,0:T(8,128)} %get-tuple-element.44), channel_id=1, source_target_pairs={{4,16},{0,68},{12,24},{8,76},{20,0},{16,84},{28,8},{24,92},{36,48}... | collective-permute-start | bytes 1572872 | tf_op jit(solution)/shard_map/ppermute | solution.py:62
  24.2 4.2 %all-to-all-done = s32[32,1,256]{2,1,0:T(1,128)S(1)} async-done(((s32[32,1,256]{2,1,0:T(1,128)}), s32[32,1,256]{2,1,0:T(1,128)S(1)}, u32[]{:S(2)}, u32[]{:S(2)}) %all-to-all-start) | async-done | bytes 32800 | tf_op jit(solution)/shard_map/all_to_all | solution.py:336
  28.8 0.4 collective-permute-start.3
  29.3 6.0 %collective-permute-done.5.refs_6_ = f32[1024,128]{1,0:T(8,128)S(1)} collective-permute-done((f32[1024,128]{1,0:T(8,128)}, f32[1024,128]{1,0:T(8,128)S(1)}, u32[]{:S(2)}, u32[]{:S(2)}) %collective-permute-start.5) | collective-permute-done | bytes 524320 | tf_op jit(solution)/shard_map/ppermute | solution.py:62
  35.3 5.5 %collective-permute-done.6.refs_7_ = f32[1024,128]{1,0:T(8,128)S(1)} collective-permute-done((f32[1024,128]{1,0:T(8,128)}, f32[1024,128]{1,0:T(8,128)S(1)}, u32[]{:S(2)}, u32[]{:S(2)}) %collective-permute-start.6) | collective-permute-done | bytes 524320 | tf_op jit(solution)/shard_map/ppermute | solution.py:62
  40.8 1.0 copy-done
  41.9 6.9 %shard_map.60 = (f32[4,256,128]{2,1,0:T(8,128)S(1)}, f32[4,256,128]{2,1,0:T(8,128)S(1)}, f32[4,256,128]{2,1,0:T(8,128)S(1)}, f32[4,256,128]{2,1,0:T(8,128)S(1)}) custom-call(s32[4]{0:T(128)S(1)} %pad_add_fusion.where_ref, s32[8192]{0:T(1024)S(1)} %fusion.13.index_ref, f32[1024,128]{1,0:T(8,128)S(1)} %copy-done, ...), custom_call_target="tpu_custom_call" | custom-call | flops 16777216 | bytes 8388608 | tf_op jit(solution)/shard_map/pallas_call | solution.py:215
  48.8 1.4 collective-permute-start.7
  50.2 3.6 %collective-permute-start.8 = (f32[4,256,128]{2,1,0:T(8,128)S(1)}, f32[4,256,128]{2,1,0:T(8,128)S(1)}, u32[]{:S(2)}, u32[]{:S(2)}) collective-permute-start(f32[4,256,128]{2,1,0:T(8,128)S(1)} %get-tuple-element.48), channel_id=1, source_target_pairs={{0,64},{4,20},{8,72},{12,28},{16,80},{20,4},{24,88},{28,12},{32,96... | collective-permute-start | bytes 1572872 | tf_op jit(solution)/shard_map/ppermute | solution.py:54
  53.8 6.9 %shard_map.61 = (f32[4,256,128]{2,1,0:T(8,128)S(1)}, f32[4,256,128]{2,1,0:T(8,128)S(1)}, f32[4,256,128]{2,1,0:T(8,128)S(1)}, f32[4,256,128]{2,1,0:T(8,128)S(1)}) custom-call(s32[4]{0:T(128)S(1)} %pad_add_fusion.where_ref, s32[8192]{0:T(1024)S(1)} %fusion.13.index_ref, f32[1024,128]{1,0:T(8,128)S(1)} %copy-done, ...), custom_call_target="tpu_custom_call" | custom-call | flops 16777216 | bytes 8388608 | tf_op jit(solution)/shard_map/pallas_call | solution.py:215
  60.9 4.7 %collective-permute-start.11 = (f32[4,256,128]{2,1,0:T(8,128)S(1)}, f32[4,256,128]{2,1,0:T(8,128)S(1)}, u32[]{:S(2)}, u32[]{:S(2)}) collective-permute-start(f32[4,256,128]{2,1,0:T(8,128)S(1)} %get-tuple-element.52), channel_id=1, source_target_pairs={{0,64},{4,20},{8,72},{12,28},{16,80},{20,4},{24,88},{28,12},{32,96... | collective-permute-start | bytes 1572872 | tf_op jit(solution)/shard_map/ppermute | solution.py:54
  65.5 1.1 collective-permute-done.8
  66.7 3.1 %collective-permute-done.9 = f32[4,256,128]{2,1,0:T(8,128)S(1)} collective-permute-done((f32[4,256,128]{2,1,0:T(8,128)S(1)}, f32[4,256,128]{2,1,0:T(8,128)S(1)}, u32[]{:S(2)}, u32[]{:S(2)}) %collective-permute-start.9) | collective-permute-done | bytes 524320 | tf_op jit(solution)/shard_map/ppermute | solution.py:54
  69.9 10.9 %all_to_all.16.mine_zero.refs_0_ = f32[4,256,128]{2,1,0:T(8,128)S(1)} all-to-all(f32[4,256,128]{2,1,0:T(8,128)S(1)} %add_add_fusion.1), channel_id=1, replica_groups={{0,8,16,24},{4,36,68,100},{32,40,48,56},{12,44,76,108},{64,72,80,88},{2..., dimensions={0} | all-to-all | bytes 1048576 | tf_op jit(solution)/shard_map/all_to_all | solution.py:50
  80.8 2.0 %collective-permute-start.13 = (f32[4,256,128]{2,1,0:T(8,128)S(1)}, f32[4,256,128]{2,1,0:T(8,128)S(1)}, u32[]{:S(2)}, u32[]{:S(2)}) collective-permute-start(f32[4,256,128]{2,1,0:T(8,128)S(1)} %all_to_all.16.mine_zero.refs_0_), channel_id=1, source_target_pairs={{0,4},{4,0},{8,12},{12,8},{16,20},{20,16},{24,28},{28,24},{32,36},... | collective-permute-start | bytes 1572872 | tf_op jit(solution)/shard_map/ppermute | solution.py:58
  82.8 0.5 collective-permute-start.14
  83.3 1.5 collective-permute-start.15
  85.0 10.9 %all_to_all.17.mine_one.refs_6_ = f32[4,256,128]{2,1,0:T(8,128)S(1)} all-to-all(f32[4,256,128]{2,1,0:T(8,128)S(1)} %add_add_fusion), channel_id=1, replica_groups={{0,8,16,24},{4,36,68,100},{32,40,48,56},{12,44,76,108},{64,72,80,88},{2..., dimensions={0} | all-to-all | bytes 1048576 | tf_op jit(solution)/shard_map/all_to_all | solution.py:50
  95.9 0.8 collective-permute-done.14.refs_2_
  96.6 1.4 collective-permute-done.15.refs_3_
  98.1 0.3 collective-permute-start.16
  98.3 1.8 collective-permute-start.17
  100.1 1.5 collective-permute-start.18
  101.7 0.6 collective-permute-start.19
  102.3 14.0 %collective-permute-done.18.refs_4_ = f32[2,256,128]{2,1,0:T(8,128)S(1)} collective-permute-done((f32[2,256,128]{2,1,0:T(8,128)S(1)}, f32[2,256,128]{2,1,0:T(8,128)S(1)}, u32[]{:S(2)}, u32[]{:S(2)}) %collective-permute-start.18) | collective-permute-done | bytes 262176 | tf_op jit(solution)/shard_map/ppermute | solution.py:66
  116.3 1.5 collective-permute-done.19.refs_5_
  117.9 0.4 collective-permute-start.21
  118.4 1.7 collective-permute-start.22
  120.1 6.6 %collective-permute-done.21.refs_10_ = f32[2,256,128]{2,1,0:T(8,128)S(1)} collective-permute-done((f32[2,256,128]{2,1,0:T(8,128)S(1)}, f32[2,256,128]{2,1,0:T(8,128)S(1)}, u32[]{:S(2)}, u32[]{:S(2)}) %collective-permute-start.21) | collective-permute-done | bytes 262176 | tf_op jit(solution)/shard_map/ppermute | solution.py:66
  126.7 1.4 collective-permute-done.22.refs_11_
  128.1 3.4 %shard_map.64 = (f32[4,128,512]{2,1,0:T(8,128)S(1)}, f32[4,128,512]{2,1,0:T(8,128)S(1)}) custom-call(s32[4]{0:T(128)S(1)} %pad_add_fusion.where_ref, f32[4,256,128]{2,1,0:T(8,128)S(1)} %all_to_all.16.mine_zero.refs_0_, f32[4,256,128]{2,1,0:T(8,128)S(1)} %collective-permute-done.13.sibling_zero.refs_1_, f32[4,256,128]{2,1,0:T(8,128)S(1)} %collective-permute-done.14.refs_2_, ...), custom_call_target="tpu_custom_call" | custom-call | flops 3221225472 | bytes 8388608 | tf_op jit(solution)/shard_map/pallas_call | solution.py:316
  131.5 2.0 %collective-permute-start.23 = (f32[4,128,512]{2,1,0:T(8,128)S(1)}, f32[4,128,512]{2,1,0:T(8,128)S(1)}, u32[]{:S(2)}, u32[]{:S(2)}) collective-permute-start(f32[4,128,512]{2,1,0:T(8,128)S(1)} %get-tuple-element.59), channel_id=1, source_target_pairs={{0,8},{4,36},{8,0},{12,44},{16,24},{20,52},{24,16},{28,60},{32,40}... | collective-permute-start | bytes 3145736 | tf_op jit(solution)/shard_map/ppermute | solution.py:54
  133.6 3.4 %shard_map.65 = (f32[4,128,512]{2,1,0:T(8,128)S(1)}, f32[4,128,512]{2,1,0:T(8,128)S(1)}) custom-call(s32[4]{0:T(128)S(1)} %pad_add_fusion.where_ref, f32[4,256,128]{2,1,0:T(8,128)S(1)} %all_to_all.16.mine_zero.refs_0_, f32[4,256,128]{2,1,0:T(8,128)S(1)} %collective-permute-done.13.sibling_zero.refs_1_, f32[4,256,128]{2,1,0:T(8,128)S(1)} %collective-permute-done.14.refs_2_, ...), custom_call_target="tpu_custom_call" | custom-call | flops 3221225472 | bytes 8388608 | tf_op jit(solution)/shard_map/pallas_call | solution.py:316
  137.0 1.1 collective-permute-start.30
  138.1 1.6 collective-permute-start.33
  139.7 6.0 %shard_map.63 = (f32[2,128,512]{2,1,0:T(8,128)S(1)}, f32[2,128,512]{2,1,0:T(8,128)S(1)}, f32[2,128,512]{2,1,0:T(8,128)S(1)}, f32[2,128,512]{2,1,0:T(8,128)S(1)},...) custom-call(s32[4]{0:T(128)S(1)} %pad_add_fusion.where_ref, f32[4,256,128]{2,1,0:T(8,128)S(1)} %all_to_all.16.mine_zero.refs_0_, ...), custom_call_target="tpu_custom_call" | custom-call | flops 3221225472 | bytes 8388608 | tf_op jit(solution)/shard_map/pallas_call | solution.py:316
  145.7 0.7 collective-permute-done.23
  146.4 0.5 collective-permute-start.24
  147.0 1.3 collective-permute-done.26
  148.3 1.6 collective-permute-start.27
  150.0 7.6 %collective-permute-done.30 = f32[4,128,512]{2,1,0:T(8,128)S(1)} collective-permute-done((f32[4,128,512]{2,1,0:T(8,128)S(1)}, f32[4,128,512]{2,1,0:T(8,128)S(1)}, u32[]{:S(2)}, u32[]{:S(2)}) %collective-permute-start.30) | collective-permute-done | bytes 1048608 | tf_op jit(solution)/shard_map/ppermute | solution.py:54
  157.7 0.5 collective-permute-start.31
  158.2 1.3 collective-permute-done.33
  159.6 1.4 collective-permute-start.34
  161.0 1.6 shard_map.62
  162.6 2.5 %collective-permute-done.24 = f32[2,128,512]{2,1,0:T(8,128)S(1)} collective-permute-done((f32[2,128,512]{2,1,0:T(8,128)S(1)}, f32[2,128,512]{2,1,0:T(8,128)S(1)}, u32[]{:S(2)}, u32[]{:S(2)}) %collective-permute-start.24) | collective-permute-done | bytes 524320 | tf_op jit(solution)/shard_map/ppermute | solution.py:54
  165.1 0.2 fusion.6
  165.4 1.5 collective-permute-start.28
  166.9 3.2 %collective-permute-start.29 = (f32[128,512]{1,0:T(8,128)S(1)}, f32[128,512]{1,0:T(8,128)S(1)}, u32[]{:S(2)}, u32[]{:S(2)}) collective-permute-start(f32[128,512]{1,0:T(8,128)S(1)} %get-tuple-element.68), channel_id=1, source_target_pairs={{0,96},{4,28},{8,104},{12,20},{16,112},{20,12},{24,120},{28,4},{32... | collective-permute-start | bytes 786440 | tf_op jit(solution)/shard_map/ppermute | solution.py:54
  170.1 6.4 %collective-permute-done.31 = f32[2,128,512]{2,1,0:T(8,128)S(1)} collective-permute-done((f32[2,128,512]{2,1,0:T(8,128)S(1)}, f32[2,128,512]{2,1,0:T(8,128)S(1)}, u32[]{:S(2)}, u32[]{:S(2)}) %collective-permute-start.31) | collective-permute-done | bytes 524320 | tf_op jit(solution)/shard_map/ppermute | solution.py:54
  176.6 0.2 fusion
  176.9 1.2 collective-permute-start.35
  178.1 3.5 %collective-permute-start.36 = (f32[128,512]{1,0:T(8,128)S(1)}, f32[128,512]{1,0:T(8,128)S(1)}, u32[]{:S(2)}, u32[]{:S(2)}) collective-permute-start(f32[128,512]{1,0:T(8,128)S(1)} %get-tuple-element.70), channel_id=1, source_target_pairs={{0,96},{4,28},{8,104},{12,20},{16,112},{20,12},{24,120},{28,4},{32... | collective-permute-start | bytes 786440 | tf_op jit(solution)/shard_map/ppermute | solution.py:54
  181.8 1.5 collective-permute-done.32
  183.3 2.1 %collective-permute-done.35 = f32[128,512]{1,0:T(8,128)S(1)} collective-permute-done((f32[128,512]{1,0:T(8,128)S(1)}, f32[128,512]{1,0:T(8,128)S(1)}, u32[]{:S(2)}, u32[]{:S(2)}) %collective-permute-start.35) | collective-permute-done | bytes 262176 | tf_op jit(solution)/shard_map/ppermute | solution.py:54
  185.4 2.7 %collective-permute-done.36 = f32[128,512]{1,0:T(8,128)S(1)} collective-permute-done((f32[128,512]{1,0:T(8,128)S(1)}, f32[128,512]{1,0:T(8,128)S(1)}, u32[]{:S(2)}, u32[]{:S(2)}) %collective-permute-start.36) | collective-permute-done | bytes 262176 | tf_op jit(solution)/shard_map/ppermute | solution.py:54
  188.2 0.8 pad_maximum_fusion
  (43 shorter events, 1.8 us)
Async XLA Ops:
  0.6 9.5 %copy-start.1 = (s32[256]{0:T(256)S(1)}, s32[256]{0:T(256)}, u32[]{:S(2)}) copy-start(s32[256]{0:T(256)} %param.6) | copy-start | bytes 3076
  7.0 21.6 %collective-permute-start = (f32[1024,128]{1,0:T(8,128)}, f32[1024,128]{1,0:T(8,128)S(1)}, u32[]{:S(2)}, u32[]{:S(2)}) collective-permute-start(f32[1024,128]{1,0:T(8,128)} %get-tuple-element.39), channel_id=1, source_target_pairs={{0,8},{4,36},{8,0},{12,44},{16,24},{20,52},{24,16},{28,60},{32,40}... | collective-permute-start | bytes 1572872 | tf_op jit(solution)/shard_map/ppermute | solution.py:54
  7.5 21.3 %collective-permute-start.1 = (f32[1024,128]{1,0:T(8,128)}, f32[1024,128]{1,0:T(8,128)S(1)}, u32[]{:S(2)}, u32[]{:S(2)}) collective-permute-start(f32[1024,128]{1,0:T(8,128)} %get-tuple-element.40), channel_id=1, source_target_pairs={{0,16},{4,68},{8,24},{12,76},{16,0},{20,84},{24,8},{28,92},{32,48}... | collective-permute-start | bytes 1572872 | tf_op jit(solution)/shard_map/ppermute | solution.py:54
  10.7 17.7 %all-to-all-start = ((s32[32,1,256]{2,1,0:T(1,128)}), s32[32,1,256]{2,1,0:T(1,128)S(1)}, u32[]{:S(2)}, u32[]{:S(2)}) async-start(s32[32,1,256]{2,1,0:T(1,128)} %broadcast_in_dim.7), calls=%async_computation | async-start | bytes 65536 | tf_op jit(solution)/shard_map/all_to_all | solution.py:336
  18.1 11.2 %collective-permute-start.2 = (f32[1024,128]{1,0:T(8,128)}, f32[1024,128]{1,0:T(8,128)S(1)}, u32[]{:S(2)}, u32[]{:S(2)}) collective-permute-start(f32[1024,128]{1,0:T(8,128)} %get-tuple-element.41), channel_id=1, source_target_pairs={{0,24},{4,100},{8,16},{12,108},{16,8},{20,116},{24,0},{28,124},{32... | collective-permute-start | bytes 1572872 | tf_op jit(solution)/shard_map/ppermute | solution.py:54
  19.7 9.6 %collective-permute-start.4 = (f32[1024,128]{1,0:T(8,128)}, f32[1024,128]{1,0:T(8,128)S(1)}, u32[]{:S(2)}, u32[]{:S(2)}) collective-permute-start(f32[1024,128]{1,0:T(8,128)} %get-tuple-element.43), channel_id=1, source_target_pairs={{4,8},{0,36},{12,0},{8,44},{20,24},{16,52},{28,16},{24,60},{36,40}... | collective-permute-start | bytes 1572872 | tf_op jit(solution)/shard_map/ppermute | solution.py:62
  20.6 14.7 %collective-permute-start.5 = (f32[1024,128]{1,0:T(8,128)}, f32[1024,128]{1,0:T(8,128)S(1)}, u32[]{:S(2)}, u32[]{:S(2)}) collective-permute-start(f32[1024,128]{1,0:T(8,128)} %get-tuple-element.44), channel_id=1, source_target_pairs={{4,16},{0,68},{12,24},{8,76},{20,0},{16,84},{28,8},{24,92},{36,48}... | collective-permute-start | bytes 1572872 | tf_op jit(solution)/shard_map/ppermute | solution.py:62
  28.5 12.3 %collective-permute-start.6 = (f32[1024,128]{1,0:T(8,128)}, f32[1024,128]{1,0:T(8,128)S(1)}, u32[]{:S(2)}, u32[]{:S(2)}) collective-permute-start(f32[1024,128]{1,0:T(8,128)} %get-tuple-element.45), channel_id=1, source_target_pairs={{4,24},{0,100},{12,16},{8,108},{20,8},{16,116},{28,0},{24,124},{36... | collective-permute-start | bytes 1572872 | tf_op jit(solution)/shard_map/ppermute | solution.py:62
  28.8 12.0 %collective-permute-start.3 = (f32[1024,128]{1,0:T(8,128)}, f32[1024,128]{1,0:T(8,128)}, u32[]{:S(2)}, u32[]{:S(2)}) collective-permute-start(f32[1024,128]{1,0:T(8,128)} %get-tuple-element.42), channel_id=1, source_target_pairs={{4,0},{0,4},{12,8},{8,12},{20,16},{16,20},{28,24},{24,28},{36,32},... | collective-permute-start | bytes 1572872 | tf_op jit(solution)/shard_map/ppermute | solution.py:62
  40.8 1.0 copy-start
  48.8 16.7 %collective-permute-start.7 = (f32[4,256,128]{2,1,0:T(8,128)S(1)}, f32[4,256,128]{2,1,0:T(8,128)S(1)}, u32[]{:S(2)}, u32[]{:S(2)}) collective-permute-start(f32[4,256,128]{2,1,0:T(8,128)S(1)} %get-tuple-element.47), channel_id=1, source_target_pairs={{0,32},{4,12},{8,40},{12,4},{16,48},{20,28},{24,56},{28,20},{32,0}... | collective-permute-start | bytes 1572872 | tf_op jit(solution)/shard_map/ppermute | solution.py:54
  50.2 16.5 %collective-permute-start.8 = (f32[4,256,128]{2,1,0:T(8,128)S(1)}, f32[4,256,128]{2,1,0:T(8,128)S(1)}, u32[]{:S(2)}, u32[]{:S(2)}) collective-permute-start(f32[4,256,128]{2,1,0:T(8,128)S(1)} %get-tuple-element.48), channel_id=1, source_target_pairs={{0,64},{4,20},{8,72},{12,28},{16,80},{20,4},{24,88},{28,12},{32,96... | collective-permute-start | bytes 1572872 | tf_op jit(solution)/shard_map/ppermute | solution.py:54
  53.8 16.0 %collective-permute-start.9 = (f32[4,256,128]{2,1,0:T(8,128)S(1)}, f32[4,256,128]{2,1,0:T(8,128)S(1)}, u32[]{:S(2)}, u32[]{:S(2)}) collective-permute-start(f32[4,256,128]{2,1,0:T(8,128)S(1)} %get-tuple-element.49), channel_id=1, source_target_pairs={{0,96},{4,28},{8,104},{12,20},{16,112},{20,12},{24,120},{28,4},{32... | collective-permute-start | bytes 1572872 | tf_op jit(solution)/shard_map/ppermute | solution.py:54
  60.8 22.5 %collective-permute-start.10 = (f32[4,256,128]{2,1,0:T(8,128)S(1)}, f32[4,256,128]{2,1,0:T(8,128)S(1)}, u32[]{:S(2)}, u32[]{:S(2)}) collective-permute-start(f32[4,256,128]{2,1,0:T(8,128)S(1)} %get-tuple-element.51), channel_id=1, source_target_pairs={{0,32},{4,12},{8,40},{12,4},{16,48},{20,28},{24,56},{28,20},{32,0}... | collective-permute-start | bytes 1572872 | tf_op jit(solution)/shard_map/ppermute | solution.py:54
  60.9 24.0 %collective-permute-start.11 = (f32[4,256,128]{2,1,0:T(8,128)S(1)}, f32[4,256,128]{2,1,0:T(8,128)S(1)}, u32[]{:S(2)}, u32[]{:S(2)}) collective-permute-start(f32[4,256,128]{2,1,0:T(8,128)S(1)} %get-tuple-element.52), channel_id=1, source_target_pairs={{0,64},{4,20},{8,72},{12,28},{16,80},{20,4},{24,88},{28,12},{32,96... | collective-permute-start | bytes 1572872 | tf_op jit(solution)/shard_map/ppermute | solution.py:54
  65.5 19.3 %collective-permute-start.12 = (f32[4,256,128]{2,1,0:T(8,128)S(1)}, f32[4,256,128]{2,1,0:T(8,128)S(1)}, u32[]{:S(2)}, u32[]{:S(2)}) collective-permute-start(f32[4,256,128]{2,1,0:T(8,128)S(1)} %get-tuple-element.53), channel_id=1, source_target_pairs={{0,96},{4,28},{8,104},{12,20},{16,112},{20,12},{24,120},{28,4},{32... | collective-permute-start | bytes 1572872 | tf_op jit(solution)/shard_map/ppermute | solution.py:54
  80.8 15.0 %collective-permute-start.13 = (f32[4,256,128]{2,1,0:T(8,128)S(1)}, f32[4,256,128]{2,1,0:T(8,128)S(1)}, u32[]{:S(2)}, u32[]{:S(2)}) collective-permute-start(f32[4,256,128]{2,1,0:T(8,128)S(1)} %all_to_all.16.mine_zero.refs_0_), channel_id=1, source_target_pairs={{0,4},{4,0},{8,12},{12,8},{16,20},{20,16},{24,28},{28,24},{32,36},... | collective-permute-start | bytes 1572872 | tf_op jit(solution)/shard_map/ppermute | solution.py:58
  82.8 13.8 %collective-permute-start.14 = (f32[4,256,128]{2,1,0:T(8,128)S(1)}, f32[4,256,128]{2,1,0:T(8,128)S(1)}, u32[]{:S(2)}, u32[]{:S(2)}) collective-permute-start(f32[4,256,128]{2,1,0:T(8,128)S(1)} %all_to_all.16.mine_zero.refs_0_), channel_id=1, source_target_pairs={{0,1},{1,2},{2,3},{3,0},{4,5},{5,6},{6,7},{7,4},{8,9},{9,10},{10,1... | collective-permute-start | bytes 1572872 | tf_op jit(solution)/shard_map/ppermute | solution.py:66
  83.3 14.8 %collective-permute-start.15 = (f32[4,256,128]{2,1,0:T(8,128)S(1)}, f32[4,256,128]{2,1,0:T(8,128)S(1)}, u32[]{:S(2)}, u32[]{:S(2)}) collective-permute-start(f32[4,256,128]{2,1,0:T(8,128)S(1)} %all_to_all.16.mine_zero.refs_0_), channel_id=1, source_target_pairs={{0,3},{1,0},{2,1},{3,2},{4,7},{5,4},{6,5},{7,6},{8,11},{9,8},{10,9... | collective-permute-start | bytes 1572872 | tf_op jit(solution)/shard_map/ppermute | solution.py:66
  98.1 19.8 %collective-permute-start.16 = (f32[4,256,128]{2,1,0:T(8,128)S(1)}, f32[4,256,128]{2,1,0:T(8,128)S(1)}, u32[]{:S(2)}, u32[]{:S(2)}) collective-permute-start(f32[4,256,128]{2,1,0:T(8,128)S(1)} %all_to_all.17.mine_one.refs_6_), channel_id=1, source_target_pairs={{0,1},{1,2},{2,3},{3,0},{4,5},{5,6},{6,7},{7,4},{8,9},{9,10},{10,1... | collective-permute-start | bytes 1572872 | tf_op jit(solution)/shard_map/ppermute | solution.py:66
  98.3 19.5 %collective-permute-start.17 = (f32[4,256,128]{2,1,0:T(8,128)S(1)}, f32[4,256,128]{2,1,0:T(8,128)S(1)}, u32[]{:S(2)}, u32[]{:S(2)}) collective-permute-start(f32[4,256,128]{2,1,0:T(8,128)S(1)} %all_to_all.17.mine_one.refs_6_), channel_id=1, source_target_pairs={{0,3},{1,0},{2,1},{3,2},{4,7},{5,4},{6,5},{7,6},{8,11},{9,8},{10,9... | collective-permute-start | bytes 1572872 | tf_op jit(solution)/shard_map/ppermute | solution.py:66
  100.1 16.2 %collective-permute-start.18 = (f32[2,256,128]{2,1,0:T(8,128)S(1)}, f32[2,256,128]{2,1,0:T(8,128)S(1)}, u32[]{:S(2)}, u32[]{:S(2)}) collective-permute-start(f32[2,256,128]{2,1,0:T(8,128)S(1)} %slice.128), channel_id=1, source_target_pairs={{0,1},{1,2},{2,3},{3,0},{4,5},{5,6},{6,7},{7,4},{8,9},{9,10},{10,1... | collective-permute-start | bytes 786440 | tf_op jit(solution)/shard_map/ppermute | solution.py:66
  101.7 16.2 %collective-permute-start.19 = (f32[2,256,128]{2,1,0:T(8,128)S(1)}, f32[2,256,128]{2,1,0:T(8,128)S(1)}, u32[]{:S(2)}, u32[]{:S(2)}) collective-permute-start(f32[2,256,128]{2,1,0:T(8,128)S(1)} %slice.129), channel_id=1, source_target_pairs={{0,3},{1,0},{2,1},{3,2},{4,7},{5,4},{6,5},{7,6},{8,11},{9,8},{10,9... | collective-permute-start | bytes 786440 | tf_op jit(solution)/shard_map/ppermute | solution.py:66
  117.9 10.2 %collective-permute-start.20 = (f32[4,256,128]{2,1,0:T(8,128)S(1)}, f32[4,256,128]{2,1,0:T(8,128)S(1)}, u32[]{:S(2)}, u32[]{:S(2)}) collective-permute-start(f32[4,256,128]{2,1,0:T(8,128)S(1)} %all_to_all.17.mine_one.refs_6_), channel_id=1, source_target_pairs={{0,4},{4,0},{8,12},{12,8},{16,20},{20,16},{24,28},{28,24},{32,36},... | collective-permute-start | bytes 1572872 | tf_op jit(solution)/shard_map/ppermute | solution.py:58
  117.9 8.8 %collective-permute-start.21 = (f32[2,256,128]{2,1,0:T(8,128)S(1)}, f32[2,256,128]{2,1,0:T(8,128)S(1)}, u32[]{:S(2)}, u32[]{:S(2)}) collective-permute-start(f32[2,256,128]{2,1,0:T(8,128)S(1)} %slice.98), channel_id=1, source_target_pairs={{0,1},{1,2},{2,3},{3,0},{4,5},{5,6},{6,7},{7,4},{8,9},{9,10},{10,1... | collective-permute-start | bytes 786440 | tf_op jit(solution)/shard_map/ppermute | solution.py:66
  118.4 9.7 %collective-permute-start.22 = (f32[2,256,128]{2,1,0:T(8,128)S(1)}, f32[2,256,128]{2,1,0:T(8,128)S(1)}, u32[]{:S(2)}, u32[]{:S(2)}) collective-permute-start(f32[2,256,128]{2,1,0:T(8,128)S(1)} %slice.99), channel_id=1, source_target_pairs={{0,3},{1,0},{2,1},{3,2},{4,7},{5,4},{6,5},{7,6},{8,11},{9,8},{10,9... | collective-permute-start | bytes 786440 | tf_op jit(solution)/shard_map/ppermute | solution.py:66
  131.5 14.9 %collective-permute-start.23 = (f32[4,128,512]{2,1,0:T(8,128)S(1)}, f32[4,128,512]{2,1,0:T(8,128)S(1)}, u32[]{:S(2)}, u32[]{:S(2)}) collective-permute-start(f32[4,128,512]{2,1,0:T(8,128)S(1)} %get-tuple-element.59), channel_id=1, source_target_pairs={{0,8},{4,36},{8,0},{12,44},{16,24},{20,52},{24,16},{28,60},{32,40}... | collective-permute-start | bytes 3145736 | tf_op jit(solution)/shard_map/ppermute | solution.py:54
  133.4 14.8 %collective-permute-start.26 = (f32[4,128,512]{2,1,0:T(8,128)S(1)}, f32[4,128,512]{2,1,0:T(8,128)S(1)}, u32[]{:S(2)}, u32[]{:S(2)}) collective-permute-start(f32[4,128,512]{2,1,0:T(8,128)S(1)} %get-tuple-element.61), channel_id=1, source_target_pairs={{0,24},{4,100},{8,16},{12,108},{16,8},{20,116},{24,0},{28,124},{32... | collective-permute-start | bytes 3145736 | tf_op jit(solution)/shard_map/ppermute | solution.py:54
  137.0 20.6 %collective-permute-start.30 = (f32[4,128,512]{2,1,0:T(8,128)S(1)}, f32[4,128,512]{2,1,0:T(8,128)S(1)}, u32[]{:S(2)}, u32[]{:S(2)}) collective-permute-start(f32[4,128,512]{2,1,0:T(8,128)S(1)} %get-tuple-element.64), channel_id=1, source_target_pairs={{0,8},{4,36},{8,0},{12,44},{16,24},{20,52},{24,16},{28,60},{32,40}... | collective-permute-start | bytes 3145736 | tf_op jit(solution)/shard_map/ppermute | solution.py:54
  138.1 21.4 %collective-permute-start.33 = (f32[4,128,512]{2,1,0:T(8,128)S(1)}, f32[4,128,512]{2,1,0:T(8,128)S(1)}, u32[]{:S(2)}, u32[]{:S(2)}) collective-permute-start(f32[4,128,512]{2,1,0:T(8,128)S(1)} %get-tuple-element.66), channel_id=1, source_target_pairs={{0,24},{4,100},{8,16},{12,108},{16,8},{20,116},{24,0},{28,124},{32... | collective-permute-start | bytes 3145736 | tf_op jit(solution)/shard_map/ppermute | solution.py:54
  146.4 18.7 %collective-permute-start.24 = (f32[2,128,512]{2,1,0:T(8,128)S(1)}, f32[2,128,512]{2,1,0:T(8,128)S(1)}, u32[]{:S(2)}, u32[]{:S(2)}) collective-permute-start(f32[2,128,512]{2,1,0:T(8,128)S(1)} %slice_add_fusion.3), channel_id=1, source_target_pairs={{0,24},{4,100},{8,16},{12,108},{16,8},{20,116},{24,0},{28,124},{32... | collective-permute-start | bytes 1572872 | tf_op jit(solution)/shard_map/ppermute | solution.py:54
  148.3 16.8 %collective-permute-start.27 = (f32[2,128,512]{2,1,0:T(8,128)S(1)}, f32[2,128,512]{2,1,0:T(8,128)S(1)}, u32[]{:S(2)}, u32[]{:S(2)}) collective-permute-start(f32[2,128,512]{2,1,0:T(8,128)S(1)} %slice_add_fusion.2), channel_id=1, source_target_pairs={{0,8},{4,36},{8,0},{12,44},{16,24},{20,52},{24,16},{28,60},{32,40}... | collective-permute-start | bytes 1572872 | tf_op jit(solution)/shard_map/ppermute | solution.py:54
  157.7 18.9 %collective-permute-start.31 = (f32[2,128,512]{2,1,0:T(8,128)S(1)}, f32[2,128,512]{2,1,0:T(8,128)S(1)}, u32[]{:S(2)}, u32[]{:S(2)}) collective-permute-start(f32[2,128,512]{2,1,0:T(8,128)S(1)} %slice_add_fusion.1), channel_id=1, source_target_pairs={{0,24},{4,100},{8,16},{12,108},{16,8},{20,116},{24,0},{28,124},{32... | collective-permute-start | bytes 1572872 | tf_op jit(solution)/shard_map/ppermute | solution.py:54
  159.6 17.0 %collective-permute-start.34 = (f32[2,128,512]{2,1,0:T(8,128)S(1)}, f32[2,128,512]{2,1,0:T(8,128)S(1)}, u32[]{:S(2)}, u32[]{:S(2)}) collective-permute-start(f32[2,128,512]{2,1,0:T(8,128)S(1)} %slice_add_fusion), channel_id=1, source_target_pairs={{0,8},{4,36},{8,0},{12,44},{16,24},{20,52},{24,16},{28,60},{32,40}... | collective-permute-start | bytes 1572872 | tf_op jit(solution)/shard_map/ppermute | solution.py:54
  165.3 12.8 %collective-permute-start.25 = (f32[128,512]{1,0:T(8,128)S(1)}, f32[128,512]{1,0:T(8,128)S(1)}, u32[]{:S(2)}, u32[]{:S(2)}) collective-permute-start(f32[128,512]{1,0:T(8,128)S(1)} %get-tuple-element.72), channel_id=1, source_target_pairs={{0,32},{4,12},{8,40},{12,4},{16,48},{20,28},{24,56},{28,20},{32,0}... | collective-permute-start | bytes 786440 | tf_op jit(solution)/shard_map/ppermute | solution.py:54
  165.4 16.2 %collective-permute-start.28 = (f32[128,512]{1,0:T(8,128)S(1)}, f32[128,512]{1,0:T(8,128)S(1)}, u32[]{:S(2)}, u32[]{:S(2)}) collective-permute-start(f32[128,512]{1,0:T(8,128)S(1)} %get-tuple-element.69), channel_id=1, source_target_pairs={{0,64},{4,20},{8,72},{12,28},{16,80},{20,4},{24,88},{28,12},{32,96... | collective-permute-start | bytes 786440 | tf_op jit(solution)/shard_map/ppermute | solution.py:54
  166.9 14.7 %collective-permute-start.29 = (f32[128,512]{1,0:T(8,128)S(1)}, f32[128,512]{1,0:T(8,128)S(1)}, u32[]{:S(2)}, u32[]{:S(2)}) collective-permute-start(f32[128,512]{1,0:T(8,128)S(1)} %get-tuple-element.68), channel_id=1, source_target_pairs={{0,96},{4,28},{8,104},{12,20},{16,112},{20,12},{24,120},{28,4},{32... | collective-permute-start | bytes 786440 | tf_op jit(solution)/shard_map/ppermute | solution.py:54
  176.8 6.5 %collective-permute-start.32 = (f32[128,512]{1,0:T(8,128)S(1)}, f32[128,512]{1,0:T(8,128)S(1)}, u32[]{:S(2)}, u32[]{:S(2)}) collective-permute-start(f32[128,512]{1,0:T(8,128)S(1)} %get-tuple-element.73), channel_id=1, source_target_pairs={{0,32},{4,12},{8,40},{12,4},{16,48},{20,28},{24,56},{28,20},{32,0}... | collective-permute-start | bytes 786440 | tf_op jit(solution)/shard_map/ppermute | solution.py:54
  176.9 8.4 %collective-permute-start.35 = (f32[128,512]{1,0:T(8,128)S(1)}, f32[128,512]{1,0:T(8,128)S(1)}, u32[]{:S(2)}, u32[]{:S(2)}) collective-permute-start(f32[128,512]{1,0:T(8,128)S(1)} %get-tuple-element.71), channel_id=1, source_target_pairs={{0,64},{4,20},{8,72},{12,28},{16,80},{20,4},{24,88},{28,12},{32,96... | collective-permute-start | bytes 786440 | tf_op jit(solution)/shard_map/ppermute | solution.py:54
  178.1 10.0 %collective-permute-start.36 = (f32[128,512]{1,0:T(8,128)S(1)}, f32[128,512]{1,0:T(8,128)S(1)}, u32[]{:S(2)}, u32[]{:S(2)}) collective-permute-start(f32[128,512]{1,0:T(8,128)S(1)} %get-tuple-element.70), channel_id=1, source_target_pairs={{0,96},{4,28},{8,104},{12,20},{16,112},{20,12},{24,120},{28,4},{32... | collective-permute-start | bytes 786440 | tf_op jit(solution)/shard_map/ppermute | solution.py:54
